TPU v7x, 128 devices: a whole 4x4x4 slice. The times are simulated.
128 devices in a mesh: seq: 8 (over x, core), tp: 16 (over z, y).
Axes of the slice: x: 4, y: 4, z: 4, core: 2. Of those that a mesh axis runs over, the one named last changes fastest.
Arguments:
- tokens: bfloat16 [4096, 4096], P('seq'), may hold values from -6 to 6
- norm_gain: bfloat16 [4096], replicated, may hold values from 0.5 to 1.5
- w_query: bfloat16 [4096, 4096], P(None, 'tp'), may hold values from -0.09375 to 0.09375
- w_key: bfloat16 [4096, 1024], P(None, 'tp'), may hold values from -0.09375 to 0.09375
- w_value: bfloat16 [4096, 1024], P(None, 'tp'), may hold values from -0.09375 to 0.09375
- w_out: bfloat16 [4096, 4096], P('tp'), may hold values from -0.09375 to 0.09375
- prefix_keys: bfloat16 [16384, 1024], P('seq', 'tp')
- prefix_values: bfloat16 [16384, 1024], P('seq', 'tp'), may hold values from -6 to 6
- keep_rows: int32 [8, 8, 384], P('seq'), may hold values from 0 to 511, all different within a row
- owners: int32 [8, 8, 384, 1], P('seq'), may hold values from 0 to 127; in each aligned block of 384 rows (0 to 383, 384 to 767, ..., all dimensions but the last counted through in order) at most 4 rows name the same one
Outputs:
- attn_out: bfloat16 [4096, 4096], P('seq', 'tp')
- kept_cache: bfloat16 [32768, 256], P(('seq', 'tp'))
Inputs may be any that keep to these rules, and one draw needn't show every extreme that they name: `keep_rows`: the 384 rows of one span and head are distinct. `owners`: at most 4 entries of one span and head name the same owner, a bound that some of them reach.
All inputs are finite; a program needn't handle non-finite values.
Results may differ from a plain program's by a relative error of at most 0.03.
Values may be sent and summed in bfloat16 or wider, within the bound.
No kernel may reach another device: no remote copies, remote signals or barrier semaphores. Data moves between devices by JAX's collectives and lax.ppermute only.
A program may use at most 128 MiB of HBM per device.

v0:
```python
import functools
import math

import jax
import jax.numpy as jnp
import numpy as np
from jax import lax
from jax.experimental import pallas as pl
from jax.experimental.pallas import tpu as pltpu
from jax.sharding import PartitionSpec as P

EPSILON = 1e-05
ROPE_BASE = 500000.0
LOWEST = -1e30
LOG2E = math.log2(math.e)
SAFE_BOUND = 60.0
HD = 128
HALF = 64
AXES = ("seq", "tp")
RING = 4
TILE = 512
CHUNKS = 4
EXTRA = 32 + 128

NT = (((1,), (1,)), ((), ()))
TN = (((0,), (1,)), ((), ()))
F32 = jnp.float32
BF16 = jnp.bfloat16


def device_at(x, core, z, y):
    return ((x & 3) * 2 + core) * 16 + (z & 3) * 4 + (y & 3)


def pairs_of(move):
    return [
        (device_at(x, c, z, y), device_at(*move(x, c, z, y)))
        for x in range(RING)
        for c in range(2)
        for z in range(RING)
        for y in range(RING)
    ]


def send(value, move):
    return lax.ppermute(value, AXES, pairs_of(move))


def to_sibling(value):
    return send(value, lambda x, c, z, y: (x, 1 - c, z, y))


def to_head_pair(value):
    return send(value, lambda x, c, z, y: (x, c, z, y ^ 1))


def along_x(value, step):
    return send(value, lambda x, c, z, y: (x + step, c, z, y))


def along_first(value, step):
    return send(
        value, lambda x, c, z, y: (x, c, z + step, y) if c == 0 else (x, c, z, y + step)
    )


def along_second(value, step):
    return send(
        value, lambda x, c, z, y: (x, c, z, y + step) if c == 0 else (x, c, z + step, y)
    )


def signs():
    index = np.arange(HD)
    both = index[:, None] & index[None, :]
    parity = np.zeros((HD, HD), np.int64)
    for bit in range(7):
        parity += both >> bit & 1
    plain = (1 - 2 * (parity % 2)).astype(np.float32)
    return np.stack([plain, np.roll(plain, HALF, axis=1)])


def rope_tables(span, spans, prefix):
    freq = np.exp(-np.arange(HALF) * (2.0 * math.log(ROPE_BASE) / HD))
    freq = np.concatenate([freq, freq])
    near = np.arange(span)[:, None] * freq[None, :]
    far = (prefix + span * np.arange(spans))[:, None] * freq[None, :]
    near = np.stack([np.cos(near), np.sin(near)]).astype(np.float32)
    far = np.stack([np.cos(far), np.sin(far)]).astype(np.float32)
    return near, far


def rope_factors(near, far, number):
    cos_far, sin_far = far[0, pl.ds(number, 1), :], far[1, pl.ds(number, 1), :]
    cosine = near[0] * cos_far - near[1] * sin_far
    sine = near[1] * cos_far + near[0] * sin_far
    lane = lax.broadcasted_iota(jnp.int32, (1, HD), 1)
    return cosine, jnp.where(lane < HALF, -sine, sine)


def project_kernel(
    info, tokens, gain, w_q, w_kt, w_vt, near, far, sign, w_out, q_out, kv_out, w0, w1, w2, w3,
    held, held_q, held_kv, held_near, held_w, sum_q, sum_kv, sems, cut_sems,
):
    core, z, y, parity, number = info[1], info[2], info[3], info[4], info[5]
    span, width = tokens.shape
    block = width // CHUNKS
    parts = [pl.ds(i * block, block) for i in range(CHUNKS)]
    arrive = []
    for i, at in enumerate(parts):
        moves = (
            (tokens.at[:, at], held.at[:, at]),
            (w_q.at[at], held_q.at[at]),
            (w_kt.at[:, at], held_kv.at[:HALF, at]),
            (w_vt.at[:, at], held_kv.at[HALF:, at]),
        )
        arrive.append([
            pltpu.make_async_copy(start, end, sems.at[4 * i + j])
            for j, (start, end) in enumerate(moves)
        ])
    tables = pltpu.make_async_copy(near, held_near, sems.at[4 * CHUNKS])
    for copies in arrive:
        for copy in copies:
            copy.start()
    tables.start()
    whole = pltpu.make_async_copy(w_out, held_w, sems.at[4 * CHUNKS + 1])
    whole.start()
    cuts = []
    for d, piece in enumerate((w0, w1, w2, w3)):
        for k in range(RING):
            row = (z + jnp.where(core == 0, d, k)) & 3
            col = (y + jnp.where(core == 0, k, d)) & 3
            begin = pl.multiple_of((row * RING + col) * 256, 256)
            cuts.append(
                pltpu.make_async_copy(
                    held_w.at[:, pl.ds(begin, 256)],
                    piece.at[:, pl.ds(k * 256, 256)],
                    cut_sems.at[d * RING + k],
                )
            )
    squares = None
    per = block // HD
    for i, at in enumerate(parts):
        for copy in arrive[i]:
            copy.wait()
        gains = jnp.concatenate([gain[j:j + 1, :] for j in range(i * per, (i + 1) * per)], 1)
        begin, end = i * block, (i + 1) * block
        hidden = held[:, begin:end].astype(F32)
        weighted = (hidden * gains.astype(F32)).astype(BF16)
        hidden = hidden * hidden
        for j in range(per):
            square = hidden[:, j * HD:(j + 1) * HD]
            squares = square if squares is None else squares + square
        part_q = jnp.dot(weighted, held_q[begin:end, :], preferred_element_type=F32)
        part_kv = lax.dot_general(
            weighted, held_kv[:, begin:end], NT, preferred_element_type=F32
        )
        if i == 0:
            sum_q[...] = part_q
            sum_kv[...] = part_kv
        else:
            sum_q[...] += part_q
            sum_kv[...] += part_kv
    whole.wait()
    for copy in cuts:
        copy.start()
    scale = lax.rsqrt(jnp.sum(squares, -1, keepdims=True) / width + EPSILON)
    kv_out[...] = (sum_kv[...] * scale).astype(BF16)
    tables.wait()
    cosine, sine = rope_factors(held_near, far, number)
    turn = sign[parity]
    for h in range(2):
        head = sum_q[:, h * HD:(h + 1) * HD] * scale
        head = head * cosine + pltpu.roll(head, HALF, 1) * sine
        head = (head * HD ** -0.5).astype(BF16)
        head = jnp.dot(head, turn, preferred_element_type=F32)
        q_out[h * span:(h + 1) * span, :] = (head * (HD ** -0.5 * LOG2E)).astype(BF16)
    for copy in cuts:
        copy.wait()


def project(info, tokens, gain, w_q, w_kt, w_vt, near, far, sign, w_out):
    span, width = tokens.shape
    remain = pl.BlockSpec(memory_space=pl.ANY)
    return pl.pallas_call(
        project_kernel,
        in_specs=[smem(), remain, vmem()] + [remain] * 4 + [vmem(), vmem(), remain],
        out_specs=[vmem(), vmem()] + [remain] * 4,
        out_shape=[
            jax.ShapeDtypeStruct((2 * span, HD), BF16),
            jax.ShapeDtypeStruct((span, HD), BF16),
        ] + [jax.ShapeDtypeStruct((w_out.shape[0], 1024), BF16)] * 4,
        scratch_shapes=[
            pltpu.VMEM((span, width), BF16),
            pltpu.VMEM((width, 2 * HD), BF16),
            pltpu.VMEM((HD, width), BF16),
            pltpu.VMEM(near.shape, F32),
            pltpu.VMEM(w_out.shape, BF16),
            pltpu.VMEM((span, 2 * HD), F32),
            pltpu.VMEM((span, HD), F32),
            pltpu.SemaphoreType.DMA((4 * CHUNKS + 2,)),
            pltpu.SemaphoreType.DMA((RING * RING,)),
        ],
        compiler_params=pltpu.CompilerParams(vmem_limit_bytes=60 << 20),
        cost_estimate=pl.CostEstimate(
            flops=2 * span * width * 384, bytes_accessed=7 << 20, transcendentals=0
        ),
    )(info, tokens, gain, w_q, w_kt, w_vt, near, far, sign, w_out)


def segment_kernel(info, own, other, near, far, sign, rows, owners, seg_out, stay_out, go_out):
    x, core, z, y, parity, number, group = (info[i] for i in range(7))
    odd = parity == 1
    mine, theirs = own[...].astype(F32), other[...].astype(F32)
    first = jnp.where(odd, theirs, mine)
    second = jnp.where(odd, mine, theirs)
    lane = lax.broadcasted_iota(jnp.int32, (1, HD), 1)
    key = jnp.where(lane < HALF, first, pltpu.roll(second, HALF, 1))
    value = jnp.where(lane < HALF, pltpu.roll(first, HALF, 1), second).astype(BF16)
    cosine, sine = rope_factors(near, far, number)
    key = (key * cosine + pltpu.roll(key, HALF, 1) * sine).astype(BF16)
    turn = sign[parity]
    unit = HD ** -0.5
    seg_out[:HD, :] = (lax.dot_general(turn, key, TN, preferred_element_type=F32) * unit).astype(BF16)
    seg_out[HD:, :] = (lax.dot_general(turn, value, TN, preferred_element_type=F32) * unit).astype(BF16)
    plain = sign[0]
    pair = jnp.concatenate(
        [
            (jnp.dot(key, plain, preferred_element_type=F32) * unit).astype(BF16),
            (jnp.dot(value, plain, preferred_element_type=F32) * unit).astype(BF16),
        ],
        1,
    )
    span, keep = own.shape[0], rows.shape[1]
    row = rows[pl.ds(group, 1), :]
    owner = owners[pl.ds(group, 1), :]
    place = lax.broadcasted_iota(jnp.int32, (256, 1), 0)
    to_core = jnp.where(place >= 128, 1 - core, core)
    step_first, step_second = (place >> 3) & 3, (place >> 1) & 3
    to_x = (x + (place >> 5)) & 3
    to_z = (z + jnp.where(to_core == 0, step_first, step_second)) & 3
    to_y = (y + jnp.where(to_core == 0, step_second, step_first)) & 3
    named = owner == device_at(to_x, to_core, to_z, to_y)
    before = lax.broadcasted_iota(jnp.int32, (keep, keep), 0) < lax.broadcasted_iota(
        jnp.int32, (keep, keep), 1
    )
    rank = jnp.dot(
        jnp.where(named, 1.0, 0.0).astype(BF16),
        jnp.where(before, 1.0, 0.0).astype(BF16),
        preferred_element_type=F32,
    )
    slot = (2 * parity + (place & 1)).astype(F32)
    picks = jnp.where(jnp.logical_and(named, rank == slot), 1.0, 0.0).astype(BF16)
    places = jnp.where(
        lax.broadcasted_iota(jnp.int32, (span, keep), 0) == row, 1.0, 0.0
    ).astype(BF16)
    chosen = lax.dot_general(picks, places, NT, preferred_element_type=F32).astype(BF16)
    kept = jnp.dot(chosen, pair, preferred_element_type=F32).astype(BF16)
    stay_out[...] = kept[:128, :]
    go_out[...] = kept[128:, :]


def vmem():
    return pl.BlockSpec(memory_space=pltpu.VMEM)


def smem():
    return pl.BlockSpec(memory_space=pltpu.SMEM)


def segment(info, own, other, near, far, sign, rows, owners):
    span = own.shape[0]
    return pl.pallas_call(
        segment_kernel,
        in_specs=[smem()] + [vmem()] * 7,
        out_specs=[vmem()] * 3,
        out_shape=[jax.ShapeDtypeStruct((2 * HD, span), BF16)]
        + [jax.ShapeDtypeStruct((128, 2 * HD), BF16)] * 2,
        compiler_params=pltpu.CompilerParams(vmem_limit_bytes=24 << 20),
        cost_estimate=pl.CostEstimate(
            flops=400_000_000, bytes_accessed=2 << 20, transcendentals=0
        ),
    )(info, own, other, near, far, sign, rows, owners)


def attend_kernel(
    step, info, q, own, other, sib_own, sib_other, seg, sib_seg, stay, came, out, acc, total, top, held
):
    x, core = info[0], info[1]
    rows = q.shape[0]
    span = seg.shape[1]
    blocks = own.shape[1] // TILE
    prefix = ((own, other), (sib_own, sib_other))

    def prefix_tile(pair, columns):
        mine, theirs = pair
        keys = jnp.concatenate([mine[:HALF, columns], theirs[:HALF, columns]], 0)
        values = jnp.concatenate([mine[HALF:, columns], theirs[HALF:, columns]], 0)
        return keys, values

    squares = []
    for pair in prefix:
        for ref in pair:
            half = ref[:HALF, :].astype(F32)
            squares.append(jnp.sum(half * half, 0, keepdims=True))
    longest = jnp.maximum(jnp.max(squares[0] + squares[1]), jnp.max(squares[2] + squares[3]))
    for ref in (seg, sib_seg):
        part = ref[:HD, :].astype(F32)
        longest = jnp.maximum(longest, jnp.max(jnp.sum(part * part, 0, keepdims=True)))
    query_f = q[...].astype(F32)
    widest = jnp.max(jnp.sum(query_f * query_f, 1, keepdims=True))
    calm = longest * widest < SAFE_BOUND * SAFE_BOUND

    if step == 0:
        whole_flags = (None, core == 1)
    else:
        later = lax.rem(x + RING - step, RING) > x
        whole_flags = (later, later)

    def causal(begin, count):
        token = lax.rem(lax.broadcasted_iota(jnp.int32, (count, span), 0) + begin, span)
        return lax.broadcasted_iota(jnp.int32, (count, span), 1) <= token

    acc[...] = jnp.zeros_like(acc)
    total[...] = jnp.zeros_like(total)

    @pl.when(calm)
    def _():
        def tile(keys, values, masked=False):
            scores = jnp.dot(q[...], keys, preferred_element_type=F32)
            weights = jnp.exp2(scores)
            if masked:
                weights = jnp.where(causal(0, rows), weights, 0.0)
            part = weights[:, :HD]
            for i in range(1, TILE // HD):
                part = part + weights[:, i * HD:(i + 1) * HD]
            mixed = lax.dot_general(weights.astype(BF16), values, NT, preferred_element_type=F32)
            acc[...] += mixed
            total[...] += part

        for pair in prefix:
            def some_tiles(i, carry, pair=pair):
                for j in range(2):
                    begin = pl.multiple_of((2 * i + j) * TILE, TILE)
                    tile(*prefix_tile(pair, pl.ds(begin, TILE)))
                return carry

            lax.fori_loop(0, blocks // 2, some_tiles, 0)
        for ref, flag in zip((seg, sib_seg), whole_flags):
            if flag is None:
                tile(ref[:HD, :], ref[HD:, :], masked=True)
            else:
                @pl.when(flag)
                def _(ref=ref):
                    tile(ref[:HD, :], ref[HD:, :])
        top[...] = jnp.zeros_like(top)

    @pl.when(jnp.logical_not(calm))
    def _():
        top[...] = jnp.full_like(top, LOWEST)
        chunk = 256
        seg_flag = 1 if whole_flags[0] is None else whole_flags[0].astype(jnp.int32)
        sib_flag = whole_flags[1].astype(jnp.int32)

        def some_keys(b, carry):
            column = pl.ds(pl.multiple_of(lax.rem(b, blocks) * TILE, TILE), TILE)
            for number, pair in enumerate(prefix):
                @pl.when(b // blocks == number)
                def _(pair=pair):
                    for i in range(2):
                        for j, ref in enumerate(pair):
                            begin = i * HD + j * HALF
                            held[begin:begin + HALF, :] = ref[i * HALF:(i + 1) * HALF, column]

            for number, ref in enumerate((seg, sib_seg)):
                @pl.when(b == 2 * blocks + number)
                def _(ref=ref):
                    held[...] = ref[...]

            last = b == 2 * blocks
            flag = jnp.where(last, seg_flag, jnp.where(b > 2 * blocks, sib_flag, 1))
            causal_from = 0 if step else jnp.where(last, 0, -span)

            def some_rows(r, carry):
                begin = pl.multiple_of(r * chunk, chunk)
                at = pl.ds(begin, chunk)
                scores = jnp.dot(q[at, :], held[:HD, :], preferred_element_type=F32)
                if step == 0:
                    token = lax.rem(
                        lax.broadcasted_iota(jnp.int32, (chunk, span), 0) + begin, span
                    )
                    column = lax.broadcasted_iota(jnp.int32, (chunk, span), 1) + causal_from
                    scores = jnp.where(column <= token, scores, -jnp.inf)
                old = top[at, :]
                new = jnp.maximum(old, jnp.max(scores, 1, keepdims=True))
                weights = jnp.exp2(scores - new[:, :1])
                factor = jnp.exp2(old - new)
                part = weights[:, :HD]
                for i in range(1, TILE // HD):
                    part = part + weights[:, i * HD:(i + 1) * HD]
                mixed = lax.dot_general(
                    weights.astype(BF16), held[HD:, :], NT, preferred_element_type=F32
                )
                acc[at, :] = acc[at, :] * factor + mixed
                total[at, :] = total[at, :] * factor + part
                top[at, :] = new
                return carry

            @pl.when(flag == 1)
            def _():
                lax.fori_loop(0, rows // chunk, some_rows, 0)

            return carry

        lax.fori_loop(0, 2 * blocks + 2, some_keys, 0)

    summed = jnp.sum(total[...], 1, keepdims=True)
    out[:rows, :] = (acc[...] / summed).astype(BF16)
    level = top[...] + jnp.log2(summed)
    eye = lax.broadcasted_iota(jnp.int32, (1, HD, HD), 1) == lax.broadcasted_iota(
        jnp.int32, (1, HD, HD), 2
    )
    packed = jnp.sum(jnp.where(eye, level.reshape(rows // HD, HD, HD), 0.0), 1)
    high = packed.astype(BF16).astype(F32)
    rest = packed - high
    middle = rest.astype(BF16).astype(F32)
    low = rest - middle
    out[rows:rows + 32, :] = jnp.concatenate(
        [high, middle, low, jnp.zeros_like(high)], 0
    ).astype(BF16)
    back = (RING - step) % RING
    for i, ref in enumerate((stay, came, stay, came)):
        out[rows + 32 * (i + 1):rows + 32 * (i + 2), :] = ref[
            32 * back:32 * (back + 1), i // 2 * HD:(i // 2 + 1) * HD
        ]


def attend(step, info, q, *rest):
    rows = q.shape[0]
    return pl.pallas_call(
        functools.partial(attend_kernel, step),
        in_specs=[smem()] + [vmem()] * 9,
        out_specs=vmem(),
        out_shape=jax.ShapeDtypeStruct((rows + EXTRA, HD), BF16),
        scratch_shapes=[pltpu.VMEM((rows, HD), F32)] * 3 + [pltpu.VMEM((2 * HD, TILE), BF16)],
        compiler_params=pltpu.CompilerParams(vmem_limit_bytes=32 << 20),
        cost_estimate=pl.CostEstimate(
            flops=8 * rows * HD * 4096, bytes_accessed=4 << 20, transcendentals=rows * 4096
        ),
    )(info, q, *rest)


def split(value):
    high = value.astype(BF16)
    return high, (value - high.astype(F32)).astype(BF16)


def shuffle(rows, source):
    here = lax.broadcasted_iota(jnp.int32, (256, 256), 0)
    there = lax.broadcasted_iota(jnp.int32, (256, 256), 1)
    moves = jnp.where(source(here) == there, 1.0, 0.0).astype(BF16)
    return jnp.dot(moves, rows, preferred_element_type=F32).astype(BF16)


def merge_kernel(info, p0, p1, p2, p3, sign, *outs):
    parity = info[4]
    parts = (p0, p1, p2, p3)
    rows = p0.shape[0] - EXTRA
    count = rows // HD
    levels = []
    for part in parts:
        stats = part[rows:rows + 32, :].astype(F32)
        levels.append(stats[:count] + stats[count:2 * count] + stats[2 * count:3 * count])
    most = functools.reduce(jnp.maximum, levels)
    shares = [jnp.exp2(level - most) for level in levels]
    whole = functools.reduce(jnp.add, shares)
    shares = [share / whole for share in shares]
    eye = lax.broadcasted_iota(jnp.int32, (HD, HD), 0) == lax.broadcasted_iota(
        jnp.int32, (HD, HD), 1
    )
    turn = sign[parity]
    per_head = count // 2
    for b in range(count):
        left, right = [], []
        for share, part in zip(shares, parts):
            block = part[b * HD:(b + 1) * HD, :]
            high, low = split(share[b:b + 1, :])
            for piece in (high, low):
                left.append(jnp.where(eye, piece.astype(F32), 0.0).astype(BF16))
                right.append(block)
        mixed = jnp.dot(
            jnp.concatenate(left, 1), jnp.concatenate(right, 0), preferred_element_type=F32
        )
        high, low = split(mixed)
        plain = lax.dot_general(high, turn, NT, preferred_element_type=F32)
        plain = plain + lax.dot_general(low, turn, NT, preferred_element_type=F32)
        head, place = b // per_head, b % per_head
        block = (plain * HD ** -0.5).astype(BF16)
        for out in outs:
            out[place * HD:(place + 1) * HD, head * HD:(head + 1) * HD] = block
    kept = jnp.concatenate(
        [
            jnp.concatenate([part[rows + 32:rows + 96, :], part[rows + 96:, :]], 1)
            for part in parts
        ],
        0,
    )
    kept = shuffle(
        kept,
        lambda r: ((r >> 4) & 3) << 6 | ((r >> 3) & 1) << 5 | (r >> 6) << 3 | (r & 7),
    )
    for k, out in enumerate(outs):
        out[rows // 2:, :] = kept[64 * k:64 * (k + 1), :]


def merge(info, parts, sign):
    rows = parts[0].shape[0] - EXTRA
    return pl.pallas_call(
        merge_kernel,
        in_specs=[smem()] + [vmem()] * 5,
        out_specs=[vmem()] * RING,
        out_shape=[jax.ShapeDtypeStruct((rows // 2 + 64, 2 * HD), BF16)] * RING,
        compiler_params=pltpu.CompilerParams(vmem_limit_bytes=24 << 20),
        cost_estimate=pl.CostEstimate(
            flops=400_000_000, bytes_accessed=2 << 20, transcendentals=0
        ),
    )(info, *parts, sign)


def out_kernel(c0, c1, c2, c3, w0, w1, w2, w3, o0, o1, o2, o3, sum_out):
    outs = (o0, o1, o2, o3)
    contexts = (c0, c1, c2, c3)
    span = sum_out.shape[0]
    for k in (2, 1, 3, 0):
        columns = slice(k * 256, (k + 1) * 256)
        whole = None
        for c, w in zip(contexts, (w0, w1, w2, w3)):
            part = jnp.dot(c[:span, :], w[:, columns], preferred_element_type=F32)
            whole = part if whole is None else whole + part
        if k:
            outs[k][:span, :] = whole.astype(BF16)
        else:
            sum_out[...] = whole
    kept = jnp.concatenate([c[span:, :] for c in contexts], 0)
    kept = shuffle(
        kept,
        lambda r: ((r >> 4) & 3) << 6
        | ((r >> 2) & 3) << 4
        | ((r >> 1) & 1) << 3
        | (r >> 6) << 1
        | (r & 1),
    )
    for k, out in enumerate(outs):
        begin = span if k else 0
        out[begin:, :] = kept[64 * k:64 * (k + 1), :]


def project_out(contexts, weights):
    total = contexts[0].shape[0]
    span = total - 64
    return pl.pallas_call(
        out_kernel,
        in_specs=[vmem()] * 8,
        out_specs=[vmem()] * 5,
        out_shape=[jax.ShapeDtypeStruct((total if k else 64, 256), BF16) for k in range(4)]
        + [jax.ShapeDtypeStruct((span, 256), F32)],
        compiler_params=pltpu.CompilerParams(vmem_limit_bytes=24 << 20),
        cost_estimate=pl.CostEstimate(
            flops=2 * span * 1024 * 1024, bytes_accessed=5 << 20, transcendentals=0
        ),
    )(*contexts, *weights)


def finish_kernel(info, share, kept, a1, a2, a3, attn_out, kept_out):
    x, core, z, y = (info[i] for i in range(4))
    arrived = (a1, a2, a3)
    span = share.shape[0]
    whole = share[...]
    for part in arrived:
        whole = whole + part[:span, :].astype(F32)
    attn_out[...] = whole.astype(BF16)
    rows = jnp.concatenate([kept[...]] + [part[span:, :] for part in arrived], 0)
    place = lax.broadcasted_iota(jnp.int32, (1, 256), 1)
    back_second, back_first = place >> 6, (place >> 4) & 3
    from_x = (x + (place >> 2)) & 3
    from_core = (core + (place >> 1)) & 1
    from_z = (z - jnp.where(core == 0, back_first, back_second)) & 3
    from_y = (y - jnp.where(core == 0, back_second, back_first)) & 3
    target = device_at(from_x, from_core, from_z, from_y) * 2 + (place & 1)
    here = lax.broadcasted_iota(jnp.int32, (256, 256), 0)
    moves = jnp.where(here == target, 1.0, 0.0).astype(BF16)
    kept_out[...] = jnp.dot(moves, rows, preferred_element_type=F32).astype(BF16)


def finish(info, share, kept, arrived):
    return pl.pallas_call(
        finish_kernel,
        in_specs=[smem()] + [vmem()] * 5,
        out_specs=[vmem()] * 2,
        out_shape=[
            jax.ShapeDtypeStruct(share.shape, BF16),
            jax.ShapeDtypeStruct((256, 2 * HD), BF16),
        ],
        compiler_params=pltpu.CompilerParams(vmem_limit_bytes=24 << 20),
    )(info, share, kept, *arrived)


def shards(
    tokens, norm_gain, w_query, w_key, w_value, w_out, prefix_keys, prefix_values, keep_rows, owners
):
    seq = lax.axis_index("seq")
    tp = lax.axis_index("tp")
    seq_count = lax.axis_size("seq")
    span = tokens.shape[0]
    prefix_len = prefix_keys.shape[0] * seq_count
    info = jnp.stack(
        [seq // 2, seq % 2, tp // RING, tp % RING, tp % 2, seq, tp // 2, seq * 0]
    ).astype(jnp.int32)
    near, far = rope_tables(span, seq_count, prefix_len)
    near, far = jnp.asarray(near), jnp.asarray(far)
    sign = jnp.asarray(signs(), BF16)

    own = jnp.concatenate([prefix_keys.T, prefix_values.T], 0)
    other = to_head_pair(own)
    sib_own = to_sibling(own)
    q, kv, *pieces = project(
        info, tokens, norm_gain.reshape(-1, HD), w_query, w_key.T, w_value.T, near, far, sign, w_out
    )
    kv_other = to_head_pair(kv)
    queries = [q] + [along_x(q, d) for d in (1, 2, 3)]
    weights = [pieces[0]] + [along_first(pieces[d], d) for d in (1, 2, 3)]
    kv_other, other, queries[1], queries[3] = lax.optimization_barrier(
        (kv_other, other, queries[1], queries[3])
    )
    sib_other = to_sibling(other)
    seg, stay, go = segment(
        info, kv, kv_other, near, far, sign, keep_rows[0], owners.reshape(owners.shape[1:3])
    )
    came = to_sibling(go)
    sib_seg = to_sibling(seg)
    parts = [None] * RING
    for d in (3, 1, 2, 0):
        part = attend(
            d, info, queries[d], own, other, sib_own, sib_other, seg, sib_seg, stay, came
        )
        parts[d] = along_x(part, -d) if d else part
    contexts = merge(info, parts, sign)
    contexts = [contexts[0]] + [along_first(contexts[d], d) for d in (1, 2, 3)]
    *shares, share = project_out(contexts, weights)
    arrived = [along_second(shares[k], k) for k in (1, 2, 3)]
    return tuple(finish(info, share, shares[0], arrived))


def solution(mesh):
    return jax.shard_map(
        shards,
        mesh=mesh,
        in_specs=(
            P("seq", None),
            P(),
            P(None, "tp"),
            P(None, "tp"),
            P(None, "tp"),
            P("tp", None),
            P("seq", "tp"),
            P("seq", "tp"),
            P("seq", None, None),
            P("seq", None, None, None),
        ),
        out_specs=(P("seq", "tp"), P(("seq", "tp"), None)),
        check_vma=False,
    )
```

profile of v0, /device:TPU:1, one launch (start us, length us, event | category | flops | bytes accessed | tf_op | source)
XLA Modules:
  0.0 157.4 jit_solution(2847358077077565233)
XLA Ops:
  0.6 1.1 pad_maximum_fusion.own
  1.7 2.2 %collective-permute-start.1 = (bf16[128,2048]{1,0:T(8,128)(2,1)S(1)}, bf16[128,2048]{1,0:T(8,128)(2,1)S(1)}, u32[]{:S(2)}, u32[]{:S(2)}) collective-permute-start(bf16[128,2048]{1,0:T(8,128)(2,1)S(1)} %pad_maximum_fusion.own), channel_id=1, source_target_pairs={{0,1},{1,0},{2,3},{3,2},{4,5},{5,4},{6,7},{7,6},{8,9},{9,8},{10,11... | collective-permute-start | bytes 1572872 | tf_op jit(solution)/shard_map/ppermute | solution.py:46
  3.9 0.6 stack.31.info
  4.5 0.0 copy-start.3
  4.5 0.0 copy-start.7
  4.5 7.3 %shard_map.140 = (bf16[1024,128]{1,0:T(8,128)(2,1)}, bf16[512,128]{1,0:T(8,128)(2,1)}, bf16[256,1024]{1,0:T(8,128)(2,1)}, bf16[256,1024]{1,0:T(8,128)(2,1)}, bf1...) custom-call(s32[8]{0:T(128)} %stack.31.info, bf16[512,4096]{1,0:T(8,128)(2,1)} %tokens.1, bf16[32,128]{1,0:T(8,128)(2,1)} %bitcast.22, ...), custom_call_target="tpu_custom_call" | custom-call | flops 1610612736 | bytes 7340032 | tf_op jit(solution)/shard_map/pallas_call | solution.py:185
  11.9 2.5 %collective-permute-start.3 = (bf16[1024,128]{1,0:T(8,128)(2,1)}, bf16[1024,128]{1,0:T(8,128)(2,1)S(1)}, u32[]{:S(2)}, u32[]{:S(2)}) collective-permute-start(bf16[1024,128]{1,0:T(8,128)(2,1)} %get-tuple-element.24.q), channel_id=1, source_target_pairs={{0,96},{1,97},{2,98},{3,99},{4,100},{5,101},{6,102},{7,103},{8,104... | collective-permute-start | bytes 786440 | tf_op jit(solution)/shard_map/ppermute | solution.py:46
  14.4 0.0 collective-permute-start.2
  14.4 0.2 collective-permute-start
  14.6 1.5 collective-permute-start.4
  16.1 2.6 %collective-permute-done.other = bf16[512,128]{1,0:T(8,128)(2,1)S(1)} collective-permute-done((bf16[512,128]{1,0:T(8,128)(2,1)}, bf16[512,128]{1,0:T(8,128)(2,1)S(1)}, u32[]{:S(2)}, u32[]{:S(2)}) %collective-permute-start) | collective-permute-done | bytes 131104 | tf_op jit(solution)/shard_map/ppermute | solution.py:46
  18.7 0.6 collective-permute-done.3.q
  19.4 3.0 %collective-permute-done.2.q = bf16[1024,128]{1,0:T(8,128)(2,1)S(1)} collective-permute-done((bf16[1024,128]{1,0:T(8,128)(2,1)}, bf16[1024,128]{1,0:T(8,128)(2,1)S(1)}, u32[]{:S(2)}, u32[]{:S(2)}) %collective-permute-start.2) | collective-permute-done | bytes 262176 | tf_op jit(solution)/shard_map/ppermute | solution.py:46
  22.4 0.0 collective-permute-done.1.other
  22.4 2.2 %collective-permute-start.5 = (bf16[128,2048]{1,0:T(8,128)(2,1)S(1)}, bf16[128,2048]{1,0:T(8,128)(2,1)S(1)}, u32[]{:S(2)}, u32[]{:S(2)}) collective-permute-start(bf16[128,2048]{1,0:T(8,128)(2,1)S(1)} %collective-permute-done.1.other), channel_id=1, source_target_pairs={{0,16},{1,17},{2,18},{3,19},{4,20},{5,21},{6,22},{7,23},{8,24},{9,... | collective-permute-start | bytes 1572872 | tf_op jit(solution)/shard_map/ppermute | solution.py:46
  24.6 0.0 copy-done.8
  24.6 0.0 copy-done
  24.6 0.0 copy-done.1
  24.6 0.0 copy-done.2
  24.6 0.0 copy-done.3
  24.6 0.0 copy-done.7
  24.6 0.0 copy-start.6
  24.6 0.9 copy-done.6
  25.5 1.6 shard_map.141
  27.1 0.1 collective-permute-start.6
  27.2 0.5 collective-permute-start.7
  27.7 0.0 collective-permute-start.9
  27.7 0.0 collective-permute-done.4.sib_own
  27.7 0.2 collective-permute-start.15
  27.9 0.9 collective-permute-done.7.came
  28.8 2.6 %collective-permute-start.16 = (bf16[256,1024]{1,0:T(8,128)(2,1)}, bf16[256,1024]{1,0:T(8,128)(2,1)S(1)}, u32[]{:S(2)}, u32[]{:S(2)}) collective-permute-start(bf16[256,1024]{1,0:T(8,128)(2,1)} %get-tuple-element.39), channel_id=1, source_target_pairs={{0,8},{1,9},{2,10},{3,11},{4,12},{5,13},{6,14},{7,15},{8,0},{9,1},... | collective-permute-start | bytes 1572872 | tf_op jit(solution)/shard_map/ppermute | solution.py:46
  31.4 0.0 collective-permute-done.6.sib_seg
  31.4 1.0 collective-permute-start.17
  32.4 0.0 collective-permute-done.5.sib_other
  32.4 23.6 %shard_map.143 = bf16[1184,128]{1,0:T(8,128)(2,1)S(1)} custom-call(s32[8]{0:T(128)S(1)} %copy-done.3, bf16[1024,128]{1,0:T(8,128)(2,1)S(1)} %collective-permute-done.2.q, bf16[128,2048]{1,0:T(8,128)(2,1)S(1)} %pad_maximum_fusion.own, bf16[128,2048]{1,0:T(8,128)(2,1)S(1)} %collective-permute-done.1.other, ...), custom_call_target="tpu_custom_call" | custom-call | flops 4294967296 | bytes 4194304 | tf_op jit(solution)/shard_map/pallas_call | solution.py:440
  56.0 0.1 collective-permute-start.8
  56.1 0.0 collective-permute-done.9.q
  56.1 23.4 %shard_map.144 = bf16[1184,128]{1,0:T(8,128)(2,1)S(1)} custom-call(s32[8]{0:T(128)S(1)} %copy-done.3, bf16[1024,128]{1,0:T(8,128)(2,1)S(1)} %collective-permute-done.9.q, bf16[128,2048]{1,0:T(8,128)(2,1)S(1)} %pad_maximum_fusion.own, bf16[128,2048]{1,0:T(8,128)(2,1)S(1)} %collective-permute-done.1.other, ...), custom_call_target="tpu_custom_call" | custom-call | flops 4294967296 | bytes 4194304 | tf_op jit(solution)/shard_map/pallas_call | solution.py:440
  79.5 0.0 copy-start.5
  79.5 0.1 collective-permute-start.10
  79.6 23.4 %shard_map.145 = bf16[1184,128]{1,0:T(8,128)(2,1)S(1)} custom-call(s32[8]{0:T(128)S(1)} %copy-done.3, bf16[1024,128]{1,0:T(8,128)(2,1)S(1)} %collective-permute-done.3.q, bf16[128,2048]{1,0:T(8,128)(2,1)S(1)} %pad_maximum_fusion.own, bf16[128,2048]{1,0:T(8,128)(2,1)S(1)} %collective-permute-done.1.other, ...), custom_call_target="tpu_custom_call" | custom-call | flops 4294967296 | bytes 4194304 | tf_op jit(solution)/shard_map/pallas_call | solution.py:440
  103.0 0.0 collective-permute-done.8.p1
  103.0 1.5 collective-permute-start.11
  104.6 24.3 %shard_map.142.p0 = bf16[1184,128]{1,0:T(8,128)(2,1)S(1)} custom-call(s32[8]{0:T(128)S(1)} %copy-done.3, bf16[1024,128]{1,0:T(8,128)(2,1)S(1)} %copy-done.5, bf16[128,2048]{1,0:T(8,128)(2,1)S(1)} %pad_maximum_fusion.own, bf16[128,2048]{1,0:T(8,128)(2,1)S(1)} %collective-permute-done.1.other, bf16[128,2048]{1,0:T(8,128)(2,1)S(1)} %collective-permute-done.4.sib_own, ...), custom_call_target="tpu_custom_call" | custom-call | flops 4294967296 | bytes 4194304 | tf_op jit(solution)/shard_map/pallas_call | solution.py:440
  128.9 0.0 collective-permute-done.10.p2
  128.9 0.0 collective-permute-done.11.p3
  128.9 2.4 %shard_map.146 = (bf16[576,256]{1,0:T(8,128)(2,1)S(1)}, bf16[576,256]{1,0:T(8,128)(2,1)S(1)}, bf16[576,256]{1,0:T(8,128)(2,1)S(1)}, bf16[576,256]{1,0:T(8,128)(2,1)S(1)}) custom-call(s32[8]{0:T(128)S(1)} %copy-done.3, bf16[1184,128]{1,0:T(8,128)(2,1)S(1)} %shard_map.142.p0, bf16[1184,128]{1,0:T(8,128)(2,1)S(1)} %collective-permute-done.8.p1, ...), custom_call_target="tpu_custom_call" | custom-call | flops 400000000 | bytes 2097152 | tf_op jit(solution)/shard_map/pallas_call | solution.py:518
  131.3 0.6 collective-permute-start.12
  131.9 0.7 collective-permute-start.13
  132.6 0.0 collective-permute-done.15.w1
  132.6 1.8 %collective-permute-start.14 = (bf16[576,256]{1,0:T(8,128)(2,1)S(1)}, bf16[576,256]{1,0:T(8,128)(2,1)S(1)}, u32[]{:S(2)}, u32[]{:S(2)}) collective-permute-start(bf16[576,256]{1,0:T(8,128)(2,1)S(1)} %get-tuple-element.36), channel_id=1, source_target_pairs={{0,12},{1,13},{2,14},{3,15},{4,0},{5,1},{6,2},{7,3},{8,4},{9,5},{1... | collective-permute-start | bytes 884744 | tf_op jit(solution)/shard_map/ppermute | solution.py:46
  134.4 0.0 collective-permute-done.16.w2
  134.4 0.0 collective-permute-done.17.w3
  134.4 7.2 %collective-permute-done.12.c1 = bf16[576,256]{1,0:T(8,128)(2,1)S(1)} collective-permute-done((bf16[576,256]{1,0:T(8,128)(2,1)S(1)}, bf16[576,256]{1,0:T(8,128)(2,1)S(1)}, u32[]{:S(2)}, u32[]{:S(2)}) %collective-permute-start.12) | collective-permute-done | bytes 294944 | tf_op jit(solution)/shard_map/ppermute | solution.py:46
  141.6 0.0 collective-permute-done.13.c2
  141.6 0.6 collective-permute-done.14.c3
  142.2 1.3 shard_map.147
  143.5 1.7 %collective-permute-start.18 = (bf16[576,256]{1,0:T(8,128)(2,1)S(1)}, bf16[576,256]{1,0:T(8,128)(2,1)S(1)}, u32[]{:S(2)}, u32[]{:S(2)}) collective-permute-start(bf16[576,256]{1,0:T(8,128)(2,1)S(1)} %get-tuple-element.43), channel_id=1, source_target_pairs={{0,1},{1,2},{2,3},{3,0},{4,5},{5,6},{6,7},{7,4},{8,9},{9,10},{10,1... | collective-permute-start | bytes 884744 | tf_op jit(solution)/shard_map/ppermute | solution.py:46
  145.2 3.0 %collective-permute-start.19 = (bf16[576,256]{1,0:T(8,128)(2,1)S(1)}, bf16[576,256]{1,0:T(8,128)(2,1)S(1)}, u32[]{:S(2)}, u32[]{:S(2)}) collective-permute-start(bf16[576,256]{1,0:T(8,128)(2,1)S(1)} %get-tuple-element.44), channel_id=1, source_target_pairs={{0,2},{1,3},{2,0},{3,1},{4,6},{5,7},{6,4},{7,5},{8,10},{9,11},{10,... | collective-permute-start | bytes 884744 | tf_op jit(solution)/shard_map/ppermute | solution.py:46
  148.2 0.7 collective-permute-start.20
  149.0 2.5 %collective-permute-done.18.a1 = bf16[576,256]{1,0:T(8,128)(2,1)S(1)} collective-permute-done((bf16[576,256]{1,0:T(8,128)(2,1)S(1)}, bf16[576,256]{1,0:T(8,128)(2,1)S(1)}, u32[]{:S(2)}, u32[]{:S(2)}) %collective-permute-start.18) | collective-permute-done | bytes 294944 | tf_op jit(solution)/shard_map/ppermute | solution.py:46
  151.5 4.3 %collective-permute-done.19.a2 = bf16[576,256]{1,0:T(8,128)(2,1)S(1)} collective-permute-done((bf16[576,256]{1,0:T(8,128)(2,1)S(1)}, bf16[576,256]{1,0:T(8,128)(2,1)S(1)}, u32[]{:S(2)}, u32[]{:S(2)}) %collective-permute-start.19) | collective-permute-done | bytes 294944 | tf_op jit(solution)/shard_map/ppermute | solution.py:46
  155.8 0.0 collective-permute-done.20.a3
  155.8 1.6 shard_map.148
  (8 shorter events, 0.0 us)
Async XLA Ops:
  1.7 20.7 %collective-permute-start.1 = (bf16[128,2048]{1,0:T(8,128)(2,1)S(1)}, bf16[128,2048]{1,0:T(8,128)(2,1)S(1)}, u32[]{:S(2)}, u32[]{:S(2)}) collective-permute-start(bf16[128,2048]{1,0:T(8,128)(2,1)S(1)} %pad_maximum_fusion.own), channel_id=1, source_target_pairs={{0,1},{1,0},{2,3},{3,2},{4,5},{5,4},{6,7},{7,6},{8,9},{9,8},{10,11... | collective-permute-start | bytes 1572872 | tf_op jit(solution)/shard_map/ppermute | solution.py:46
  4.5 20.1 %copy-start.8 = (s32[1,8,384,1]{2,3,1,0:T(1,128)S(1)}, s32[1,8,384,1]{2,3,1,0:T(1,128)}, u32[]{:S(2)}) copy-start(s32[1,8,384,1]{2,3,1,0:T(1,128)} %param.22) | copy-start | bytes 36868
  4.5 20.1 %copy-start = (f32[2,512,128]{2,1,0:T(8,128)S(1)}, f32[2,512,128]{2,1,0:T(8,128)}, u32[]{:S(2)}) copy-start(f32[2,512,128]{2,1,0:T(8,128)} %constant.70.clone.near) | copy-start | bytes 1572868
  4.5 20.1 %copy-start.1 = (bf16[2,128,128]{2,1,0:T(8,128)(2,1)S(1)}, bf16[2,128,128]{2,1,0:T(8,128)(2,1)}, u32[]{:S(2)}) copy-start(bf16[2,128,128]{2,1,0:T(8,128)(2,1)} %constant.72.clone.sign) | copy-start | bytes 196612
  4.5 20.1 %copy-start.2 = (f32[2,8,128]{2,1,0:T(8,128)S(1)}, f32[2,8,128]{2,1,0:T(8,128)}, u32[]{:S(2)}) copy-start(f32[2,8,128]{2,1,0:T(8,128)} %constant.71.clone.far) | copy-start | bytes 24580
  4.5 20.1 %copy-start.3 = (s32[8]{0:T(128)S(1)}, s32[8]{0:T(128)}, u32[]{:S(2)}) copy-start(s32[8]{0:T(128)} %stack.31.info) | copy-start | bytes 100
  4.5 20.1 %copy-start.7 = (s32[1,8,384]{2,1,0:T(8,128)S(1)}, s32[1,8,384]{2,1,0:T(8,128)}, u32[]{:S(2)}) copy-start(s32[1,8,384]{2,1,0:T(8,128)} %param.21) | copy-start | bytes 36868
  11.9 7.5 %collective-permute-start.3 = (bf16[1024,128]{1,0:T(8,128)(2,1)}, bf16[1024,128]{1,0:T(8,128)(2,1)S(1)}, u32[]{:S(2)}, u32[]{:S(2)}) collective-permute-start(bf16[1024,128]{1,0:T(8,128)(2,1)} %get-tuple-element.24.q), channel_id=1, source_target_pairs={{0,96},{1,97},{2,98},{3,99},{4,100},{5,101},{6,102},{7,103},{8,104... | collective-permute-start | bytes 786440 | tf_op jit(solution)/shard_map/ppermute | solution.py:46
  14.4 8.0 %collective-permute-start.2 = (bf16[1024,128]{1,0:T(8,128)(2,1)}, bf16[1024,128]{1,0:T(8,128)(2,1)S(1)}, u32[]{:S(2)}, u32[]{:S(2)}) collective-permute-start(bf16[1024,128]{1,0:T(8,128)(2,1)} %get-tuple-element.24.q), channel_id=1, source_target_pairs={{0,32},{1,33},{2,34},{3,35},{4,36},{5,37},{6,38},{7,39},{8,40},{9,... | collective-permute-start | bytes 786440 | tf_op jit(solution)/shard_map/ppermute | solution.py:46
  14.4 4.3 %collective-permute-start = (bf16[512,128]{1,0:T(8,128)(2,1)}, bf16[512,128]{1,0:T(8,128)(2,1)S(1)}, u32[]{:S(2)}, u32[]{:S(2)}) collective-permute-start(bf16[512,128]{1,0:T(8,128)(2,1)} %get-tuple-element.25.own), channel_id=1, source_target_pairs={{0,1},{1,0},{2,3},{3,2},{4,5},{5,4},{6,7},{7,6},{8,9},{9,8},{10,11... | collective-permute-start | bytes 393224 | tf_op jit(solution)/shard_map/ppermute | solution.py:46
  14.6 13.1 %collective-permute-start.4 = (bf16[128,2048]{1,0:T(8,128)(2,1)S(1)}, bf16[128,2048]{1,0:T(8,128)(2,1)S(1)}, u32[]{:S(2)}, u32[]{:S(2)}) collective-permute-start(bf16[128,2048]{1,0:T(8,128)(2,1)S(1)} %pad_maximum_fusion.own), channel_id=1, source_target_pairs={{0,16},{1,17},{2,18},{3,19},{4,20},{5,21},{6,22},{7,23},{8,24},{9,... | collective-permute-start | bytes 1572872 | tf_op jit(solution)/shard_map/ppermute | solution.py:46
  22.4 10.0 %collective-permute-start.5 = (bf16[128,2048]{1,0:T(8,128)(2,1)S(1)}, bf16[128,2048]{1,0:T(8,128)(2,1)S(1)}, u32[]{:S(2)}, u32[]{:S(2)}) collective-permute-start(bf16[128,2048]{1,0:T(8,128)(2,1)S(1)} %collective-permute-done.1.other), channel_id=1, source_target_pairs={{0,16},{1,17},{2,18},{3,19},{4,20},{5,21},{6,22},{7,23},{8,24},{9,... | collective-permute-start | bytes 1572872 | tf_op jit(solution)/shard_map/ppermute | solution.py:46
  24.6 0.9 copy-start.6
  27.1 4.3 %collective-permute-start.6 = (bf16[256,512]{1,0:T(8,128)(2,1)S(1)}, bf16[256,512]{1,0:T(8,128)(2,1)S(1)}, u32[]{:S(2)}, u32[]{:S(2)}) collective-permute-start(bf16[256,512]{1,0:T(8,128)(2,1)S(1)} %get-tuple-element.28.seg), channel_id=1, source_target_pairs={{0,16},{1,17},{2,18},{3,19},{4,20},{5,21},{6,22},{7,23},{8,24},{9,... | collective-permute-start | bytes 786440 | tf_op jit(solution)/shard_map/ppermute | solution.py:46
  27.2 1.6 %collective-permute-start.7 = (bf16[128,256]{1,0:T(8,128)(2,1)S(1)}, bf16[128,256]{1,0:T(8,128)(2,1)S(1)}, u32[]{:S(2)}, u32[]{:S(2)}) collective-permute-start(bf16[128,256]{1,0:T(8,128)(2,1)S(1)} %get-tuple-element.30), channel_id=1, source_target_pairs={{0,16},{1,17},{2,18},{3,19},{4,20},{5,21},{6,22},{7,23},{8,24},{9,... | collective-permute-start | bytes 196616 | tf_op jit(solution)/shard_map/ppermute | solution.py:46
  27.7 28.4 %collective-permute-start.9 = (bf16[1024,128]{1,0:T(8,128)(2,1)}, bf16[1024,128]{1,0:T(8,128)(2,1)S(1)}, u32[]{:S(2)}, u32[]{:S(2)}) collective-permute-start(bf16[1024,128]{1,0:T(8,128)(2,1)} %get-tuple-element.24.q), channel_id=1, source_target_pairs={{0,64},{1,65},{2,66},{3,67},{4,68},{5,69},{6,70},{7,71},{8,72},{9,... | collective-permute-start | bytes 786440 | tf_op jit(solution)/shard_map/ppermute | solution.py:46
  27.7 104.9 %collective-permute-start.15 = (bf16[256,1024]{1,0:T(8,128)(2,1)}, bf16[256,1024]{1,0:T(8,128)(2,1)S(1)}, u32[]{:S(2)}, u32[]{:S(2)}) collective-permute-start(bf16[256,1024]{1,0:T(8,128)(2,1)} %get-tuple-element.38), channel_id=1, source_target_pairs={{0,4},{1,5},{2,6},{3,7},{4,8},{5,9},{6,10},{7,11},{8,12},{9,13},{1... | collective-permute-start | bytes 1572872 | tf_op jit(solution)/shard_map/ppermute | solution.py:46
  28.8 105.6 %collective-permute-start.16 = (bf16[256,1024]{1,0:T(8,128)(2,1)}, bf16[256,1024]{1,0:T(8,128)(2,1)S(1)}, u32[]{:S(2)}, u32[]{:S(2)}) collective-permute-start(bf16[256,1024]{1,0:T(8,128)(2,1)} %get-tuple-element.39), channel_id=1, source_target_pairs={{0,8},{1,9},{2,10},{3,11},{4,12},{5,13},{6,14},{7,15},{8,0},{9,1},... | collective-permute-start | bytes 1572872 | tf_op jit(solution)/shard_map/ppermute | solution.py:46
  31.4 102.9 %collective-permute-start.17 = (bf16[256,1024]{1,0:T(8,128)(2,1)}, bf16[256,1024]{1,0:T(8,128)(2,1)S(1)}, u32[]{:S(2)}, u32[]{:S(2)}) collective-permute-start(bf16[256,1024]{1,0:T(8,128)(2,1)} %get-tuple-element.40), channel_id=1, source_target_pairs={{0,12},{1,13},{2,14},{3,15},{4,0},{5,1},{6,2},{7,3},{8,4},{9,5},{1... | collective-permute-start | bytes 1572872 | tf_op jit(solution)/shard_map/ppermute | solution.py:46
  56.0 47.1 %collective-permute-start.8 = (bf16[1184,128]{1,0:T(8,128)(2,1)S(1)}, bf16[1184,128]{1,0:T(8,128)(2,1)S(1)}, u32[]{:S(2)}, u32[]{:S(2)}) collective-permute-start(bf16[1184,128]{1,0:T(8,128)(2,1)S(1)} %shard_map.143), channel_id=1, source_target_pairs={{0,96},{1,97},{2,98},{3,99},{4,100},{5,101},{6,102},{7,103},{8,104... | collective-permute-start | bytes 909320 | tf_op jit(solution)/shard_map/ppermute | solution.py:46
  79.5 25.1 %copy-start.5 = (bf16[1024,128]{1,0:T(8,128)(2,1)S(1)}, bf16[1024,128]{1,0:T(8,128)(2,1)}, u32[]{:S(2)}) copy-start(bf16[1024,128]{1,0:T(8,128)(2,1)} %get-tuple-element.24.q) | copy-start | bytes 786436
  79.5 49.4 %collective-permute-start.10 = (bf16[1184,128]{1,0:T(8,128)(2,1)S(1)}, bf16[1184,128]{1,0:T(8,128)(2,1)S(1)}, u32[]{:S(2)}, u32[]{:S(2)}) collective-permute-start(bf16[1184,128]{1,0:T(8,128)(2,1)S(1)} %shard_map.144), channel_id=1, source_target_pairs={{0,64},{1,65},{2,66},{3,67},{4,68},{5,69},{6,70},{7,71},{8,72},{9,... | collective-permute-start | bytes 909320 | tf_op jit(solution)/shard_map/ppermute | solution.py:46
  103.0 39.2 %copy-start.4 = (bf16[256,1024]{1,0:T(8,128)(2,1)S(1)}, bf16[256,1024]{1,0:T(8,128)(2,1)}, u32[]{:S(2)}) copy-start(bf16[256,1024]{1,0:T(8,128)(2,1)} %get-tuple-element.37.w0) | copy-start | bytes 1572868
  103.0 25.8 %collective-permute-start.11 = (bf16[1184,128]{1,0:T(8,128)(2,1)S(1)}, bf16[1184,128]{1,0:T(8,128)(2,1)S(1)}, u32[]{:S(2)}, u32[]{:S(2)}) collective-permute-start(bf16[1184,128]{1,0:T(8,128)(2,1)S(1)} %shard_map.145), channel_id=1, source_target_pairs={{0,32},{1,33},{2,34},{3,35},{4,36},{5,37},{6,38},{7,39},{8,40},{9,... | collective-permute-start | bytes 909320 | tf_op jit(solution)/shard_map/ppermute | solution.py:46
  131.3 10.3 %collective-permute-start.12 = (bf16[576,256]{1,0:T(8,128)(2,1)S(1)}, bf16[576,256]{1,0:T(8,128)(2,1)S(1)}, u32[]{:S(2)}, u32[]{:S(2)}) collective-permute-start(bf16[576,256]{1,0:T(8,128)(2,1)S(1)} %get-tuple-element.34), channel_id=1, source_target_pairs={{0,4},{1,5},{2,6},{3,7},{4,8},{5,9},{6,10},{7,11},{8,12},{9,13},{1... | collective-permute-start | bytes 884744 | tf_op jit(solution)/shard_map/ppermute | solution.py:46
  131.9 9.7 %collective-permute-start.13 = (bf16[576,256]{1,0:T(8,128)(2,1)S(1)}, bf16[576,256]{1,0:T(8,128)(2,1)S(1)}, u32[]{:S(2)}, u32[]{:S(2)}) collective-permute-start(bf16[576,256]{1,0:T(8,128)(2,1)S(1)} %get-tuple-element.35), channel_id=1, source_target_pairs={{0,8},{1,9},{2,10},{3,11},{4,12},{5,13},{6,14},{7,15},{8,0},{9,1},... | collective-permute-start | bytes 884744 | tf_op jit(solution)/shard_map/ppermute | solution.py:46
  132.6 9.7 %collective-permute-start.14 = (bf16[576,256]{1,0:T(8,128)(2,1)S(1)}, bf16[576,256]{1,0:T(8,128)(2,1)S(1)}, u32[]{:S(2)}, u32[]{:S(2)}) collective-permute-start(bf16[576,256]{1,0:T(8,128)(2,1)S(1)} %get-tuple-element.36), channel_id=1, source_target_pairs={{0,12},{1,13},{2,14},{3,15},{4,0},{5,1},{6,2},{7,3},{8,4},{9,5},{1... | collective-permute-start | bytes 884744 | tf_op jit(solution)/shard_map/ppermute | solution.py:46
  143.5 7.9 %collective-permute-start.18 = (bf16[576,256]{1,0:T(8,128)(2,1)S(1)}, bf16[576,256]{1,0:T(8,128)(2,1)S(1)}, u32[]{:S(2)}, u32[]{:S(2)}) collective-permute-start(bf16[576,256]{1,0:T(8,128)(2,1)S(1)} %get-tuple-element.43), channel_id=1, source_target_pairs={{0,1},{1,2},{2,3},{3,0},{4,5},{5,6},{6,7},{7,4},{8,9},{9,10},{10,1... | collective-permute-start | bytes 884744 | tf_op jit(solution)/shard_map/ppermute | solution.py:46
  145.2 10.6 %collective-permute-start.19 = (bf16[576,256]{1,0:T(8,128)(2,1)S(1)}, bf16[576,256]{1,0:T(8,128)(2,1)S(1)}, u32[]{:S(2)}, u32[]{:S(2)}) collective-permute-start(bf16[576,256]{1,0:T(8,128)(2,1)S(1)} %get-tuple-element.44), channel_id=1, source_target_pairs={{0,2},{1,3},{2,0},{3,1},{4,6},{5,7},{6,4},{7,5},{8,10},{9,11},{10,... | collective-permute-start | bytes 884744 | tf_op jit(solution)/shard_map/ppermute | solution.py:46
  148.2 7.6 %collective-permute-start.20 = (bf16[576,256]{1,0:T(8,128)(2,1)S(1)}, bf16[576,256]{1,0:T(8,128)(2,1)S(1)}, u32[]{:S(2)}, u32[]{:S(2)}) collective-permute-start(bf16[576,256]{1,0:T(8,128)(2,1)S(1)} %get-tuple-element.45), channel_id=1, source_target_pairs={{0,3},{1,0},{2,1},{3,2},{4,7},{5,4},{6,5},{7,6},{8,11},{9,8},{10,9... | collective-permute-start | bytes 884744 | tf_op jit(solution)/shard_map/ppermute | solution.py:46
where the time goes:
time: 158 us; the launch traced here: 157 us
  Pallas kernels  109 us (69%)
  starting transfers between devices  23.1 us (15%)
  waiting for transfers between devices  22 us (14%)
    pallas_call x4, Pallas kernels, attend(): pl.pallas_call(functools.partial(attend_kernel, step), in_specs=[smem()]...  94.7 us
    ppermute x21, starting transfers between devices, send(): return lax.ppermute(value, AXES, pairs_of(move))  23.1 us
    ppermute x21, waiting for transfers between devices, send(): return lax.ppermute(value, AXES, pairs_of(move))  22 us
    pallas_call x1, Pallas kernels, project(): pl.pallas_call(project_kernel, in_specs=[smem(), remain, vmem()] + [remai...  7.33 us
  transfers between devices with their start and end apart: 21, of which 8 were waited for; matrix products, arithmetic and copies ran while one was open for 0% of the time, Pallas kernels for 67%

commit v1 on v0

--- a/solution.py
+++ b/solution.py
@@ -70,6 +70,11 @@
     )
 
 
+def position():
+    seq, tp = lax.axis_index("seq"), lax.axis_index("tp")
+    return seq >> 1, seq & 1, tp >> 2, tp & 3, tp & 1, seq, tp >> 1
+
+
 def signs():
     index = np.arange(HD)
     both = index[:, None] & index[None, :]
@@ -99,10 +104,10 @@
 
 
 def project_kernel(
-    info, tokens, gain, w_q, w_kt, w_vt, near, far, sign, w_out, q_out, kv_out, w0, w1, w2, w3,
+    tokens, gain, w_q, w_kt, w_vt, near, far, sign, w_out, q_out, kv_out, w0, w1, w2, w3,
     held, held_q, held_kv, held_near, held_w, sum_q, sum_kv, sems, cut_sems,
 ):
-    core, z, y, parity, number = info[1], info[2], info[3], info[4], info[5]
+    x, core, z, y, parity, number, group = position()
     span, width = tokens.shape
     block = width // CHUNKS
     parts = [pl.ds(i * block, block) for i in range(CHUNKS)]
@@ -179,12 +184,12 @@
         copy.wait()
 
 
-def project(info, tokens, gain, w_q, w_kt, w_vt, near, far, sign, w_out):
+def project(tokens, gain, w_q, w_kt, w_vt, near, far, sign, w_out):
     span, width = tokens.shape
     remain = pl.BlockSpec(memory_space=pl.ANY)
     return pl.pallas_call(
         project_kernel,
-        in_specs=[smem(), remain, vmem()] + [remain] * 4 + [vmem(), vmem(), remain],
+        in_specs=[remain, vmem()] + [remain] * 4 + [vmem(), vmem(), remain],
         out_specs=[vmem(), vmem()] + [remain] * 4,
         out_shape=[
             jax.ShapeDtypeStruct((2 * span, HD), BF16),
@@ -205,11 +210,11 @@
         cost_estimate=pl.CostEstimate(
             flops=2 * span * width * 384, bytes_accessed=7 << 20, transcendentals=0
         ),
-    )(info, tokens, gain, w_q, w_kt, w_vt, near, far, sign, w_out)
-
-
-def segment_kernel(info, own, other, near, far, sign, rows, owners, seg_out, stay_out, go_out):
-    x, core, z, y, parity, number, group = (info[i] for i in range(7))
+    )(tokens, gain, w_q, w_kt, w_vt, near, far, sign, w_out)
+
+
+def segment_kernel(own, other, near, far, sign, rows, owners, seg_out, stay_out, go_out):
+    x, core, z, y, parity, number, group = position()
     odd = parity == 1
     mine, theirs = own[...].astype(F32), other[...].astype(F32)
     first = jnp.where(odd, theirs, mine)
@@ -264,15 +269,11 @@
     return pl.BlockSpec(memory_space=pltpu.VMEM)
 
 
-def smem():
-    return pl.BlockSpec(memory_space=pltpu.SMEM)
-
-
-def segment(info, own, other, near, far, sign, rows, owners):
+def segment(own, other, near, far, sign, rows, owners):
     span = own.shape[0]
     return pl.pallas_call(
         segment_kernel,
-        in_specs=[smem()] + [vmem()] * 7,
+        in_specs=[vmem()] * 7,
         out_specs=[vmem()] * 3,
         out_shape=[jax.ShapeDtypeStruct((2 * HD, span), BF16)]
         + [jax.ShapeDtypeStruct((128, 2 * HD), BF16)] * 2,
@@ -280,13 +281,13 @@
         cost_estimate=pl.CostEstimate(
             flops=400_000_000, bytes_accessed=2 << 20, transcendentals=0
         ),
-    )(info, own, other, near, far, sign, rows, owners)
+    )(own, other, near, far, sign, rows, owners)
 
 
 def attend_kernel(
-    step, info, q, own, other, sib_own, sib_other, seg, sib_seg, stay, came, out, acc, total, top, held
+    step, q, own, other, sib_own, sib_other, seg, sib_seg, stay, came, out, acc, total, top, held
 ):
-    x, core = info[0], info[1]
+    x, core = position()[:2]
     rows = q.shape[0]
     span = seg.shape[1]
     blocks = own.shape[1] // TILE
@@ -435,11 +436,11 @@
         ]
 
 
-def attend(step, info, q, *rest):
+def attend(step, q, *rest):
     rows = q.shape[0]
     return pl.pallas_call(
         functools.partial(attend_kernel, step),
-        in_specs=[smem()] + [vmem()] * 9,
+        in_specs=[vmem()] * 9,
         out_specs=vmem(),
         out_shape=jax.ShapeDtypeStruct((rows + EXTRA, HD), BF16),
         scratch_shapes=[pltpu.VMEM((rows, HD), F32)] * 3 + [pltpu.VMEM((2 * HD, TILE), BF16)],
@@ -447,12 +448,7 @@
         cost_estimate=pl.CostEstimate(
             flops=8 * rows * HD * 4096, bytes_accessed=4 << 20, transcendentals=rows * 4096
         ),
-    )(info, q, *rest)
-
-
-def split(value):
-    high = value.astype(BF16)
-    return high, (value - high.astype(F32)).astype(BF16)
+    )(q, *rest)
 
 
 def shuffle(rows, source):
@@ -462,8 +458,8 @@
     return jnp.dot(moves, rows, preferred_element_type=F32).astype(BF16)
 
 
-def merge_kernel(info, p0, p1, p2, p3, sign, *outs):
-    parity = info[4]
+def merge_kernel(p0, p1, p2, p3, sign, *outs):
+    parity = position()[4]
     parts = (p0, p1, p2, p3)
     rows = p0.shape[0] - EXTRA
     count = rows // HD
@@ -484,16 +480,12 @@
         left, right = [], []
         for share, part in zip(shares, parts):
             block = part[b * HD:(b + 1) * HD, :]
-            high, low = split(share[b:b + 1, :])
-            for piece in (high, low):
-                left.append(jnp.where(eye, piece.astype(F32), 0.0).astype(BF16))
-                right.append(block)
+            left.append(jnp.where(eye, share[b:b + 1, :], 0.0).astype(BF16))
+            right.append(block)
         mixed = jnp.dot(
             jnp.concatenate(left, 1), jnp.concatenate(right, 0), preferred_element_type=F32
         )
-        high, low = split(mixed)
-        plain = lax.dot_general(high, turn, NT, preferred_element_type=F32)
-        plain = plain + lax.dot_general(low, turn, NT, preferred_element_type=F32)
+        plain = lax.dot_general(mixed.astype(BF16), turn, NT, preferred_element_type=F32)
         head, place = b // per_head, b % per_head
         block = (plain * HD ** -0.5).astype(BF16)
         for out in outs:
@@ -513,18 +505,18 @@
         out[rows // 2:, :] = kept[64 * k:64 * (k + 1), :]
 
 
-def merge(info, parts, sign):
+def merge(parts, sign):
     rows = parts[0].shape[0] - EXTRA
     return pl.pallas_call(
         merge_kernel,
-        in_specs=[smem()] + [vmem()] * 5,
+        in_specs=[vmem()] * 5,
         out_specs=[vmem()] * RING,
         out_shape=[jax.ShapeDtypeStruct((rows // 2 + 64, 2 * HD), BF16)] * RING,
         compiler_params=pltpu.CompilerParams(vmem_limit_bytes=24 << 20),
         cost_estimate=pl.CostEstimate(
             flops=400_000_000, bytes_accessed=2 << 20, transcendentals=0
         ),
-    )(info, *parts, sign)
+    )(*parts, sign)
 
 
 def out_kernel(c0, c1, c2, c3, w0, w1, w2, w3, o0, o1, o2, o3, sum_out):
@@ -571,8 +563,8 @@
     )(*contexts, *weights)
 
 
-def finish_kernel(info, share, kept, a1, a2, a3, attn_out, kept_out):
-    x, core, z, y = (info[i] for i in range(4))
+def finish_kernel(share, kept, a1, a2, a3, attn_out, kept_out):
+    x, core, z, y = position()[:4]
     arrived = (a1, a2, a3)
     span = share.shape[0]
     whole = share[...]
@@ -592,30 +584,25 @@
     kept_out[...] = jnp.dot(moves, rows, preferred_element_type=F32).astype(BF16)
 
 
-def finish(info, share, kept, arrived):
+def finish(share, kept, arrived):
     return pl.pallas_call(
         finish_kernel,
-        in_specs=[smem()] + [vmem()] * 5,
+        in_specs=[vmem()] * 5,
         out_specs=[vmem()] * 2,
         out_shape=[
             jax.ShapeDtypeStruct(share.shape, BF16),
             jax.ShapeDtypeStruct((256, 2 * HD), BF16),
         ],
         compiler_params=pltpu.CompilerParams(vmem_limit_bytes=24 << 20),
-    )(info, share, kept, *arrived)
+    )(share, kept, *arrived)
 
 
 def shards(
     tokens, norm_gain, w_query, w_key, w_value, w_out, prefix_keys, prefix_values, keep_rows, owners
 ):
-    seq = lax.axis_index("seq")
-    tp = lax.axis_index("tp")
     seq_count = lax.axis_size("seq")
     span = tokens.shape[0]
     prefix_len = prefix_keys.shape[0] * seq_count
-    info = jnp.stack(
-        [seq // 2, seq % 2, tp // RING, tp % RING, tp % 2, seq, tp // 2, seq * 0]
-    ).astype(jnp.int32)
     near, far = rope_tables(span, seq_count, prefix_len)
     near, far = jnp.asarray(near), jnp.asarray(far)
     sign = jnp.asarray(signs(), BF16)
@@ -624,7 +611,7 @@
     other = to_head_pair(own)
     sib_own = to_sibling(own)
     q, kv, *pieces = project(
-        info, tokens, norm_gain.reshape(-1, HD), w_query, w_key.T, w_value.T, near, far, sign, w_out
+        tokens, norm_gain.reshape(-1, HD), w_query, w_key.T, w_value.T, near, far, sign, w_out
     )
     kv_other = to_head_pair(kv)
     queries = [q] + [along_x(q, d) for d in (1, 2, 3)]
@@ -634,21 +621,22 @@
     )
     sib_other = to_sibling(other)
     seg, stay, go = segment(
-        info, kv, kv_other, near, far, sign, keep_rows[0], owners.reshape(owners.shape[1:3])
+        kv, kv_other, near, far, sign, keep_rows[0], owners.reshape(owners.shape[1:3])
     )
     came = to_sibling(go)
     sib_seg = to_sibling(seg)
+    queries[3], weights[2] = lax.optimization_barrier((queries[3], weights[2]))
     parts = [None] * RING
     for d in (3, 1, 2, 0):
         part = attend(
-            d, info, queries[d], own, other, sib_own, sib_other, seg, sib_seg, stay, came
+            d, queries[d], own, other, sib_own, sib_other, seg, sib_seg, stay, came
         )
         parts[d] = along_x(part, -d) if d else part
-    contexts = merge(info, parts, sign)
+    contexts = merge(parts, sign)
     contexts = [contexts[0]] + [along_first(contexts[d], d) for d in (1, 2, 3)]
     *shares, share = project_out(contexts, weights)
     arrived = [along_second(shares[k], k) for k in (1, 2, 3)]
-    return tuple(finish(info, share, shares[0], arrived))
+    return tuple(finish(share, shares[0], arrived))
 
 
 def solution(mesh):

time: 158 us -> 152 us (0.962)
  Pallas kernels: 109 us -> 104 us
  waiting for transfers between devices: 22 us -> 18 us
  starting transfers between devices: 23.1 us -> 26.9 us
    pallas_call x8, Pallas kernels: 108 us -> 103 us  [the longest x4 92.5 us: attend(): pl.pallas_call(functools.partial(attend_kernel, step), in_specs=[vmem()]...]
    ppermute x21, waiting for transfers between devices: 22 us -> 18 us  [send(): return lax.ppermute(value, AXES, pairs_of(move))]
    ppermute x21, starting transfers between devices: 23.1 us -> 26.9 us  [send(): return lax.ppermute(value, AXES, pairs_of(move))]
  transfers between devices with their start and end apart: 21 -> 21, of which waited for: 8 -> 6; matrix products, arithmetic and copies ran while one was open for 0% -> 0% of each run, Pallas kernels for 67% -> 67%
where the time goes in v1:
time: 152 us
  Pallas kernels  104 us (68%)
  starting transfers between devices  26.9 us (18%)
  waiting for transfers between devices  18 us (12%)
    pallas_call x4, Pallas kernels, attend(): pl.pallas_call(functools.partial(attend_kernel, step), in_specs=[vmem()]...  92.5 us
    ppermute x21, starting transfers between devices, send(): return lax.ppermute(value, AXES, pairs_of(move))  26.9 us
    ppermute x21, waiting for transfers between devices, send(): return lax.ppermute(value, AXES, pairs_of(move))  18 us
    pallas_call x1, Pallas kernels, project(): pl.pallas_call(project_kernel, in_specs=[remain, vmem()] + [remain] * 4 +...  7.32 us
  transfers between devices with their start and end apart: 21, of which 6 were waited for; matrix products, arithmetic and copies ran while one was open for 0% of the time, Pallas kernels for 67%

profile of v1, /device:TPU:1, one launch (start us, length us, event | category | flops | bytes accessed | tf_op | source)
XLA Modules:
  0.0 152.3 jit_solution(4679465300438756478)
XLA Ops:
  0.6 1.1 pad_maximum_fusion.own
  1.7 2.2 %collective-permute-start.1 = (bf16[128,2048]{1,0:T(8,128)(2,1)S(1)}, bf16[128,2048]{1,0:T(8,128)(2,1)S(1)}, u32[]{:S(2)}, u32[]{:S(2)}) collective-permute-start(bf16[128,2048]{1,0:T(8,128)(2,1)S(1)} %pad_maximum_fusion.own), channel_id=1, source_target_pairs={{0,1},{1,0},{2,3},{3,2},{4,5},{5,4},{6,7},{7,6},{8,9},{9,8},{10,11... | collective-permute-start | bytes 1572872 | tf_op jit(solution)/shard_map/ppermute | solution.py:46
  3.9 0.0 copy-start.6
  3.9 7.3 %shard_map.140 = (bf16[1024,128]{1,0:T(8,128)(2,1)}, bf16[512,128]{1,0:T(8,128)(2,1)}, bf16[256,1024]{1,0:T(8,128)(2,1)}, bf16[256,1024]{1,0:T(8,128)(2,1)}, bf1...) custom-call(bf16[512,4096]{1,0:T(8,128)(2,1)} %tokens.1, bf16[32,128]{1,0:T(8,128)(2,1)} %bitcast.15, ...), custom_call_target="tpu_custom_call" | custom-call | flops 1610612736 | bytes 7340032 | tf_op jit(solution)/shard_map/pallas_call | solution.py:190
  11.3 1.3 collective-permute-start.2
  12.5 1.5 collective-permute-start.3
  14.0 0.1 collective-permute-start
  14.1 3.0 %collective-permute-start.11 = (bf16[256,1024]{1,0:T(8,128)(2,1)}, bf16[256,1024]{1,0:T(8,128)(2,1)S(1)}, u32[]{:S(2)}, u32[]{:S(2)}) collective-permute-start(bf16[256,1024]{1,0:T(8,128)(2,1)} %get-tuple-element.35), channel_id=1, source_target_pairs={{0,8},{1,9},{2,10},{3,11},{4,12},{5,13},{6,14},{7,15},{8,0},{9,1},... | collective-permute-start | bytes 1572872 | tf_op jit(solution)/shard_map/ppermute | solution.py:46
  17.1 1.2 collective-permute-done.other
  18.3 3.7 %collective-permute-start.4 = (bf16[128,2048]{1,0:T(8,128)(2,1)S(1)}, bf16[128,2048]{1,0:T(8,128)(2,1)S(1)}, u32[]{:S(2)}, u32[]{:S(2)}) collective-permute-start(bf16[128,2048]{1,0:T(8,128)(2,1)S(1)} %pad_maximum_fusion.own), channel_id=1, source_target_pairs={{0,16},{1,17},{2,18},{3,19},{4,20},{5,21},{6,22},{7,23},{8,24},{9,... | collective-permute-start | bytes 1572872 | tf_op jit(solution)/shard_map/ppermute | solution.py:46
  22.1 0.0 collective-permute-done.2.q
  22.1 0.0 collective-permute-done.3.q
  22.1 0.0 collective-permute-done.1.other
  22.1 0.1 collective-permute-start.5
  22.2 0.0 copy-done.7
  22.2 0.0 copy-done
  22.2 0.0 copy-done.1
  22.2 0.0 copy-done.2
  22.2 0.0 copy-done.6
  22.2 0.0 copy-start.5
  22.3 0.9 copy-done.5
  23.2 1.0 shard_map.141
  24.2 0.6 collective-permute-start.6
  24.7 0.1 collective-permute-start.7
  24.8 2.3 %collective-permute-done.11.w2 = bf16[256,1024]{1,0:T(8,128)(2,1)S(1)} collective-permute-done((bf16[256,1024]{1,0:T(8,128)(2,1)}, bf16[256,1024]{1,0:T(8,128)(2,1)S(1)}, u32[]{:S(2)}, u32[]{:S(2)}) %collective-permute-start.11) | collective-permute-done | bytes 524320 | tf_op jit(solution)/shard_map/ppermute | solution.py:46
  27.1 2.7 %collective-permute-start.9 = (bf16[1024,128]{1,0:T(8,128)(2,1)}, bf16[1024,128]{1,0:T(8,128)(2,1)S(1)}, u32[]{:S(2)}, u32[]{:S(2)}) collective-permute-start(bf16[1024,128]{1,0:T(8,128)(2,1)} %get-tuple-element.26.q), channel_id=1, source_target_pairs={{0,64},{1,65},{2,66},{3,67},{4,68},{5,69},{6,70},{7,71},{8,72},{9,... | collective-permute-start | bytes 786440 | tf_op jit(solution)/shard_map/ppermute | solution.py:46
  29.9 0.0 collective-permute-done.4.sib_own
  29.9 0.0 collective-permute-start.16
  29.9 0.0 collective-permute-done.7.came
  29.9 2.7 %collective-permute-start.17 = (bf16[256,1024]{1,0:T(8,128)(2,1)}, bf16[256,1024]{1,0:T(8,128)(2,1)S(1)}, u32[]{:S(2)}, u32[]{:S(2)}) collective-permute-start(bf16[256,1024]{1,0:T(8,128)(2,1)} %get-tuple-element.44), channel_id=1, source_target_pairs={{0,12},{1,13},{2,14},{3,15},{4,0},{5,1},{6,2},{7,3},{8,4},{9,5},{1... | collective-permute-start | bytes 1572872 | tf_op jit(solution)/shard_map/ppermute | solution.py:46
  32.6 0.0 collective-permute-done.6.sib_seg
  32.6 0.0 collective-permute-done.5.sib_other
  32.6 23.1 %shard_map.145 = bf16[1184,128]{1,0:T(8,128)(2,1)S(1)} custom-call(bf16[1024,128]{1,0:T(8,128)(2,1)S(1)} %collective-permute-done.3.q, bf16[128,2048]{1,0:T(8,128)(2,1)S(1)} %pad_maximum_fusion.own, bf16[128,2048]{1,0:T(8,128)(2,1)S(1)} %collective-permute-done.1.other, bf16[128,2048]{1,0:T(8,128)(2,1)S(1)} %collective-permute-done.4.sib_own, ...), custom_call_target="tpu_custom_call" | custom-call | flops 4294967296 | bytes 4194304 | tf_op jit(solution)/shard_map/pallas_call | solution.py:441
  55.6 0.4 collective-permute-start.12
  56.0 0.0 collective-permute-done.9.q
  56.0 22.9 %shard_map.144 = bf16[1184,128]{1,0:T(8,128)(2,1)S(1)} custom-call(bf16[1024,128]{1,0:T(8,128)(2,1)S(1)} %collective-permute-done.9.q, bf16[128,2048]{1,0:T(8,128)(2,1)S(1)} %pad_maximum_fusion.own, bf16[128,2048]{1,0:T(8,128)(2,1)S(1)} %collective-permute-done.1.other, bf16[128,2048]{1,0:T(8,128)(2,1)S(1)} %collective-permute-done.4.sib_own, ...), custom_call_target="tpu_custom_call" | custom-call | flops 4294967296 | bytes 4194304 | tf_op jit(solution)/shard_map/pallas_call | solution.py:441
  78.9 0.0 copy-start.4
  78.9 0.1 collective-permute-start.10
  79.0 22.9 %shard_map.143 = bf16[1184,128]{1,0:T(8,128)(2,1)S(1)} custom-call(bf16[1024,128]{1,0:T(8,128)(2,1)S(1)} %collective-permute-done.2.q, bf16[128,2048]{1,0:T(8,128)(2,1)S(1)} %pad_maximum_fusion.own, bf16[128,2048]{1,0:T(8,128)(2,1)S(1)} %collective-permute-done.1.other, bf16[128,2048]{1,0:T(8,128)(2,1)S(1)} %collective-permute-done.4.sib_own, ...), custom_call_target="tpu_custom_call" | custom-call | flops 4294967296 | bytes 4194304 | tf_op jit(solution)/shard_map/pallas_call | solution.py:441
  101.9 0.0 copy-start.3
  101.9 0.1 collective-permute-start.8
  102.0 0.0 copy-done.4
  102.0 23.7 %shard_map.142.p0 = bf16[1184,128]{1,0:T(8,128)(2,1)S(1)} custom-call(bf16[1024,128]{1,0:T(8,128)(2,1)S(1)} %copy-done.4, bf16[128,2048]{1,0:T(8,128)(2,1)S(1)} %pad_maximum_fusion.own, bf16[128,2048]{1,0:T(8,128)(2,1)S(1)} %collective-permute-done.1.other, bf16[128,2048]{1,0:T(8,128)(2,1)S(1)} %collective-permute-done.4.sib_own, ...), custom_call_target="tpu_custom_call" | custom-call | flops 4294967296 | bytes 4194304 | tf_op jit(solution)/shard_map/pallas_call | solution.py:441
  125.7 0.0 collective-permute-done.12.p3
  125.7 0.0 collective-permute-done.10.p2
  125.7 0.0 collective-permute-done.8.p1
  125.7 1.3 shard_map.146
  127.0 0.1 collective-permute-start.13
  127.1 1.2 collective-permute-start.14
  128.3 1.5 collective-permute-start.15
  129.8 0.0 collective-permute-done.16.w1
  129.8 0.0 collective-permute-done.17.w3
  129.8 7.3 %collective-permute-done.13.c1 = bf16[576,256]{1,0:T(8,128)(2,1)S(1)} collective-permute-done((bf16[576,256]{1,0:T(8,128)(2,1)S(1)}, bf16[576,256]{1,0:T(8,128)(2,1)S(1)}, u32[]{:S(2)}, u32[]{:S(2)}) %collective-permute-start.13) | collective-permute-done | bytes 294944 | tf_op jit(solution)/shard_map/ppermute | solution.py:46
  137.1 0.0 collective-permute-done.14.c2
  137.1 0.6 collective-permute-done.15.c3
  137.7 0.0 copy-done.3
  137.7 1.3 shard_map.147
  139.0 1.7 %collective-permute-start.18 = (bf16[576,256]{1,0:T(8,128)(2,1)S(1)}, bf16[576,256]{1,0:T(8,128)(2,1)S(1)}, u32[]{:S(2)}, u32[]{:S(2)}) collective-permute-start(bf16[576,256]{1,0:T(8,128)(2,1)S(1)} %get-tuple-element.47), channel_id=1, source_target_pairs={{0,1},{1,2},{2,3},{3,0},{4,5},{5,6},{6,7},{7,4},{8,9},{9,10},{10,1... | collective-permute-start | bytes 884744 | tf_op jit(solution)/shard_map/ppermute | solution.py:46
  140.7 3.3 %collective-permute-start.19 = (bf16[576,256]{1,0:T(8,128)(2,1)S(1)}, bf16[576,256]{1,0:T(8,128)(2,1)S(1)}, u32[]{:S(2)}, u32[]{:S(2)}) collective-permute-start(bf16[576,256]{1,0:T(8,128)(2,1)S(1)} %get-tuple-element.48), channel_id=1, source_target_pairs={{0,2},{1,3},{2,0},{3,1},{4,6},{5,7},{6,4},{7,5},{8,10},{9,11},{10,... | collective-permute-start | bytes 884744 | tf_op jit(solution)/shard_map/ppermute | solution.py:46
  144.0 0.7 collective-permute-start.20
  144.7 2.2 %collective-permute-done.18.a1 = bf16[576,256]{1,0:T(8,128)(2,1)S(1)} collective-permute-done((bf16[576,256]{1,0:T(8,128)(2,1)S(1)}, bf16[576,256]{1,0:T(8,128)(2,1)S(1)}, u32[]{:S(2)}, u32[]{:S(2)}) %collective-permute-start.18) | collective-permute-done | bytes 294944 | tf_op jit(solution)/shard_map/ppermute | solution.py:46
  146.9 4.3 %collective-permute-done.19.a2 = bf16[576,256]{1,0:T(8,128)(2,1)S(1)} collective-permute-done((bf16[576,256]{1,0:T(8,128)(2,1)S(1)}, bf16[576,256]{1,0:T(8,128)(2,1)S(1)}, u32[]{:S(2)}, u32[]{:S(2)}) %collective-permute-start.19) | collective-permute-done | bytes 294944 | tf_op jit(solution)/shard_map/ppermute | solution.py:46
  151.3 0.0 collective-permute-done.20.a3
  151.3 1.0 shard_map.148
  (5 shorter events, 0.0 us)
Async XLA Ops:
  1.7 20.4 %collective-permute-start.1 = (bf16[128,2048]{1,0:T(8,128)(2,1)S(1)}, bf16[128,2048]{1,0:T(8,128)(2,1)S(1)}, u32[]{:S(2)}, u32[]{:S(2)}) collective-permute-start(bf16[128,2048]{1,0:T(8,128)(2,1)S(1)} %pad_maximum_fusion.own), channel_id=1, source_target_pairs={{0,1},{1,0},{2,3},{3,2},{4,5},{5,4},{6,7},{7,6},{8,9},{9,8},{10,11... | collective-permute-start | bytes 1572872 | tf_op jit(solution)/shard_map/ppermute | solution.py:46
  3.9 18.3 %copy-start.7 = (s32[1,8,384,1]{2,3,1,0:T(1,128)S(1)}, s32[1,8,384,1]{2,3,1,0:T(1,128)}, u32[]{:S(2)}) copy-start(s32[1,8,384,1]{2,3,1,0:T(1,128)} %param.22) | copy-start | bytes 36868
  3.9 18.3 %copy-start = (f32[2,512,128]{2,1,0:T(8,128)S(1)}, f32[2,512,128]{2,1,0:T(8,128)}, u32[]{:S(2)}) copy-start(f32[2,512,128]{2,1,0:T(8,128)} %constant.6.clone.near) | copy-start | bytes 1572868
  3.9 18.3 %copy-start.1 = (bf16[2,128,128]{2,1,0:T(8,128)(2,1)S(1)}, bf16[2,128,128]{2,1,0:T(8,128)(2,1)}, u32[]{:S(2)}) copy-start(bf16[2,128,128]{2,1,0:T(8,128)(2,1)} %constant.8.clone.sign) | copy-start | bytes 196612
  3.9 18.3 %copy-start.2 = (f32[2,8,128]{2,1,0:T(8,128)S(1)}, f32[2,8,128]{2,1,0:T(8,128)}, u32[]{:S(2)}) copy-start(f32[2,8,128]{2,1,0:T(8,128)} %constant.7.clone.far) | copy-start | bytes 24580
  3.9 18.3 %copy-start.6 = (s32[1,8,384]{2,1,0:T(8,128)S(1)}, s32[1,8,384]{2,1,0:T(8,128)}, u32[]{:S(2)}) copy-start(s32[1,8,384]{2,1,0:T(8,128)} %param.21) | copy-start | bytes 36868
  11.3 10.8 %collective-permute-start.2 = (bf16[1024,128]{1,0:T(8,128)(2,1)}, bf16[1024,128]{1,0:T(8,128)(2,1)S(1)}, u32[]{:S(2)}, u32[]{:S(2)}) collective-permute-start(bf16[1024,128]{1,0:T(8,128)(2,1)} %get-tuple-element.26.q), channel_id=1, source_target_pairs={{0,32},{1,33},{2,34},{3,35},{4,36},{5,37},{6,38},{7,39},{8,40},{9,... | collective-permute-start | bytes 786440 | tf_op jit(solution)/shard_map/ppermute | solution.py:46
  12.5 9.5 %collective-permute-start.3 = (bf16[1024,128]{1,0:T(8,128)(2,1)}, bf16[1024,128]{1,0:T(8,128)(2,1)S(1)}, u32[]{:S(2)}, u32[]{:S(2)}) collective-permute-start(bf16[1024,128]{1,0:T(8,128)(2,1)} %get-tuple-element.26.q), channel_id=1, source_target_pairs={{0,96},{1,97},{2,98},{3,99},{4,100},{5,101},{6,102},{7,103},{8,104... | collective-permute-start | bytes 786440 | tf_op jit(solution)/shard_map/ppermute | solution.py:46
  14.0 4.3 %collective-permute-start = (bf16[512,128]{1,0:T(8,128)(2,1)}, bf16[512,128]{1,0:T(8,128)(2,1)S(1)}, u32[]{:S(2)}, u32[]{:S(2)}) collective-permute-start(bf16[512,128]{1,0:T(8,128)(2,1)} %get-tuple-element.27.own), channel_id=1, source_target_pairs={{0,1},{1,0},{2,3},{3,2},{4,5},{5,4},{6,7},{7,6},{8,9},{9,8},{10,11... | collective-permute-start | bytes 393224 | tf_op jit(solution)/shard_map/ppermute | solution.py:46
  14.1 13.1 %collective-permute-start.11 = (bf16[256,1024]{1,0:T(8,128)(2,1)}, bf16[256,1024]{1,0:T(8,128)(2,1)S(1)}, u32[]{:S(2)}, u32[]{:S(2)}) collective-permute-start(bf16[256,1024]{1,0:T(8,128)(2,1)} %get-tuple-element.35), channel_id=1, source_target_pairs={{0,8},{1,9},{2,10},{3,11},{4,12},{5,13},{6,14},{7,15},{8,0},{9,1},... | collective-permute-start | bytes 1572872 | tf_op jit(solution)/shard_map/ppermute | solution.py:46
  18.3 11.6 %collective-permute-start.4 = (bf16[128,2048]{1,0:T(8,128)(2,1)S(1)}, bf16[128,2048]{1,0:T(8,128)(2,1)S(1)}, u32[]{:S(2)}, u32[]{:S(2)}) collective-permute-start(bf16[128,2048]{1,0:T(8,128)(2,1)S(1)} %pad_maximum_fusion.own), channel_id=1, source_target_pairs={{0,16},{1,17},{2,18},{3,19},{4,20},{5,21},{6,22},{7,23},{8,24},{9,... | collective-permute-start | bytes 1572872 | tf_op jit(solution)/shard_map/ppermute | solution.py:46
  22.1 10.5 %collective-permute-start.5 = (bf16[128,2048]{1,0:T(8,128)(2,1)S(1)}, bf16[128,2048]{1,0:T(8,128)(2,1)S(1)}, u32[]{:S(2)}, u32[]{:S(2)}) collective-permute-start(bf16[128,2048]{1,0:T(8,128)(2,1)S(1)} %collective-permute-done.1.other), channel_id=1, source_target_pairs={{0,16},{1,17},{2,18},{3,19},{4,20},{5,21},{6,22},{7,23},{8,24},{9,... | collective-permute-start | bytes 1572872 | tf_op jit(solution)/shard_map/ppermute | solution.py:46
  22.2 0.9 copy-start.5
  24.2 8.4 %collective-permute-start.6 = (bf16[256,512]{1,0:T(8,128)(2,1)S(1)}, bf16[256,512]{1,0:T(8,128)(2,1)S(1)}, u32[]{:S(2)}, u32[]{:S(2)}) collective-permute-start(bf16[256,512]{1,0:T(8,128)(2,1)S(1)} %get-tuple-element.30.seg), channel_id=1, source_target_pairs={{0,16},{1,17},{2,18},{3,19},{4,20},{5,21},{6,22},{7,23},{8,24},{9,... | collective-permute-start | bytes 786440 | tf_op jit(solution)/shard_map/ppermute | solution.py:46
  24.7 5.2 %collective-permute-start.7 = (bf16[128,256]{1,0:T(8,128)(2,1)S(1)}, bf16[128,256]{1,0:T(8,128)(2,1)S(1)}, u32[]{:S(2)}, u32[]{:S(2)}) collective-permute-start(bf16[128,256]{1,0:T(8,128)(2,1)S(1)} %get-tuple-element.32), channel_id=1, source_target_pairs={{0,16},{1,17},{2,18},{3,19},{4,20},{5,21},{6,22},{7,23},{8,24},{9,... | collective-permute-start | bytes 196616 | tf_op jit(solution)/shard_map/ppermute | solution.py:46
  27.1 28.9 %collective-permute-start.9 = (bf16[1024,128]{1,0:T(8,128)(2,1)}, bf16[1024,128]{1,0:T(8,128)(2,1)S(1)}, u32[]{:S(2)}, u32[]{:S(2)}) collective-permute-start(bf16[1024,128]{1,0:T(8,128)(2,1)} %get-tuple-element.26.q), channel_id=1, source_target_pairs={{0,64},{1,65},{2,66},{3,67},{4,68},{5,69},{6,70},{7,71},{8,72},{9,... | collective-permute-start | bytes 786440 | tf_op jit(solution)/shard_map/ppermute | solution.py:46
  29.9 99.9 %collective-permute-start.16 = (bf16[256,1024]{1,0:T(8,128)(2,1)}, bf16[256,1024]{1,0:T(8,128)(2,1)S(1)}, u32[]{:S(2)}, u32[]{:S(2)}) collective-permute-start(bf16[256,1024]{1,0:T(8,128)(2,1)} %get-tuple-element.42), channel_id=1, source_target_pairs={{0,4},{1,5},{2,6},{3,7},{4,8},{5,9},{6,10},{7,11},{8,12},{9,13},{1... | collective-permute-start | bytes 1572872 | tf_op jit(solution)/shard_map/ppermute | solution.py:46
  29.9 99.9 %collective-permute-start.17 = (bf16[256,1024]{1,0:T(8,128)(2,1)}, bf16[256,1024]{1,0:T(8,128)(2,1)S(1)}, u32[]{:S(2)}, u32[]{:S(2)}) collective-permute-start(bf16[256,1024]{1,0:T(8,128)(2,1)} %get-tuple-element.44), channel_id=1, source_target_pairs={{0,12},{1,13},{2,14},{3,15},{4,0},{5,1},{6,2},{7,3},{8,4},{9,5},{1... | collective-permute-start | bytes 1572872 | tf_op jit(solution)/shard_map/ppermute | solution.py:46
  55.6 70.1 %collective-permute-start.12 = (bf16[1184,128]{1,0:T(8,128)(2,1)S(1)}, bf16[1184,128]{1,0:T(8,128)(2,1)S(1)}, u32[]{:S(2)}, u32[]{:S(2)}) collective-permute-start(bf16[1184,128]{1,0:T(8,128)(2,1)S(1)} %shard_map.145), channel_id=1, source_target_pairs={{0,32},{1,33},{2,34},{3,35},{4,36},{5,37},{6,38},{7,39},{8,40},{9,... | collective-permute-start | bytes 909320 | tf_op jit(solution)/shard_map/ppermute | solution.py:46
  78.9 23.1 %copy-start.4 = (bf16[1024,128]{1,0:T(8,128)(2,1)S(1)}, bf16[1024,128]{1,0:T(8,128)(2,1)}, u32[]{:S(2)}) copy-start(bf16[1024,128]{1,0:T(8,128)(2,1)} %get-tuple-element.26.q) | copy-start | bytes 786436
  78.9 46.8 %collective-permute-start.10 = (bf16[1184,128]{1,0:T(8,128)(2,1)S(1)}, bf16[1184,128]{1,0:T(8,128)(2,1)S(1)}, u32[]{:S(2)}, u32[]{:S(2)}) collective-permute-start(bf16[1184,128]{1,0:T(8,128)(2,1)S(1)} %shard_map.144), channel_id=1, source_target_pairs={{0,64},{1,65},{2,66},{3,67},{4,68},{5,69},{6,70},{7,71},{8,72},{9,... | collective-permute-start | bytes 909320 | tf_op jit(solution)/shard_map/ppermute | solution.py:46
  101.9 35.8 %copy-start.3 = (bf16[256,1024]{1,0:T(8,128)(2,1)S(1)}, bf16[256,1024]{1,0:T(8,128)(2,1)}, u32[]{:S(2)}) copy-start(bf16[256,1024]{1,0:T(8,128)(2,1)} %get-tuple-element.41.w0) | copy-start | bytes 1572868
  101.9 23.8 %collective-permute-start.8 = (bf16[1184,128]{1,0:T(8,128)(2,1)S(1)}, bf16[1184,128]{1,0:T(8,128)(2,1)S(1)}, u32[]{:S(2)}, u32[]{:S(2)}) collective-permute-start(bf16[1184,128]{1,0:T(8,128)(2,1)S(1)} %shard_map.143), channel_id=1, source_target_pairs={{0,96},{1,97},{2,98},{3,99},{4,100},{5,101},{6,102},{7,103},{8,104... | collective-permute-start | bytes 909320 | tf_op jit(solution)/shard_map/ppermute | solution.py:46
  127.0 10.0 %collective-permute-start.13 = (bf16[576,256]{1,0:T(8,128)(2,1)S(1)}, bf16[576,256]{1,0:T(8,128)(2,1)S(1)}, u32[]{:S(2)}, u32[]{:S(2)}) collective-permute-start(bf16[576,256]{1,0:T(8,128)(2,1)S(1)} %get-tuple-element.38), channel_id=1, source_target_pairs={{0,4},{1,5},{2,6},{3,7},{4,8},{5,9},{6,10},{7,11},{8,12},{9,13},{1... | collective-permute-start | bytes 884744 | tf_op jit(solution)/shard_map/ppermute | solution.py:46
  127.1 9.9 %collective-permute-start.14 = (bf16[576,256]{1,0:T(8,128)(2,1)S(1)}, bf16[576,256]{1,0:T(8,128)(2,1)S(1)}, u32[]{:S(2)}, u32[]{:S(2)}) collective-permute-start(bf16[576,256]{1,0:T(8,128)(2,1)S(1)} %get-tuple-element.39), channel_id=1, source_target_pairs={{0,8},{1,9},{2,10},{3,11},{4,12},{5,13},{6,14},{7,15},{8,0},{9,1},... | collective-permute-start | bytes 884744 | tf_op jit(solution)/shard_map/ppermute | solution.py:46
  128.3 9.4 %collective-permute-start.15 = (bf16[576,256]{1,0:T(8,128)(2,1)S(1)}, bf16[576,256]{1,0:T(8,128)(2,1)S(1)}, u32[]{:S(2)}, u32[]{:S(2)}) collective-permute-start(bf16[576,256]{1,0:T(8,128)(2,1)S(1)} %get-tuple-element.40), channel_id=1, source_target_pairs={{0,12},{1,13},{2,14},{3,15},{4,0},{5,1},{6,2},{7,3},{8,4},{9,5},{1... | collective-permute-start | bytes 884744 | tf_op jit(solution)/shard_map/ppermute | solution.py:46
  139.0 7.9 %collective-permute-start.18 = (bf16[576,256]{1,0:T(8,128)(2,1)S(1)}, bf16[576,256]{1,0:T(8,128)(2,1)S(1)}, u32[]{:S(2)}, u32[]{:S(2)}) collective-permute-start(bf16[576,256]{1,0:T(8,128)(2,1)S(1)} %get-tuple-element.47), channel_id=1, source_target_pairs={{0,1},{1,2},{2,3},{3,0},{4,5},{5,6},{6,7},{7,4},{8,9},{9,10},{10,1... | collective-permute-start | bytes 884744 | tf_op jit(solution)/shard_map/ppermute | solution.py:46
  140.7 10.6 %collective-permute-start.19 = (bf16[576,256]{1,0:T(8,128)(2,1)S(1)}, bf16[576,256]{1,0:T(8,128)(2,1)S(1)}, u32[]{:S(2)}, u32[]{:S(2)}) collective-permute-start(bf16[576,256]{1,0:T(8,128)(2,1)S(1)} %get-tuple-element.48), channel_id=1, source_target_pairs={{0,2},{1,3},{2,0},{3,1},{4,6},{5,7},{6,4},{7,5},{8,10},{9,11},{10,... | collective-permute-start | bytes 884744 | tf_op jit(solution)/shard_map/ppermute | solution.py:46
  144.0 7.3 %collective-permute-start.20 = (bf16[576,256]{1,0:T(8,128)(2,1)S(1)}, bf16[576,256]{1,0:T(8,128)(2,1)S(1)}, u32[]{:S(2)}, u32[]{:S(2)}) collective-permute-start(bf16[576,256]{1,0:T(8,128)(2,1)S(1)} %get-tuple-element.49), channel_id=1, source_target_pairs={{0,3},{1,0},{2,1},{3,2},{4,7},{5,4},{6,5},{7,6},{8,11},{9,8},{10,9... | collective-permute-start | bytes 884744 | tf_op jit(solution)/shard_map/ppermute | solution.py:46

commit v2 on v1

--- a/solution.py
+++ b/solution.py
@@ -20,6 +20,9 @@
 RING = 4
 TILE = 512
 CHUNKS = 4
+CUT_AT = 2
+WHOLE_AT = 1
+NOTE = 16
 EXTRA = 32 + 128
 
 NT = (((1,), (1,)), ((), ()))
@@ -124,12 +127,13 @@
             for j, (start, end) in enumerate(moves)
         ])
     tables = pltpu.make_async_copy(near, held_near, sems.at[4 * CHUNKS])
-    for copies in arrive:
+    whole = pltpu.make_async_copy(w_out, held_w, sems.at[4 * CHUNKS + 1])
+    for i, copies in enumerate(arrive):
         for copy in copies:
             copy.start()
+        if i == WHOLE_AT:
+            whole.start()
     tables.start()
-    whole = pltpu.make_async_copy(w_out, held_w, sems.at[4 * CHUNKS + 1])
-    whole.start()
     cuts = []
     for d, piece in enumerate((w0, w1, w2, w3)):
         for k in range(RING):
@@ -148,6 +152,10 @@
     for i, at in enumerate(parts):
         for copy in arrive[i]:
             copy.wait()
+        if i == CUT_AT:
+            whole.wait()
+            for copy in cuts:
+                copy.start()
         gains = jnp.concatenate([gain[j:j + 1, :] for j in range(i * per, (i + 1) * per)], 1)
         begin, end = i * block, (i + 1) * block
         hidden = held[:, begin:end].astype(F32)
@@ -166,9 +174,6 @@
         else:
             sum_q[...] += part_q
             sum_kv[...] += part_kv
-    whole.wait()
-    for copy in cuts:
-        copy.start()
     scale = lax.rsqrt(jnp.sum(squares, -1, keepdims=True) / width + EPSILON)
     kv_out[...] = (sum_kv[...] * scale).astype(BF16)
     tables.wait()
@@ -213,7 +218,13 @@
     )(tokens, gain, w_q, w_kt, w_vt, near, far, sign, w_out)
 
 
-def segment_kernel(own, other, near, far, sign, rows, owners, seg_out, stay_out, go_out):
+def largest(rows, axis):
+    return jnp.max(jnp.sum(rows * rows, axis, keepdims=True))
+
+
+def segment_kernel(
+    own, other, prefix, prefix_other, near, far, sign, rows, owners, seg_out, stay_out, go_out
+):
     x, core, z, y, parity, number, group = position()
     odd = parity == 1
     mine, theirs = own[...].astype(F32), other[...].astype(F32)
@@ -226,8 +237,13 @@
     key = (key * cosine + pltpu.roll(key, HALF, 1) * sine).astype(BF16)
     turn = sign[parity]
     unit = HD ** -0.5
-    seg_out[:HD, :] = (lax.dot_general(turn, key, TN, preferred_element_type=F32) * unit).astype(BF16)
-    seg_out[HD:, :] = (lax.dot_general(turn, value, TN, preferred_element_type=F32) * unit).astype(BF16)
+    for i, part in enumerate((key, value)):
+        turned = lax.dot_general(turn, part, TN, preferred_element_type=F32) * unit
+        seg_out[i * HD:(i + 1) * HD, :] = turned.astype(BF16)
+    longest = largest(seg_out[:HD, :].astype(F32), 0)
+    halves = [ref[:HALF, :].astype(F32) for ref in (prefix, prefix_other)]
+    longest = jnp.maximum(longest, largest(jnp.concatenate(halves, 0), 0)) * 1.01
+    seg_out[2 * HD:, :] = jnp.full((NOTE, own.shape[0]), longest, F32).astype(BF16)
     plain = sign[0]
     pair = jnp.concatenate(
         [
@@ -269,19 +285,19 @@
     return pl.BlockSpec(memory_space=pltpu.VMEM)
 
 
-def segment(own, other, near, far, sign, rows, owners):
+def segment(own, *rest):
     span = own.shape[0]
     return pl.pallas_call(
         segment_kernel,
-        in_specs=[vmem()] * 7,
+        in_specs=[vmem()] * 9,
         out_specs=[vmem()] * 3,
-        out_shape=[jax.ShapeDtypeStruct((2 * HD, span), BF16)]
+        out_shape=[jax.ShapeDtypeStruct((2 * HD + NOTE, span), BF16)]
         + [jax.ShapeDtypeStruct((128, 2 * HD), BF16)] * 2,
         compiler_params=pltpu.CompilerParams(vmem_limit_bytes=24 << 20),
         cost_estimate=pl.CostEstimate(
             flops=400_000_000, bytes_accessed=2 << 20, transcendentals=0
         ),
-    )(own, other, near, far, sign, rows, owners)
+    )(own, *rest)
 
 
 def attend_kernel(
@@ -299,17 +315,10 @@
         values = jnp.concatenate([mine[HALF:, columns], theirs[HALF:, columns]], 0)
         return keys, values
 
-    squares = []
-    for pair in prefix:
-        for ref in pair:
-            half = ref[:HALF, :].astype(F32)
-            squares.append(jnp.sum(half * half, 0, keepdims=True))
-    longest = jnp.maximum(jnp.max(squares[0] + squares[1]), jnp.max(squares[2] + squares[3]))
-    for ref in (seg, sib_seg):
-        part = ref[:HD, :].astype(F32)
-        longest = jnp.maximum(longest, jnp.max(jnp.sum(part * part, 0, keepdims=True)))
-    query_f = q[...].astype(F32)
-    widest = jnp.max(jnp.sum(query_f * query_f, 1, keepdims=True))
+    longest = jnp.maximum(
+        jnp.max(seg[2 * HD:, :HD].astype(F32)), jnp.max(sib_seg[2 * HD:, :HD].astype(F32))
+    )
+    widest = largest(q[...].astype(F32), 1)
     calm = longest * widest < SAFE_BOUND * SAFE_BOUND
 
     if step == 0:
@@ -349,11 +358,11 @@
             lax.fori_loop(0, blocks // 2, some_tiles, 0)
         for ref, flag in zip((seg, sib_seg), whole_flags):
             if flag is None:
-                tile(ref[:HD, :], ref[HD:, :], masked=True)
+                tile(ref[:HD, :], ref[HD:2 * HD, :], masked=True)
             else:
                 @pl.when(flag)
                 def _(ref=ref):
-                    tile(ref[:HD, :], ref[HD:, :])
+                    tile(ref[:HD, :], ref[HD:2 * HD, :])
         top[...] = jnp.zeros_like(top)
 
     @pl.when(jnp.logical_not(calm))
@@ -376,7 +385,7 @@
             for number, ref in enumerate((seg, sib_seg)):
                 @pl.when(b == 2 * blocks + number)
                 def _(ref=ref):
-                    held[...] = ref[...]
+                    held[...] = ref[:2 * HD, :]
 
             last = b == 2 * blocks
             flag = jnp.where(last, seg_flag, jnp.where(b > 2 * blocks, sib_flag, 1))
@@ -621,7 +630,7 @@
     )
     sib_other = to_sibling(other)
     seg, stay, go = segment(
-        kv, kv_other, near, far, sign, keep_rows[0], owners.reshape(owners.shape[1:3])
+        kv, kv_other, own, other, near, far, sign, keep_rows[0], owners.reshape(owners.shape[1:3])
     )
     came = to_sibling(go)
     sib_seg = to_sibling(seg)

time: 152 us -> 152 us (level)
  no operation moved by 1% of the time
where the time goes in v2:
time: 152 us
  Pallas kernels  104 us (68%)
  starting transfers between devices  26.9 us (18%)
  waiting for transfers between devices  18.5 us (12%)
    pallas_call x4, Pallas kernels, attend(): pl.pallas_call(functools.partial(attend_kernel, step), in_specs=[vmem()]...  92.1 us
    ppermute x21, starting transfers between devices, send(): return lax.ppermute(value, AXES, pairs_of(move))  26.9 us
    ppermute x21, waiting for transfers between devices, send(): return lax.ppermute(value, AXES, pairs_of(move))  18.5 us
    pallas_call x1, Pallas kernels, project(): pl.pallas_call(project_kernel, in_specs=[remain, vmem()] + [remain] * 4 +...  6.81 us
  transfers between devices with their start and end apart: 21, of which 6 were waited for; matrix products, arithmetic and copies ran while one was open for 0% of the time, Pallas kernels for 67%

profile of v2, /device:TPU:1, one launch (start us, length us, event | category | flops | bytes accessed | tf_op | source)
XLA Modules:
  0.0 151.9 jit_solution(11453104178416432842)
XLA Ops:
  0.6 1.1 pad_maximum_fusion.prefix.own
  1.7 2.2 %collective-permute-start.1 = (bf16[128,2048]{1,0:T(8,128)(2,1)S(1)}, bf16[128,2048]{1,0:T(8,128)(2,1)S(1)}, u32[]{:S(2)}, u32[]{:S(2)}) collective-permute-start(bf16[128,2048]{1,0:T(8,128)(2,1)S(1)} %pad_maximum_fusion.prefix.own), channel_id=1, source_target_pairs={{0,1},{1,0},{2,3},{3,2},{4,5},{5,4},{6,7},{7,6},{8,9},{9,8},{10,11... | collective-permute-start | bytes 1572872 | tf_op jit(solution)/shard_map/ppermute | solution.py:49
  3.9 0.0 copy-start.4
  3.9 6.8 %shard_map.140 = (bf16[1024,128]{1,0:T(8,128)(2,1)}, bf16[512,128]{1,0:T(8,128)(2,1)}, bf16[256,1024]{1,0:T(8,128)(2,1)}, bf16[256,1024]{1,0:T(8,128)(2,1)}, bf1...) custom-call(bf16[512,4096]{1,0:T(8,128)(2,1)} %tokens.1, bf16[32,128]{1,0:T(8,128)(2,1)} %bitcast.15, ...), custom_call_target="tpu_custom_call" | custom-call | flops 1610612736 | bytes 7340032 | tf_op jit(solution)/shard_map/pallas_call | solution.py:195
  10.8 1.3 collective-permute-start.2
  12.0 1.5 collective-permute-start.3
  13.5 0.0 collective-permute-start
  13.6 3.0 %collective-permute-start.11 = (bf16[256,1024]{1,0:T(8,128)(2,1)}, bf16[256,1024]{1,0:T(8,128)(2,1)S(1)}, u32[]{:S(2)}, u32[]{:S(2)}) collective-permute-start(bf16[256,1024]{1,0:T(8,128)(2,1)} %get-tuple-element.35), channel_id=1, source_target_pairs={{0,8},{1,9},{2,10},{3,11},{4,12},{5,13},{6,14},{7,15},{8,0},{9,1},... | collective-permute-start | bytes 1572872 | tf_op jit(solution)/shard_map/ppermute | solution.py:49
  16.6 1.3 collective-permute-done.other
  17.8 3.7 %collective-permute-start.4 = (bf16[128,2048]{1,0:T(8,128)(2,1)S(1)}, bf16[128,2048]{1,0:T(8,128)(2,1)S(1)}, u32[]{:S(2)}, u32[]{:S(2)}) collective-permute-start(bf16[128,2048]{1,0:T(8,128)(2,1)S(1)} %pad_maximum_fusion.prefix.own), channel_id=1, source_target_pairs={{0,16},{1,17},{2,18},{3,19},{4,20},{5,21},{6,22},{7,23},{8,24},{9,... | collective-permute-start | bytes 1572872 | tf_op jit(solution)/shard_map/ppermute | solution.py:49
  21.6 0.0 collective-permute-done.2.q
  21.6 0.0 collective-permute-done.3.q
  21.6 0.0 collective-permute-done.1.prefix_other.other
  21.6 0.1 collective-permute-start.5
  21.7 0.0 copy-done.7
  21.7 0.0 copy-done
  21.7 0.0 copy-done.1
  21.7 0.0 copy-done.3
  21.7 0.0 copy-done.4
  21.7 0.0 copy-start.2
  21.7 0.9 copy-done.2
  22.6 1.0 shard_map.141
  23.7 0.5 collective-permute-start.6
  24.2 0.1 collective-permute-start.7
  24.3 2.8 %collective-permute-done.11.w2 = bf16[256,1024]{1,0:T(8,128)(2,1)S(1)} collective-permute-done((bf16[256,1024]{1,0:T(8,128)(2,1)}, bf16[256,1024]{1,0:T(8,128)(2,1)S(1)}, u32[]{:S(2)}, u32[]{:S(2)}) %collective-permute-start.11) | collective-permute-done | bytes 524320 | tf_op jit(solution)/shard_map/ppermute | solution.py:49
  27.1 2.7 %collective-permute-start.9 = (bf16[1024,128]{1,0:T(8,128)(2,1)}, bf16[1024,128]{1,0:T(8,128)(2,1)S(1)}, u32[]{:S(2)}, u32[]{:S(2)}) collective-permute-start(bf16[1024,128]{1,0:T(8,128)(2,1)} %get-tuple-element.26.q), channel_id=1, source_target_pairs={{0,64},{1,65},{2,66},{3,67},{4,68},{5,69},{6,70},{7,71},{8,72},{9,... | collective-permute-start | bytes 786440 | tf_op jit(solution)/shard_map/ppermute | solution.py:49
  29.9 0.0 collective-permute-done.4.sib_own
  29.9 0.0 collective-permute-start.16
  29.9 0.0 collective-permute-done.7.came
  29.9 2.7 %collective-permute-start.17 = (bf16[256,1024]{1,0:T(8,128)(2,1)}, bf16[256,1024]{1,0:T(8,128)(2,1)S(1)}, u32[]{:S(2)}, u32[]{:S(2)}) collective-permute-start(bf16[256,1024]{1,0:T(8,128)(2,1)} %get-tuple-element.44), channel_id=1, source_target_pairs={{0,12},{1,13},{2,14},{3,15},{4,0},{5,1},{6,2},{7,3},{8,4},{9,5},{1... | collective-permute-start | bytes 1572872 | tf_op jit(solution)/shard_map/ppermute | solution.py:49
  32.6 0.0 collective-permute-done.6.sib_seg
  32.6 0.0 collective-permute-done.5.sib_other
  32.6 22.9 %shard_map.145 = bf16[1184,128]{1,0:T(8,128)(2,1)S(1)} custom-call(bf16[1024,128]{1,0:T(8,128)(2,1)S(1)} %collective-permute-done.3.q, bf16[128,2048]{1,0:T(8,128)(2,1)S(1)} %pad_maximum_fusion.prefix.own, bf16[128,2048]{1,0:T(8,128)(2,1)S(1)} %collective-permute-done.1.prefix_other.other, bf16[128,2048]{1,0:T(8,128)(2,1)S(1)} %collective-permute-done.4.sib_own, ...), custom_call_target="tpu_custom_call" | custom-call | flops 4294967296 | bytes 4194304 | tf_op jit(solution)/shard_map/pallas_call | solution.py:450
  55.5 0.4 collective-permute-start.12
  55.9 0.0 collective-permute-done.9.q
  55.9 22.8 %shard_map.144 = bf16[1184,128]{1,0:T(8,128)(2,1)S(1)} custom-call(bf16[1024,128]{1,0:T(8,128)(2,1)S(1)} %collective-permute-done.9.q, bf16[128,2048]{1,0:T(8,128)(2,1)S(1)} %pad_maximum_fusion.prefix.own, bf16[128,2048]{1,0:T(8,128)(2,1)S(1)} %collective-permute-done.1.prefix_other.other, bf16[128,2048]{1,0:T(8,128)(2,1)S(1)} %collective-permute-done.4.sib_own, ...), custom_call_target="tpu_custom_call" | custom-call | flops 4294967296 | bytes 4194304 | tf_op jit(solution)/shard_map/pallas_call | solution.py:450
  78.7 0.0 copy-start.6
  78.7 0.1 collective-permute-start.10
  78.8 22.8 %shard_map.143 = bf16[1184,128]{1,0:T(8,128)(2,1)S(1)} custom-call(bf16[1024,128]{1,0:T(8,128)(2,1)S(1)} %collective-permute-done.2.q, bf16[128,2048]{1,0:T(8,128)(2,1)S(1)} %pad_maximum_fusion.prefix.own, bf16[128,2048]{1,0:T(8,128)(2,1)S(1)} %collective-permute-done.1.prefix_other.other, bf16[128,2048]{1,0:T(8,128)(2,1)S(1)} %collective-permute-done.4.sib_own, ...), custom_call_target="tpu_custom_call" | custom-call | flops 4294967296 | bytes 4194304 | tf_op jit(solution)/shard_map/pallas_call | solution.py:450
  101.6 0.0 copy-start.5
  101.6 0.1 collective-permute-start.8
  101.7 0.0 copy-done.6
  101.7 23.6 %shard_map.142.p0 = bf16[1184,128]{1,0:T(8,128)(2,1)S(1)} custom-call(bf16[1024,128]{1,0:T(8,128)(2,1)S(1)} %copy-done.6, bf16[128,2048]{1,0:T(8,128)(2,1)S(1)} %pad_maximum_fusion.prefix.own, bf16[128,2048]{1,0:T(8,128)(2,1)S(1)} %collective-permute-done.1.prefix_other.other, bf16[128,2048]{1,0:T(8,128)(2,1)S(1)} %collective-permute-done.4.sib_own, ...), custom_call_target="tpu_custom_call" | custom-call | flops 4294967296 | bytes 4194304 | tf_op jit(solution)/shard_map/pallas_call | solution.py:450
  125.3 0.0 collective-permute-done.12.p3
  125.3 0.0 collective-permute-done.10.p2
  125.3 0.0 collective-permute-done.8.p1
  125.3 1.3 shard_map.146
  126.6 0.1 collective-permute-start.13
  126.7 1.2 collective-permute-start.14
  127.9 1.5 collective-permute-start.15
  129.4 0.0 collective-permute-done.16.w1
  129.4 0.0 collective-permute-done.17.w3
  129.4 7.3 %collective-permute-done.13.c1 = bf16[576,256]{1,0:T(8,128)(2,1)S(1)} collective-permute-done((bf16[576,256]{1,0:T(8,128)(2,1)S(1)}, bf16[576,256]{1,0:T(8,128)(2,1)S(1)}, u32[]{:S(2)}, u32[]{:S(2)}) %collective-permute-start.13) | collective-permute-done | bytes 294944 | tf_op jit(solution)/shard_map/ppermute | solution.py:49
  136.7 0.0 collective-permute-done.14.c2
  136.7 0.6 collective-permute-done.15.c3
  137.3 0.0 copy-done.5
  137.3 1.3 shard_map.147
  138.6 1.7 %collective-permute-start.18 = (bf16[576,256]{1,0:T(8,128)(2,1)S(1)}, bf16[576,256]{1,0:T(8,128)(2,1)S(1)}, u32[]{:S(2)}, u32[]{:S(2)}) collective-permute-start(bf16[576,256]{1,0:T(8,128)(2,1)S(1)} %get-tuple-element.47), channel_id=1, source_target_pairs={{0,1},{1,2},{2,3},{3,0},{4,5},{5,6},{6,7},{7,4},{8,9},{9,10},{10,1... | collective-permute-start | bytes 884744 | tf_op jit(solution)/shard_map/ppermute | solution.py:49
  140.3 3.3 %collective-permute-start.19 = (bf16[576,256]{1,0:T(8,128)(2,1)S(1)}, bf16[576,256]{1,0:T(8,128)(2,1)S(1)}, u32[]{:S(2)}, u32[]{:S(2)}) collective-permute-start(bf16[576,256]{1,0:T(8,128)(2,1)S(1)} %get-tuple-element.48), channel_id=1, source_target_pairs={{0,2},{1,3},{2,0},{3,1},{4,6},{5,7},{6,4},{7,5},{8,10},{9,11},{10,... | collective-permute-start | bytes 884744 | tf_op jit(solution)/shard_map/ppermute | solution.py:49
  143.6 0.7 collective-permute-start.20
  144.3 2.5 %collective-permute-done.18.a1 = bf16[576,256]{1,0:T(8,128)(2,1)S(1)} collective-permute-done((bf16[576,256]{1,0:T(8,128)(2,1)S(1)}, bf16[576,256]{1,0:T(8,128)(2,1)S(1)}, u32[]{:S(2)}, u32[]{:S(2)}) %collective-permute-start.18) | collective-permute-done | bytes 294944 | tf_op jit(solution)/shard_map/ppermute | solution.py:49
  146.8 4.0 %collective-permute-done.19.a2 = bf16[576,256]{1,0:T(8,128)(2,1)S(1)} collective-permute-done((bf16[576,256]{1,0:T(8,128)(2,1)S(1)}, bf16[576,256]{1,0:T(8,128)(2,1)S(1)}, u32[]{:S(2)}, u32[]{:S(2)}) %collective-permute-start.19) | collective-permute-done | bytes 294944 | tf_op jit(solution)/shard_map/ppermute | solution.py:49
  150.8 0.0 collective-permute-done.20.a3
  150.8 1.0 shard_map.148
  (5 shorter events, 0.0 us)
Async XLA Ops:
  1.7 19.9 %collective-permute-start.1 = (bf16[128,2048]{1,0:T(8,128)(2,1)S(1)}, bf16[128,2048]{1,0:T(8,128)(2,1)S(1)}, u32[]{:S(2)}, u32[]{:S(2)}) collective-permute-start(bf16[128,2048]{1,0:T(8,128)(2,1)S(1)} %pad_maximum_fusion.prefix.own), channel_id=1, source_target_pairs={{0,1},{1,0},{2,3},{3,2},{4,5},{5,4},{6,7},{7,6},{8,9},{9,8},{10,11... | collective-permute-start | bytes 1572872 | tf_op jit(solution)/shard_map/ppermute | solution.py:49
  3.9 17.7 %copy-start.7 = (s32[1,8,384,1]{2,3,1,0:T(1,128)S(1)}, s32[1,8,384,1]{2,3,1,0:T(1,128)}, u32[]{:S(2)}) copy-start(s32[1,8,384,1]{2,3,1,0:T(1,128)} %param.22) | copy-start | bytes 36868
  3.9 17.8 %copy-start = (f32[2,512,128]{2,1,0:T(8,128)S(1)}, f32[2,512,128]{2,1,0:T(8,128)}, u32[]{:S(2)}) copy-start(f32[2,512,128]{2,1,0:T(8,128)} %constant.6.clone.near) | copy-start | bytes 1572868
  3.9 17.8 %copy-start.1 = (bf16[2,128,128]{2,1,0:T(8,128)(2,1)S(1)}, bf16[2,128,128]{2,1,0:T(8,128)(2,1)}, u32[]{:S(2)}) copy-start(bf16[2,128,128]{2,1,0:T(8,128)(2,1)} %constant.8.clone.sign) | copy-start | bytes 196612
  3.9 17.8 %copy-start.3 = (f32[2,8,128]{2,1,0:T(8,128)S(1)}, f32[2,8,128]{2,1,0:T(8,128)}, u32[]{:S(2)}) copy-start(f32[2,8,128]{2,1,0:T(8,128)} %constant.7.clone.far) | copy-start | bytes 24580
  3.9 17.8 %copy-start.4 = (s32[1,8,384]{2,1,0:T(8,128)S(1)}, s32[1,8,384]{2,1,0:T(8,128)}, u32[]{:S(2)}) copy-start(s32[1,8,384]{2,1,0:T(8,128)} %param.21) | copy-start | bytes 36868
  10.8 10.8 %collective-permute-start.2 = (bf16[1024,128]{1,0:T(8,128)(2,1)}, bf16[1024,128]{1,0:T(8,128)(2,1)S(1)}, u32[]{:S(2)}, u32[]{:S(2)}) collective-permute-start(bf16[1024,128]{1,0:T(8,128)(2,1)} %get-tuple-element.26.q), channel_id=1, source_target_pairs={{0,32},{1,33},{2,34},{3,35},{4,36},{5,37},{6,38},{7,39},{8,40},{9,... | collective-permute-start | bytes 786440 | tf_op jit(solution)/shard_map/ppermute | solution.py:49
  12.0 9.5 %collective-permute-start.3 = (bf16[1024,128]{1,0:T(8,128)(2,1)}, bf16[1024,128]{1,0:T(8,128)(2,1)S(1)}, u32[]{:S(2)}, u32[]{:S(2)}) collective-permute-start(bf16[1024,128]{1,0:T(8,128)(2,1)} %get-tuple-element.26.q), channel_id=1, source_target_pairs={{0,96},{1,97},{2,98},{3,99},{4,100},{5,101},{6,102},{7,103},{8,104... | collective-permute-start | bytes 786440 | tf_op jit(solution)/shard_map/ppermute | solution.py:49
  13.5 4.3 %collective-permute-start = (bf16[512,128]{1,0:T(8,128)(2,1)}, bf16[512,128]{1,0:T(8,128)(2,1)S(1)}, u32[]{:S(2)}, u32[]{:S(2)}) collective-permute-start(bf16[512,128]{1,0:T(8,128)(2,1)} %get-tuple-element.27.own), channel_id=1, source_target_pairs={{0,1},{1,0},{2,3},{3,2},{4,5},{5,4},{6,7},{7,6},{8,9},{9,8},{10,11... | collective-permute-start | bytes 393224 | tf_op jit(solution)/shard_map/ppermute | solution.py:49
  13.6 13.6 %collective-permute-start.11 = (bf16[256,1024]{1,0:T(8,128)(2,1)}, bf16[256,1024]{1,0:T(8,128)(2,1)S(1)}, u32[]{:S(2)}, u32[]{:S(2)}) collective-permute-start(bf16[256,1024]{1,0:T(8,128)(2,1)} %get-tuple-element.35), channel_id=1, source_target_pairs={{0,8},{1,9},{2,10},{3,11},{4,12},{5,13},{6,14},{7,15},{8,0},{9,1},... | collective-permute-start | bytes 1572872 | tf_op jit(solution)/shard_map/ppermute | solution.py:49
  17.8 12.1 %collective-permute-start.4 = (bf16[128,2048]{1,0:T(8,128)(2,1)S(1)}, bf16[128,2048]{1,0:T(8,128)(2,1)S(1)}, u32[]{:S(2)}, u32[]{:S(2)}) collective-permute-start(bf16[128,2048]{1,0:T(8,128)(2,1)S(1)} %pad_maximum_fusion.prefix.own), channel_id=1, source_target_pairs={{0,16},{1,17},{2,18},{3,19},{4,20},{5,21},{6,22},{7,23},{8,24},{9,... | collective-permute-start | bytes 1572872 | tf_op jit(solution)/shard_map/ppermute | solution.py:49
  21.6 11.0 %collective-permute-start.5 = (bf16[128,2048]{1,0:T(8,128)(2,1)S(1)}, bf16[128,2048]{1,0:T(8,128)(2,1)S(1)}, u32[]{:S(2)}, u32[]{:S(2)}) collective-permute-start(bf16[128,2048]{1,0:T(8,128)(2,1)S(1)} %collective-permute-done.1.prefix_other.other), channel_id=1, source_target_pairs={{0,16},{1,17},{2,18},{3,19},{4,20},{5,21},{6,22},{7,23},{8,24},{9,... | collective-permute-start | bytes 1572872 | tf_op jit(solution)/shard_map/ppermute | solution.py:49
  21.7 0.9 copy-start.2
  23.7 8.9 %collective-permute-start.6 = (bf16[272,512]{1,0:T(8,128)(2,1)S(1)}, bf16[272,512]{1,0:T(8,128)(2,1)S(1)}, u32[]{:S(2)}, u32[]{:S(2)}) collective-permute-start(bf16[272,512]{1,0:T(8,128)(2,1)S(1)} %get-tuple-element.30.seg), channel_id=1, source_target_pairs={{0,16},{1,17},{2,18},{3,19},{4,20},{5,21},{6,22},{7,23},{8,24},{9,... | collective-permute-start | bytes 835592 | tf_op jit(solution)/shard_map/ppermute | solution.py:49
  24.2 5.7 %collective-permute-start.7 = (bf16[128,256]{1,0:T(8,128)(2,1)S(1)}, bf16[128,256]{1,0:T(8,128)(2,1)S(1)}, u32[]{:S(2)}, u32[]{:S(2)}) collective-permute-start(bf16[128,256]{1,0:T(8,128)(2,1)S(1)} %get-tuple-element.32), channel_id=1, source_target_pairs={{0,16},{1,17},{2,18},{3,19},{4,20},{5,21},{6,22},{7,23},{8,24},{9,... | collective-permute-start | bytes 196616 | tf_op jit(solution)/shard_map/ppermute | solution.py:49
  27.1 28.8 %collective-permute-start.9 = (bf16[1024,128]{1,0:T(8,128)(2,1)}, bf16[1024,128]{1,0:T(8,128)(2,1)S(1)}, u32[]{:S(2)}, u32[]{:S(2)}) collective-permute-start(bf16[1024,128]{1,0:T(8,128)(2,1)} %get-tuple-element.26.q), channel_id=1, source_target_pairs={{0,64},{1,65},{2,66},{3,67},{4,68},{5,69},{6,70},{7,71},{8,72},{9,... | collective-permute-start | bytes 786440 | tf_op jit(solution)/shard_map/ppermute | solution.py:49
  29.9 99.5 %collective-permute-start.16 = (bf16[256,1024]{1,0:T(8,128)(2,1)}, bf16[256,1024]{1,0:T(8,128)(2,1)S(1)}, u32[]{:S(2)}, u32[]{:S(2)}) collective-permute-start(bf16[256,1024]{1,0:T(8,128)(2,1)} %get-tuple-element.42), channel_id=1, source_target_pairs={{0,4},{1,5},{2,6},{3,7},{4,8},{5,9},{6,10},{7,11},{8,12},{9,13},{1... | collective-permute-start | bytes 1572872 | tf_op jit(solution)/shard_map/ppermute | solution.py:49
  29.9 99.5 %collective-permute-start.17 = (bf16[256,1024]{1,0:T(8,128)(2,1)}, bf16[256,1024]{1,0:T(8,128)(2,1)S(1)}, u32[]{:S(2)}, u32[]{:S(2)}) collective-permute-start(bf16[256,1024]{1,0:T(8,128)(2,1)} %get-tuple-element.44), channel_id=1, source_target_pairs={{0,12},{1,13},{2,14},{3,15},{4,0},{5,1},{6,2},{7,3},{8,4},{9,5},{1... | collective-permute-start | bytes 1572872 | tf_op jit(solution)/shard_map/ppermute | solution.py:49
  55.5 69.8 %collective-permute-start.12 = (bf16[1184,128]{1,0:T(8,128)(2,1)S(1)}, bf16[1184,128]{1,0:T(8,128)(2,1)S(1)}, u32[]{:S(2)}, u32[]{:S(2)}) collective-permute-start(bf16[1184,128]{1,0:T(8,128)(2,1)S(1)} %shard_map.145), channel_id=1, source_target_pairs={{0,32},{1,33},{2,34},{3,35},{4,36},{5,37},{6,38},{7,39},{8,40},{9,... | collective-permute-start | bytes 909320 | tf_op jit(solution)/shard_map/ppermute | solution.py:49
  78.7 23.0 %copy-start.6 = (bf16[1024,128]{1,0:T(8,128)(2,1)S(1)}, bf16[1024,128]{1,0:T(8,128)(2,1)}, u32[]{:S(2)}) copy-start(bf16[1024,128]{1,0:T(8,128)(2,1)} %get-tuple-element.26.q) | copy-start | bytes 786436
  78.7 46.6 %collective-permute-start.10 = (bf16[1184,128]{1,0:T(8,128)(2,1)S(1)}, bf16[1184,128]{1,0:T(8,128)(2,1)S(1)}, u32[]{:S(2)}, u32[]{:S(2)}) collective-permute-start(bf16[1184,128]{1,0:T(8,128)(2,1)S(1)} %shard_map.144), channel_id=1, source_target_pairs={{0,64},{1,65},{2,66},{3,67},{4,68},{5,69},{6,70},{7,71},{8,72},{9,... | collective-permute-start | bytes 909320 | tf_op jit(solution)/shard_map/ppermute | solution.py:49
  101.6 35.7 %copy-start.5 = (bf16[256,1024]{1,0:T(8,128)(2,1)S(1)}, bf16[256,1024]{1,0:T(8,128)(2,1)}, u32[]{:S(2)}) copy-start(bf16[256,1024]{1,0:T(8,128)(2,1)} %get-tuple-element.41.w0) | copy-start | bytes 1572868
  101.6 23.7 %collective-permute-start.8 = (bf16[1184,128]{1,0:T(8,128)(2,1)S(1)}, bf16[1184,128]{1,0:T(8,128)(2,1)S(1)}, u32[]{:S(2)}, u32[]{:S(2)}) collective-permute-start(bf16[1184,128]{1,0:T(8,128)(2,1)S(1)} %shard_map.143), channel_id=1, source_target_pairs={{0,96},{1,97},{2,98},{3,99},{4,100},{5,101},{6,102},{7,103},{8,104... | collective-permute-start | bytes 909320 | tf_op jit(solution)/shard_map/ppermute | solution.py:49
  126.6 10.0 %collective-permute-start.13 = (bf16[576,256]{1,0:T(8,128)(2,1)S(1)}, bf16[576,256]{1,0:T(8,128)(2,1)S(1)}, u32[]{:S(2)}, u32[]{:S(2)}) collective-permute-start(bf16[576,256]{1,0:T(8,128)(2,1)S(1)} %get-tuple-element.38), channel_id=1, source_target_pairs={{0,4},{1,5},{2,6},{3,7},{4,8},{5,9},{6,10},{7,11},{8,12},{9,13},{1... | collective-permute-start | bytes 884744 | tf_op jit(solution)/shard_map/ppermute | solution.py:49
  126.7 9.9 %collective-permute-start.14 = (bf16[576,256]{1,0:T(8,128)(2,1)S(1)}, bf16[576,256]{1,0:T(8,128)(2,1)S(1)}, u32[]{:S(2)}, u32[]{:S(2)}) collective-permute-start(bf16[576,256]{1,0:T(8,128)(2,1)S(1)} %get-tuple-element.39), channel_id=1, source_target_pairs={{0,8},{1,9},{2,10},{3,11},{4,12},{5,13},{6,14},{7,15},{8,0},{9,1},... | collective-permute-start | bytes 884744 | tf_op jit(solution)/shard_map/ppermute | solution.py:49
  127.9 9.4 %collective-permute-start.15 = (bf16[576,256]{1,0:T(8,128)(2,1)S(1)}, bf16[576,256]{1,0:T(8,128)(2,1)S(1)}, u32[]{:S(2)}, u32[]{:S(2)}) collective-permute-start(bf16[576,256]{1,0:T(8,128)(2,1)S(1)} %get-tuple-element.40), channel_id=1, source_target_pairs={{0,12},{1,13},{2,14},{3,15},{4,0},{5,1},{6,2},{7,3},{8,4},{9,5},{1... | collective-permute-start | bytes 884744 | tf_op jit(solution)/shard_map/ppermute | solution.py:49
  138.6 8.2 %collective-permute-start.18 = (bf16[576,256]{1,0:T(8,128)(2,1)S(1)}, bf16[576,256]{1,0:T(8,128)(2,1)S(1)}, u32[]{:S(2)}, u32[]{:S(2)}) collective-permute-start(bf16[576,256]{1,0:T(8,128)(2,1)S(1)} %get-tuple-element.47), channel_id=1, source_target_pairs={{0,1},{1,2},{2,3},{3,0},{4,5},{5,6},{6,7},{7,4},{8,9},{9,10},{10,1... | collective-permute-start | bytes 884744 | tf_op jit(solution)/shard_map/ppermute | solution.py:49
  140.3 10.6 %collective-permute-start.19 = (bf16[576,256]{1,0:T(8,128)(2,1)S(1)}, bf16[576,256]{1,0:T(8,128)(2,1)S(1)}, u32[]{:S(2)}, u32[]{:S(2)}) collective-permute-start(bf16[576,256]{1,0:T(8,128)(2,1)S(1)} %get-tuple-element.48), channel_id=1, source_target_pairs={{0,2},{1,3},{2,0},{3,1},{4,6},{5,7},{6,4},{7,5},{8,10},{9,11},{10,... | collective-permute-start | bytes 884744 | tf_op jit(solution)/shard_map/ppermute | solution.py:49
  143.6 7.3 %collective-permute-start.20 = (bf16[576,256]{1,0:T(8,128)(2,1)S(1)}, bf16[576,256]{1,0:T(8,128)(2,1)S(1)}, u32[]{:S(2)}, u32[]{:S(2)}) collective-permute-start(bf16[576,256]{1,0:T(8,128)(2,1)S(1)} %get-tuple-element.49), channel_id=1, source_target_pairs={{0,3},{1,0},{2,1},{3,2},{4,7},{5,4},{6,5},{7,6},{8,11},{9,8},{10,9... | collective-permute-start | bytes 884744 | tf_op jit(solution)/shard_map/ppermute | solution.py:49

commit v3 on v2

--- a/solution.py
+++ b/solution.py
@@ -223,11 +223,39 @@
 
 
 def segment_kernel(
-    own, other, prefix, prefix_other, near, far, sign, rows, owners, seg_out, stay_out, go_out
+    own, other, prefix, prefix_other, near, far, sign, rows, owners, seg_out, stay_out,
+    held, sem,
 ):
     x, core, z, y, parity, number, group = position()
     odd = parity == 1
-    mine, theirs = own[...].astype(F32), other[...].astype(F32)
+    arrive = pltpu.make_async_copy(own, held, sem)
+    arrive.start()
+    span, keep = own.shape[0], rows.shape[1]
+    row = rows[pl.ds(group, 1), :]
+    owner = owners[pl.ds(group, 1), :]
+    place = lax.broadcasted_iota(jnp.int32, (256, 1), 0)
+    to_core = jnp.where(place >= 128, 1 - core, core)
+    step_first, step_second = (place >> 3) & 3, (place >> 1) & 3
+    to_x = (x + (place >> 5)) & 3
+    to_z = (z + jnp.where(to_core == 0, step_first, step_second)) & 3
+    to_y = (y + jnp.where(to_core == 0, step_second, step_first)) & 3
+    named = owner == device_at(to_x, to_core, to_z, to_y)
+    before = lax.broadcasted_iota(jnp.int32, (keep, keep), 0) < lax.broadcasted_iota(
+        jnp.int32, (keep, keep), 1
+    )
+    rank = jnp.dot(
+        jnp.where(named, 1.0, 0.0).astype(BF16),
+        jnp.where(before, 1.0, 0.0).astype(BF16),
+        preferred_element_type=F32,
+    )
+    slot = (2 * parity + (place & 1)).astype(F32)
+    picks = jnp.where(jnp.logical_and(named, rank == slot), 1.0, 0.0).astype(BF16)
+    places = jnp.where(
+        lax.broadcasted_iota(jnp.int32, (span, keep), 0) == row, 1.0, 0.0
+    ).astype(BF16)
+    chosen = lax.dot_general(picks, places, NT, preferred_element_type=F32).astype(BF16)
+    arrive.wait()
+    mine, theirs = held[...].astype(F32), other[...].astype(F32)
     first = jnp.where(odd, theirs, mine)
     second = jnp.where(odd, mine, theirs)
     lane = lax.broadcasted_iota(jnp.int32, (1, HD), 1)
@@ -243,7 +271,7 @@
     longest = largest(seg_out[:HD, :].astype(F32), 0)
     halves = [ref[:HALF, :].astype(F32) for ref in (prefix, prefix_other)]
     longest = jnp.maximum(longest, largest(jnp.concatenate(halves, 0), 0)) * 1.01
-    seg_out[2 * HD:, :] = jnp.full((NOTE, own.shape[0]), longest, F32).astype(BF16)
+    seg_out[2 * HD:2 * HD + NOTE, :] = jnp.full((NOTE, own.shape[0]), longest, F32).astype(BF16)
     plain = sign[0]
     pair = jnp.concatenate(
         [
@@ -252,33 +280,10 @@
         ],
         1,
     )
-    span, keep = own.shape[0], rows.shape[1]
-    row = rows[pl.ds(group, 1), :]
-    owner = owners[pl.ds(group, 1), :]
-    place = lax.broadcasted_iota(jnp.int32, (256, 1), 0)
-    to_core = jnp.where(place >= 128, 1 - core, core)
-    step_first, step_second = (place >> 3) & 3, (place >> 1) & 3
-    to_x = (x + (place >> 5)) & 3
-    to_z = (z + jnp.where(to_core == 0, step_first, step_second)) & 3
-    to_y = (y + jnp.where(to_core == 0, step_second, step_first)) & 3
-    named = owner == device_at(to_x, to_core, to_z, to_y)
-    before = lax.broadcasted_iota(jnp.int32, (keep, keep), 0) < lax.broadcasted_iota(
-        jnp.int32, (keep, keep), 1
-    )
-    rank = jnp.dot(
-        jnp.where(named, 1.0, 0.0).astype(BF16),
-        jnp.where(before, 1.0, 0.0).astype(BF16),
-        preferred_element_type=F32,
-    )
-    slot = (2 * parity + (place & 1)).astype(F32)
-    picks = jnp.where(jnp.logical_and(named, rank == slot), 1.0, 0.0).astype(BF16)
-    places = jnp.where(
-        lax.broadcasted_iota(jnp.int32, (span, keep), 0) == row, 1.0, 0.0
-    ).astype(BF16)
-    chosen = lax.dot_general(picks, places, NT, preferred_element_type=F32).astype(BF16)
     kept = jnp.dot(chosen, pair, preferred_element_type=F32).astype(BF16)
     stay_out[...] = kept[:128, :]
-    go_out[...] = kept[128:, :]
+    for i in range(2):
+        seg_out[2 * HD + NOTE:, i * 256:(i + 1) * 256] = kept[128 + 64 * i:192 + 64 * i, :]
 
 
 def vmem():
@@ -289,10 +294,13 @@
     span = own.shape[0]
     return pl.pallas_call(
         segment_kernel,
-        in_specs=[vmem()] * 9,
-        out_specs=[vmem()] * 3,
-        out_shape=[jax.ShapeDtypeStruct((2 * HD + NOTE, span), BF16)]
-        + [jax.ShapeDtypeStruct((128, 2 * HD), BF16)] * 2,
+        in_specs=[pl.BlockSpec(memory_space=pl.ANY)] + [vmem()] * 8,
+        out_specs=[vmem()] * 2,
+        out_shape=[
+            jax.ShapeDtypeStruct((2 * HD + NOTE + 64, span), BF16),
+            jax.ShapeDtypeStruct((128, 2 * HD), BF16),
+        ],
+        scratch_shapes=[pltpu.VMEM((span, HD), BF16), pltpu.SemaphoreType.DMA],
         compiler_params=pltpu.CompilerParams(vmem_limit_bytes=24 << 20),
         cost_estimate=pl.CostEstimate(
             flops=400_000_000, bytes_accessed=2 << 20, transcendentals=0
@@ -301,7 +309,7 @@
 
 
 def attend_kernel(
-    step, q, own, other, sib_own, sib_other, seg, sib_seg, stay, came, out, acc, total, top, held
+    step, q, own, other, sib_own, sib_other, seg, sib_seg, stay, out, acc, total, top, held
 ):
     x, core = position()[:2]
     rows = q.shape[0]
@@ -316,7 +324,8 @@
         return keys, values
 
     longest = jnp.maximum(
-        jnp.max(seg[2 * HD:, :HD].astype(F32)), jnp.max(sib_seg[2 * HD:, :HD].astype(F32))
+        jnp.max(seg[2 * HD:2 * HD + NOTE, :HD].astype(F32)),
+        jnp.max(sib_seg[2 * HD:2 * HD + NOTE, :HD].astype(F32)),
     )
     widest = largest(q[...].astype(F32), 1)
     calm = longest * widest < SAFE_BOUND * SAFE_BOUND
@@ -439,17 +448,19 @@
         [high, middle, low, jnp.zeros_like(high)], 0
     ).astype(BF16)
     back = (RING - step) % RING
-    for i, ref in enumerate((stay, came, stay, came)):
-        out[rows + 32 * (i + 1):rows + 32 * (i + 2), :] = ref[
-            32 * back:32 * (back + 1), i // 2 * HD:(i // 2 + 1) * HD
-        ]
+    begin, lanes = 2 * HD + NOTE + 32 * (back % 2), 2 * HD * (back // 2)
+    for i in range(2):
+        place, half = rows + 32 + 64 * i, slice(i * HD, (i + 1) * HD)
+        out[place:place + 32, :] = stay[32 * back:32 * (back + 1), half]
+        half = slice(lanes + i * HD, lanes + (i + 1) * HD)
+        out[place + 32:place + 64, :] = sib_seg[begin:begin + 32, half]
 
 
 def attend(step, q, *rest):
     rows = q.shape[0]
     return pl.pallas_call(
         functools.partial(attend_kernel, step),
-        in_specs=[vmem()] * 9,
+        in_specs=[vmem()] * 8,
         out_specs=vmem(),
         out_shape=jax.ShapeDtypeStruct((rows + EXTRA, HD), BF16),
         scratch_shapes=[pltpu.VMEM((rows, HD), F32)] * 3 + [pltpu.VMEM((2 * HD, TILE), BF16)],
@@ -528,20 +539,9 @@
     )(*parts, sign)
 
 
-def out_kernel(c0, c1, c2, c3, w0, w1, w2, w3, o0, o1, o2, o3, sum_out):
-    outs = (o0, o1, o2, o3)
+def out_kernel(places, c0, c1, c2, c3, w0, w1, w2, w3, *outs):
     contexts = (c0, c1, c2, c3)
-    span = sum_out.shape[0]
-    for k in (2, 1, 3, 0):
-        columns = slice(k * 256, (k + 1) * 256)
-        whole = None
-        for c, w in zip(contexts, (w0, w1, w2, w3)):
-            part = jnp.dot(c[:span, :], w[:, columns], preferred_element_type=F32)
-            whole = part if whole is None else whole + part
-        if k:
-            outs[k][:span, :] = whole.astype(BF16)
-        else:
-            sum_out[...] = whole
+    span = c0.shape[0] - 64
     kept = jnp.concatenate([c[span:, :] for c in contexts], 0)
     kept = shuffle(
         kept,
@@ -551,23 +551,34 @@
         | (r >> 6) << 1
         | (r & 1),
     )
-    for k, out in enumerate(outs):
+    for k, out in zip(places, outs):
+        columns = slice(k * 256, (k + 1) * 256)
+        whole = None
+        for c, w in zip(contexts, (w0, w1, w2, w3)):
+            part = jnp.dot(c[:span, :], w[:, columns], preferred_element_type=F32)
+            whole = part if whole is None else whole + part
         begin = span if k else 0
+        if k:
+            out[:span, :] = whole.astype(BF16)
+        else:
+            outs[-1][...] = whole
         out[begin:, :] = kept[64 * k:64 * (k + 1), :]
 
 
-def project_out(contexts, weights):
+def project_out(places, contexts, weights):
     total = contexts[0].shape[0]
     span = total - 64
+    shapes = [jax.ShapeDtypeStruct((total if k else 64, 256), BF16) for k in places]
+    if 0 in places:
+        shapes.append(jax.ShapeDtypeStruct((span, 256), F32))
     return pl.pallas_call(
-        out_kernel,
+        functools.partial(out_kernel, places),
         in_specs=[vmem()] * 8,
-        out_specs=[vmem()] * 5,
-        out_shape=[jax.ShapeDtypeStruct((total if k else 64, 256), BF16) for k in range(4)]
-        + [jax.ShapeDtypeStruct((span, 256), F32)],
+        out_specs=[vmem()] * len(shapes),
+        out_shape=shapes,
         compiler_params=pltpu.CompilerParams(vmem_limit_bytes=24 << 20),
         cost_estimate=pl.CostEstimate(
-            flops=2 * span * 1024 * 1024, bytes_accessed=5 << 20, transcendentals=0
+            flops=512 * span * 1024 * len(places), bytes_accessed=5 << 20, transcendentals=0
         ),
     )(*contexts, *weights)
 
@@ -629,23 +640,25 @@
         (kv_other, other, queries[1], queries[3])
     )
     sib_other = to_sibling(other)
-    seg, stay, go = segment(
+    seg, stay = segment(
         kv, kv_other, own, other, near, far, sign, keep_rows[0], owners.reshape(owners.shape[1:3])
     )
-    came = to_sibling(go)
     sib_seg = to_sibling(seg)
     queries[3], weights[2] = lax.optimization_barrier((queries[3], weights[2]))
     parts = [None] * RING
     for d in (3, 1, 2, 0):
         part = attend(
-            d, queries[d], own, other, sib_own, sib_other, seg, sib_seg, stay, came
+            d, queries[d], own, other, sib_own, sib_other, seg, sib_seg, stay
         )
         parts[d] = along_x(part, -d) if d else part
     contexts = merge(parts, sign)
     contexts = [contexts[0]] + [along_first(contexts[d], d) for d in (1, 2, 3)]
-    *shares, share = project_out(contexts, weights)
-    arrived = [along_second(shares[k], k) for k in (1, 2, 3)]
-    return tuple(finish(share, shares[0], arrived))
+    far_share, = project_out((2,), contexts, weights)
+    share_1, share_3, kept_own, share = project_out((1, 3, 0), contexts, weights)
+    arrived = [
+        along_second(value, k) for value, k in ((share_1, 1), (far_share, 2), (share_3, 3))
+    ]
+    return tuple(finish(share, kept_own, arrived))
 
 
 def solution(mesh):

time: 152 us -> 149 us (0.980)
  waiting for transfers between devices: 18.5 us -> 14 us
    ppermute x21 -> x20, waiting for transfers between devices: 18.5 us -> 14 us  [send(): return lax.ppermute(value, AXES, pairs_of(move))]
    ppermute x21 -> x20, starting transfers between devices: 26.9 us -> 27.8 us  [send(): return lax.ppermute(value, AXES, pairs_of(move))]
  transfers between devices with their start and end apart: 21 -> 20, of which waited for: 6 -> 6; matrix products, arithmetic and copies ran while one was open for 0% -> 0% of each run, Pallas kernels for 67% -> 69%
where the time goes in v3:
time: 149 us
  Pallas kernels  104 us (70%)
  starting transfers between devices  27.8 us (19%)
  waiting for transfers between devices  14 us (9%)
    pallas_call x4, Pallas kernels, attend(): pl.pallas_call(functools.partial(attend_kernel, step), in_specs=[vmem()]...  92.1 us
    ppermute x20, starting transfers between devices, send(): return lax.ppermute(value, AXES, pairs_of(move))  27.8 us
    ppermute x20, waiting for transfers between devices, send(): return lax.ppermute(value, AXES, pairs_of(move))  14 us
    pallas_call x1, Pallas kernels, project(): pl.pallas_call(project_kernel, in_specs=[remain, vmem()] + [remain] * 4 +...  6.81 us
  transfers between devices with their start and end apart: 20, of which 6 were waited for; matrix products, arithmetic and copies ran while one was open for 0% of the time, Pallas kernels for 69%

profile of v3, /device:TPU:1, one launch (start us, length us, event | category | flops | bytes accessed | tf_op | source)
XLA Modules:
  0.0 148.8 jit_solution(3430563843339935107)
XLA Ops:
  0.6 1.1 pad_maximum_fusion.prefix.own
  1.7 2.2 %collective-permute-start.1 = (bf16[128,2048]{1,0:T(8,128)(2,1)S(1)}, bf16[128,2048]{1,0:T(8,128)(2,1)S(1)}, u32[]{:S(2)}, u32[]{:S(2)}) collective-permute-start(bf16[128,2048]{1,0:T(8,128)(2,1)S(1)} %pad_maximum_fusion.prefix.own), channel_id=1, source_target_pairs={{0,1},{1,0},{2,3},{3,2},{4,5},{5,4},{6,7},{7,6},{8,9},{9,8},{10,11... | collective-permute-start | bytes 1572872 | tf_op jit(solution)/shard_map/ppermute | solution.py:49
  3.9 0.0 copy-start.7
  3.9 0.0 copy-start.5
  3.9 6.8 %shard_map.140 = (bf16[1024,128]{1,0:T(8,128)(2,1)}, bf16[512,128]{1,0:T(8,128)(2,1)}, bf16[256,1024]{1,0:T(8,128)(2,1)}, bf16[256,1024]{1,0:T(8,128)(2,1)}, bf1...) custom-call(bf16[512,4096]{1,0:T(8,128)(2,1)} %tokens.1, bf16[32,128]{1,0:T(8,128)(2,1)} %bitcast.15, ...), custom_call_target="tpu_custom_call" | custom-call | flops 1610612736 | bytes 7340032 | tf_op jit(solution)/shard_map/pallas_call | solution.py:195
  10.8 1.3 collective-permute-start.2
  12.0 1.5 collective-permute-start.3
  13.5 0.0 collective-permute-start
  13.6 3.0 %collective-permute-start.10 = (bf16[256,1024]{1,0:T(8,128)(2,1)}, bf16[256,1024]{1,0:T(8,128)(2,1)S(1)}, u32[]{:S(2)}, u32[]{:S(2)}) collective-permute-start(bf16[256,1024]{1,0:T(8,128)(2,1)} %get-tuple-element.32), channel_id=1, source_target_pairs={{0,8},{1,9},{2,10},{3,11},{4,12},{5,13},{6,14},{7,15},{8,0},{9,1},... | collective-permute-start | bytes 1572872 | tf_op jit(solution)/shard_map/ppermute | solution.py:49
  16.6 1.3 collective-permute-done.other
  17.8 3.7 %collective-permute-start.4 = (bf16[128,2048]{1,0:T(8,128)(2,1)S(1)}, bf16[128,2048]{1,0:T(8,128)(2,1)S(1)}, u32[]{:S(2)}, u32[]{:S(2)}) collective-permute-start(bf16[128,2048]{1,0:T(8,128)(2,1)S(1)} %pad_maximum_fusion.prefix.own), channel_id=1, source_target_pairs={{0,16},{1,17},{2,18},{3,19},{4,20},{5,21},{6,22},{7,23},{8,24},{9,... | collective-permute-start | bytes 1572872 | tf_op jit(solution)/shard_map/ppermute | solution.py:49
  21.6 0.0 collective-permute-done.2.q
  21.6 0.0 collective-permute-done.3.q
  21.6 0.0 collective-permute-done.1.prefix_other.other
  21.6 0.1 collective-permute-start.5
  21.7 0.0 copy-done.7
  21.7 0.0 copy-done.1
  21.7 0.0 copy-done.2
  21.7 0.0 copy-done.4
  21.7 0.0 copy-done.5
  21.7 0.0 copy-start.3
  21.7 0.9 copy-done.3
  22.6 1.4 shard_map.141
  24.1 0.5 collective-permute-start.6
  24.6 2.1 %collective-permute-start.8 = (bf16[1024,128]{1,0:T(8,128)(2,1)}, bf16[1024,128]{1,0:T(8,128)(2,1)S(1)}, u32[]{:S(2)}, u32[]{:S(2)}) collective-permute-start(bf16[1024,128]{1,0:T(8,128)(2,1)} %get-tuple-element.24.q), channel_id=1, source_target_pairs={{0,64},{1,65},{2,66},{3,67},{4,68},{5,69},{6,70},{7,71},{8,72},{9,... | collective-permute-start | bytes 786440 | tf_op jit(solution)/shard_map/ppermute | solution.py:49
  26.7 0.4 collective-permute-done.10.w2
  27.1 0.9 collective-permute-start.15
  28.0 0.0 collective-permute-done.4.sib_own
  28.0 1.8 %collective-permute-start.16 = (bf16[256,1024]{1,0:T(8,128)(2,1)}, bf16[256,1024]{1,0:T(8,128)(2,1)S(1)}, u32[]{:S(2)}, u32[]{:S(2)}) collective-permute-start(bf16[256,1024]{1,0:T(8,128)(2,1)} %get-tuple-element.41), channel_id=1, source_target_pairs={{0,12},{1,13},{2,14},{3,15},{4,0},{5,1},{6,2},{7,3},{8,4},{9,5},{1... | collective-permute-start | bytes 1572872 | tf_op jit(solution)/shard_map/ppermute | solution.py:49
  29.8 0.0 collective-permute-done.6.sib_seg
  29.8 0.0 collective-permute-done.5.sib_other
  29.8 22.9 %shard_map.145 = bf16[1184,128]{1,0:T(8,128)(2,1)S(1)} custom-call(bf16[1024,128]{1,0:T(8,128)(2,1)S(1)} %collective-permute-done.3.q, bf16[128,2048]{1,0:T(8,128)(2,1)S(1)} %pad_maximum_fusion.prefix.own, bf16[128,2048]{1,0:T(8,128)(2,1)S(1)} %collective-permute-done.1.prefix_other.other, bf16[128,2048]{1,0:T(8,128)(2,1)S(1)} %collective-permute-done.4.sib_own, ...), custom_call_target="tpu_custom_call" | custom-call | flops 4294967296 | bytes 4194304 | tf_op jit(solution)/shard_map/pallas_call | solution.py:461
  52.8 1.3 collective-permute-start.11
  54.1 0.0 collective-permute-done.8.q
  54.1 22.8 %shard_map.144 = bf16[1184,128]{1,0:T(8,128)(2,1)S(1)} custom-call(bf16[1024,128]{1,0:T(8,128)(2,1)S(1)} %collective-permute-done.8.q, bf16[128,2048]{1,0:T(8,128)(2,1)S(1)} %pad_maximum_fusion.prefix.own, bf16[128,2048]{1,0:T(8,128)(2,1)S(1)} %collective-permute-done.1.prefix_other.other, bf16[128,2048]{1,0:T(8,128)(2,1)S(1)} %collective-permute-done.4.sib_own, ...), custom_call_target="tpu_custom_call" | custom-call | flops 4294967296 | bytes 4194304 | tf_op jit(solution)/shard_map/pallas_call | solution.py:461
  76.8 0.0 copy-start.6
  76.8 0.1 collective-permute-start.9
  76.9 22.8 %shard_map.143 = bf16[1184,128]{1,0:T(8,128)(2,1)S(1)} custom-call(bf16[1024,128]{1,0:T(8,128)(2,1)S(1)} %collective-permute-done.2.q, bf16[128,2048]{1,0:T(8,128)(2,1)S(1)} %pad_maximum_fusion.prefix.own, bf16[128,2048]{1,0:T(8,128)(2,1)S(1)} %collective-permute-done.1.prefix_other.other, bf16[128,2048]{1,0:T(8,128)(2,1)S(1)} %collective-permute-done.4.sib_own, ...), custom_call_target="tpu_custom_call" | custom-call | flops 4294967296 | bytes 4194304 | tf_op jit(solution)/shard_map/pallas_call | solution.py:461
  99.7 0.0 copy-start
  99.7 0.1 collective-permute-start.7
  99.8 0.0 copy-done.6
  99.8 23.6 %shard_map.142.p0 = bf16[1184,128]{1,0:T(8,128)(2,1)S(1)} custom-call(bf16[1024,128]{1,0:T(8,128)(2,1)S(1)} %copy-done.6, bf16[128,2048]{1,0:T(8,128)(2,1)S(1)} %pad_maximum_fusion.prefix.own, bf16[128,2048]{1,0:T(8,128)(2,1)S(1)} %collective-permute-done.1.prefix_other.other, bf16[128,2048]{1,0:T(8,128)(2,1)S(1)} %collective-permute-done.4.sib_own, ...), custom_call_target="tpu_custom_call" | custom-call | flops 4294967296 | bytes 4194304 | tf_op jit(solution)/shard_map/pallas_call | solution.py:461
  123.4 0.0 collective-permute-done.11.p3
  123.4 0.0 collective-permute-done.9.p2
  123.5 0.0 collective-permute-done.7.p1
  123.5 1.3 shard_map.146
  124.8 0.1 collective-permute-start.12
  124.9 1.4 collective-permute-start.13
  126.2 1.3 collective-permute-start.14
  127.5 0.0 collective-permute-done.15.w1
  127.5 0.0 collective-permute-done.16.w3
  127.5 7.3 %collective-permute-done.12.c1 = bf16[576,256]{1,0:T(8,128)(2,1)S(1)} collective-permute-done((bf16[576,256]{1,0:T(8,128)(2,1)S(1)}, bf16[576,256]{1,0:T(8,128)(2,1)S(1)}, u32[]{:S(2)}, u32[]{:S(2)}) %collective-permute-start.12) | collective-permute-done | bytes 294944 | tf_op jit(solution)/shard_map/ppermute | solution.py:49
  134.8 0.0 collective-permute-done.13.c2
  134.8 0.6 collective-permute-done.14.c3
  135.4 0.0 copy-done
  135.4 0.5 shard_map.148
  135.9 3.7 %collective-permute-start.18 = (bf16[576,256]{1,0:T(8,128)(2,1)S(1)}, bf16[576,256]{1,0:T(8,128)(2,1)S(1)}, u32[]{:S(2)}, u32[]{:S(2)}) collective-permute-start(bf16[576,256]{1,0:T(8,128)(2,1)S(1)} %shard_map.148), channel_id=1, source_target_pairs={{0,2},{1,3},{2,0},{3,1},{4,6},{5,7},{6,4},{7,5},{8,10},{9,11},{10,... | collective-permute-start | bytes 884744 | tf_op jit(solution)/shard_map/ppermute | solution.py:49
  139.6 1.1 shard_map.147
  140.7 0.8 collective-permute-start.17
  141.5 1.9 %collective-permute-start.19 = (bf16[576,256]{1,0:T(8,128)(2,1)S(1)}, bf16[576,256]{1,0:T(8,128)(2,1)S(1)}, u32[]{:S(2)}, u32[]{:S(2)}) collective-permute-start(bf16[576,256]{1,0:T(8,128)(2,1)S(1)} %get-tuple-element.45), channel_id=1, source_target_pairs={{0,3},{1,0},{2,1},{3,2},{4,7},{5,4},{6,5},{7,6},{8,11},{9,8},{10,9... | collective-permute-start | bytes 884744 | tf_op jit(solution)/shard_map/ppermute | solution.py:49
  143.4 0.4 collective-permute-done.18.a2
  143.9 4.0 %collective-permute-done.17.a1 = bf16[576,256]{1,0:T(8,128)(2,1)S(1)} collective-permute-done((bf16[576,256]{1,0:T(8,128)(2,1)S(1)}, bf16[576,256]{1,0:T(8,128)(2,1)S(1)}, u32[]{:S(2)}, u32[]{:S(2)}) %collective-permute-start.17) | collective-permute-done | bytes 294944 | tf_op jit(solution)/shard_map/ppermute | solution.py:49
  147.8 0.0 collective-permute-done.19.a3
  147.8 1.0 shard_map.149
  (4 shorter events, 0.0 us)
Async XLA Ops:
  1.7 19.9 %collective-permute-start.1 = (bf16[128,2048]{1,0:T(8,128)(2,1)S(1)}, bf16[128,2048]{1,0:T(8,128)(2,1)S(1)}, u32[]{:S(2)}, u32[]{:S(2)}) collective-permute-start(bf16[128,2048]{1,0:T(8,128)(2,1)S(1)} %pad_maximum_fusion.prefix.own), channel_id=1, source_target_pairs={{0,1},{1,0},{2,3},{3,2},{4,5},{5,4},{6,7},{7,6},{8,9},{9,8},{10,11... | collective-permute-start | bytes 1572872 | tf_op jit(solution)/shard_map/ppermute | solution.py:49
  3.9 17.7 %copy-start.7 = (s32[1,8,384,1]{2,3,1,0:T(1,128)S(1)}, s32[1,8,384,1]{2,3,1,0:T(1,128)}, u32[]{:S(2)}) copy-start(s32[1,8,384,1]{2,3,1,0:T(1,128)} %param.22) | copy-start | bytes 36868
  3.9 17.8 %copy-start.1 = (f32[2,512,128]{2,1,0:T(8,128)S(1)}, f32[2,512,128]{2,1,0:T(8,128)}, u32[]{:S(2)}) copy-start(f32[2,512,128]{2,1,0:T(8,128)} %constant.6.clone.near) | copy-start | bytes 1572868
  3.9 17.8 %copy-start.2 = (bf16[2,128,128]{2,1,0:T(8,128)(2,1)S(1)}, bf16[2,128,128]{2,1,0:T(8,128)(2,1)}, u32[]{:S(2)}) copy-start(bf16[2,128,128]{2,1,0:T(8,128)(2,1)} %constant.8.clone.sign) | copy-start | bytes 196612
  3.9 17.8 %copy-start.4 = (f32[2,8,128]{2,1,0:T(8,128)S(1)}, f32[2,8,128]{2,1,0:T(8,128)}, u32[]{:S(2)}) copy-start(f32[2,8,128]{2,1,0:T(8,128)} %constant.7.clone.far) | copy-start | bytes 24580
  3.9 17.8 %copy-start.5 = (s32[1,8,384]{2,1,0:T(8,128)S(1)}, s32[1,8,384]{2,1,0:T(8,128)}, u32[]{:S(2)}) copy-start(s32[1,8,384]{2,1,0:T(8,128)} %param.21) | copy-start | bytes 36868
  10.8 10.8 %collective-permute-start.2 = (bf16[1024,128]{1,0:T(8,128)(2,1)}, bf16[1024,128]{1,0:T(8,128)(2,1)S(1)}, u32[]{:S(2)}, u32[]{:S(2)}) collective-permute-start(bf16[1024,128]{1,0:T(8,128)(2,1)} %get-tuple-element.24.q), channel_id=1, source_target_pairs={{0,32},{1,33},{2,34},{3,35},{4,36},{5,37},{6,38},{7,39},{8,40},{9,... | collective-permute-start | bytes 786440 | tf_op jit(solution)/shard_map/ppermute | solution.py:49
  12.0 9.5 %collective-permute-start.3 = (bf16[1024,128]{1,0:T(8,128)(2,1)}, bf16[1024,128]{1,0:T(8,128)(2,1)S(1)}, u32[]{:S(2)}, u32[]{:S(2)}) collective-permute-start(bf16[1024,128]{1,0:T(8,128)(2,1)} %get-tuple-element.24.q), channel_id=1, source_target_pairs={{0,96},{1,97},{2,98},{3,99},{4,100},{5,101},{6,102},{7,103},{8,104... | collective-permute-start | bytes 786440 | tf_op jit(solution)/shard_map/ppermute | solution.py:49
  13.5 4.3 %collective-permute-start = (bf16[512,128]{1,0:T(8,128)(2,1)}, bf16[512,128]{1,0:T(8,128)(2,1)S(1)}, u32[]{:S(2)}, u32[]{:S(2)}) collective-permute-start(bf16[512,128]{1,0:T(8,128)(2,1)} %get-tuple-element.25.own), channel_id=1, source_target_pairs={{0,1},{1,0},{2,3},{3,2},{4,5},{5,4},{6,7},{7,6},{8,9},{9,8},{10,11... | collective-permute-start | bytes 393224 | tf_op jit(solution)/shard_map/ppermute | solution.py:49
  13.6 13.6 %collective-permute-start.10 = (bf16[256,1024]{1,0:T(8,128)(2,1)}, bf16[256,1024]{1,0:T(8,128)(2,1)S(1)}, u32[]{:S(2)}, u32[]{:S(2)}) collective-permute-start(bf16[256,1024]{1,0:T(8,128)(2,1)} %get-tuple-element.32), channel_id=1, source_target_pairs={{0,8},{1,9},{2,10},{3,11},{4,12},{5,13},{6,14},{7,15},{8,0},{9,1},... | collective-permute-start | bytes 1572872 | tf_op jit(solution)/shard_map/ppermute | solution.py:49
  17.8 10.2 %collective-permute-start.4 = (bf16[128,2048]{1,0:T(8,128)(2,1)S(1)}, bf16[128,2048]{1,0:T(8,128)(2,1)S(1)}, u32[]{:S(2)}, u32[]{:S(2)}) collective-permute-start(bf16[128,2048]{1,0:T(8,128)(2,1)S(1)} %pad_maximum_fusion.prefix.own), channel_id=1, source_target_pairs={{0,16},{1,17},{2,18},{3,19},{4,20},{5,21},{6,22},{7,23},{8,24},{9,... | collective-permute-start | bytes 1572872 | tf_op jit(solution)/shard_map/ppermute | solution.py:49
  21.6 8.3 %collective-permute-start.5 = (bf16[128,2048]{1,0:T(8,128)(2,1)S(1)}, bf16[128,2048]{1,0:T(8,128)(2,1)S(1)}, u32[]{:S(2)}, u32[]{:S(2)}) collective-permute-start(bf16[128,2048]{1,0:T(8,128)(2,1)S(1)} %collective-permute-done.1.prefix_other.other), channel_id=1, source_target_pairs={{0,16},{1,17},{2,18},{3,19},{4,20},{5,21},{6,22},{7,23},{8,24},{9,... | collective-permute-start | bytes 1572872 | tf_op jit(solution)/shard_map/ppermute | solution.py:49
  21.7 0.9 copy-start.3
  24.1 5.8 %collective-permute-start.6 = (bf16[336,512]{1,0:T(8,128)(2,1)S(1)}, bf16[336,512]{1,0:T(8,128)(2,1)S(1)}, u32[]{:S(2)}, u32[]{:S(2)}) collective-permute-start(bf16[336,512]{1,0:T(8,128)(2,1)S(1)} %get-tuple-element.28.seg), channel_id=1, source_target_pairs={{0,16},{1,17},{2,18},{3,19},{4,20},{5,21},{6,22},{7,23},{8,24},{9,... | collective-permute-start | bytes 1032200 | tf_op jit(solution)/shard_map/ppermute | solution.py:49
  24.6 29.5 %collective-permute-start.8 = (bf16[1024,128]{1,0:T(8,128)(2,1)}, bf16[1024,128]{1,0:T(8,128)(2,1)S(1)}, u32[]{:S(2)}, u32[]{:S(2)}) collective-permute-start(bf16[1024,128]{1,0:T(8,128)(2,1)} %get-tuple-element.24.q), channel_id=1, source_target_pairs={{0,64},{1,65},{2,66},{3,67},{4,68},{5,69},{6,70},{7,71},{8,72},{9,... | collective-permute-start | bytes 786440 | tf_op jit(solution)/shard_map/ppermute | solution.py:49
  27.1 100.4 %collective-permute-start.15 = (bf16[256,1024]{1,0:T(8,128)(2,1)}, bf16[256,1024]{1,0:T(8,128)(2,1)S(1)}, u32[]{:S(2)}, u32[]{:S(2)}) collective-permute-start(bf16[256,1024]{1,0:T(8,128)(2,1)} %get-tuple-element.39), channel_id=1, source_target_pairs={{0,4},{1,5},{2,6},{3,7},{4,8},{5,9},{6,10},{7,11},{8,12},{9,13},{1... | collective-permute-start | bytes 1572872 | tf_op jit(solution)/shard_map/ppermute | solution.py:49
  28.0 99.5 %collective-permute-start.16 = (bf16[256,1024]{1,0:T(8,128)(2,1)}, bf16[256,1024]{1,0:T(8,128)(2,1)S(1)}, u32[]{:S(2)}, u32[]{:S(2)}) collective-permute-start(bf16[256,1024]{1,0:T(8,128)(2,1)} %get-tuple-element.41), channel_id=1, source_target_pairs={{0,12},{1,13},{2,14},{3,15},{4,0},{5,1},{6,2},{7,3},{8,4},{9,5},{1... | collective-permute-start | bytes 1572872 | tf_op jit(solution)/shard_map/ppermute | solution.py:49
  52.8 70.7 %collective-permute-start.11 = (bf16[1184,128]{1,0:T(8,128)(2,1)S(1)}, bf16[1184,128]{1,0:T(8,128)(2,1)S(1)}, u32[]{:S(2)}, u32[]{:S(2)}) collective-permute-start(bf16[1184,128]{1,0:T(8,128)(2,1)S(1)} %shard_map.145), channel_id=1, source_target_pairs={{0,32},{1,33},{2,34},{3,35},{4,36},{5,37},{6,38},{7,39},{8,40},{9,... | collective-permute-start | bytes 909320 | tf_op jit(solution)/shard_map/ppermute | solution.py:49
  76.8 23.0 %copy-start.6 = (bf16[1024,128]{1,0:T(8,128)(2,1)S(1)}, bf16[1024,128]{1,0:T(8,128)(2,1)}, u32[]{:S(2)}) copy-start(bf16[1024,128]{1,0:T(8,128)(2,1)} %get-tuple-element.24.q) | copy-start | bytes 786436
  76.8 46.6 %collective-permute-start.9 = (bf16[1184,128]{1,0:T(8,128)(2,1)S(1)}, bf16[1184,128]{1,0:T(8,128)(2,1)S(1)}, u32[]{:S(2)}, u32[]{:S(2)}) collective-permute-start(bf16[1184,128]{1,0:T(8,128)(2,1)S(1)} %shard_map.144), channel_id=1, source_target_pairs={{0,64},{1,65},{2,66},{3,67},{4,68},{5,69},{6,70},{7,71},{8,72},{9,... | collective-permute-start | bytes 909320 | tf_op jit(solution)/shard_map/ppermute | solution.py:49
  99.7 35.7 %copy-start = (bf16[256,1024]{1,0:T(8,128)(2,1)S(1)}, bf16[256,1024]{1,0:T(8,128)(2,1)}, u32[]{:S(2)}) copy-start(bf16[256,1024]{1,0:T(8,128)(2,1)} %get-tuple-element.38.w0) | copy-start | bytes 1572868
  99.7 23.7 %collective-permute-start.7 = (bf16[1184,128]{1,0:T(8,128)(2,1)S(1)}, bf16[1184,128]{1,0:T(8,128)(2,1)S(1)}, u32[]{:S(2)}, u32[]{:S(2)}) collective-permute-start(bf16[1184,128]{1,0:T(8,128)(2,1)S(1)} %shard_map.143), channel_id=1, source_target_pairs={{0,96},{1,97},{2,98},{3,99},{4,100},{5,101},{6,102},{7,103},{8,104... | collective-permute-start | bytes 909320 | tf_op jit(solution)/shard_map/ppermute | solution.py:49
  124.8 10.0 %collective-permute-start.12 = (bf16[576,256]{1,0:T(8,128)(2,1)S(1)}, bf16[576,256]{1,0:T(8,128)(2,1)S(1)}, u32[]{:S(2)}, u32[]{:S(2)}) collective-permute-start(bf16[576,256]{1,0:T(8,128)(2,1)S(1)} %get-tuple-element.35), channel_id=1, source_target_pairs={{0,4},{1,5},{2,6},{3,7},{4,8},{5,9},{6,10},{7,11},{8,12},{9,13},{1... | collective-permute-start | bytes 884744 | tf_op jit(solution)/shard_map/ppermute | solution.py:49
  124.9 9.9 %collective-permute-start.13 = (bf16[576,256]{1,0:T(8,128)(2,1)S(1)}, bf16[576,256]{1,0:T(8,128)(2,1)S(1)}, u32[]{:S(2)}, u32[]{:S(2)}) collective-permute-start(bf16[576,256]{1,0:T(8,128)(2,1)S(1)} %get-tuple-element.36), channel_id=1, source_target_pairs={{0,8},{1,9},{2,10},{3,11},{4,12},{5,13},{6,14},{7,15},{8,0},{9,1},... | collective-permute-start | bytes 884744 | tf_op jit(solution)/shard_map/ppermute | solution.py:49
  126.2 9.2 %collective-permute-start.14 = (bf16[576,256]{1,0:T(8,128)(2,1)S(1)}, bf16[576,256]{1,0:T(8,128)(2,1)S(1)}, u32[]{:S(2)}, u32[]{:S(2)}) collective-permute-start(bf16[576,256]{1,0:T(8,128)(2,1)S(1)} %get-tuple-element.37), channel_id=1, source_target_pairs={{0,12},{1,13},{2,14},{3,15},{4,0},{5,1},{6,2},{7,3},{8,4},{9,5},{1... | collective-permute-start | bytes 884744 | tf_op jit(solution)/shard_map/ppermute | solution.py:49
  135.9 7.9 %collective-permute-start.18 = (bf16[576,256]{1,0:T(8,128)(2,1)S(1)}, bf16[576,256]{1,0:T(8,128)(2,1)S(1)}, u32[]{:S(2)}, u32[]{:S(2)}) collective-permute-start(bf16[576,256]{1,0:T(8,128)(2,1)S(1)} %shard_map.148), channel_id=1, source_target_pairs={{0,2},{1,3},{2,0},{3,1},{4,6},{5,7},{6,4},{7,5},{8,10},{9,11},{10,... | collective-permute-start | bytes 884744 | tf_op jit(solution)/shard_map/ppermute | solution.py:49
  140.7 7.1 %collective-permute-start.17 = (bf16[576,256]{1,0:T(8,128)(2,1)S(1)}, bf16[576,256]{1,0:T(8,128)(2,1)S(1)}, u32[]{:S(2)}, u32[]{:S(2)}) collective-permute-start(bf16[576,256]{1,0:T(8,128)(2,1)S(1)} %get-tuple-element.44), channel_id=1, source_target_pairs={{0,1},{1,2},{2,3},{3,0},{4,5},{5,6},{6,7},{7,4},{8,9},{9,10},{10,1... | collective-permute-start | bytes 884744 | tf_op jit(solution)/shard_map/ppermute | solution.py:49
  141.5 6.3 %collective-permute-start.19 = (bf16[576,256]{1,0:T(8,128)(2,1)S(1)}, bf16[576,256]{1,0:T(8,128)(2,1)S(1)}, u32[]{:S(2)}, u32[]{:S(2)}) collective-permute-start(bf16[576,256]{1,0:T(8,128)(2,1)S(1)} %get-tuple-element.45), channel_id=1, source_target_pairs={{0,3},{1,0},{2,1},{3,2},{4,7},{5,4},{6,5},{7,6},{8,11},{9,8},{10,9... | collective-permute-start | bytes 884744 | tf_op jit(solution)/shard_map/ppermute | solution.py:49

commit v4 on v3

--- a/solution.py
+++ b/solution.py
@@ -23,6 +23,7 @@
 CUT_AT = 2
 WHOLE_AT = 1
 NOTE = 16
+SPANS = 8
 EXTRA = 32 + 128
 
 NT = (((1,), (1,)), ((), ()))
@@ -85,7 +86,7 @@
     for bit in range(7):
         parity += both >> bit & 1
     plain = (1 - 2 * (parity % 2)).astype(np.float32)
-    return np.stack([plain, np.roll(plain, HALF, axis=1)])
+    return np.concatenate([plain, np.roll(plain, HALF, axis=1)])
 
 
 def rope_tables(span, spans, prefix):
@@ -93,21 +94,27 @@
     freq = np.concatenate([freq, freq])
     near = np.arange(span)[:, None] * freq[None, :]
     far = (prefix + span * np.arange(spans))[:, None] * freq[None, :]
-    near = np.stack([np.cos(near), np.sin(near)]).astype(np.float32)
-    far = np.stack([np.cos(far), np.sin(far)]).astype(np.float32)
-    return near, far
-
-
-def rope_factors(near, far, number):
-    cos_far, sin_far = far[0, pl.ds(number, 1), :], far[1, pl.ds(number, 1), :]
-    cosine = near[0] * cos_far - near[1] * sin_far
-    sine = near[1] * cos_far + near[0] * sin_far
+    both = [np.cos(near), np.sin(near), np.cos(far), np.sin(far), signs()]
+    return np.concatenate(both).astype(np.float32)
+
+
+def turn_of(tables, parity, span):
+    begin = 2 * span + 2 * SPANS + HD * parity
+    return tables[pl.ds(begin, HD), :].astype(BF16)
+
+
+def rope_factors(tables, number, span):
+    cos_near, sin_near = tables[:span, :], tables[span:2 * span, :]
+    cos_far = tables[pl.ds(2 * span + number, 1), :]
+    sin_far = tables[pl.ds(2 * span + SPANS + number, 1), :]
+    cosine = cos_near * cos_far - sin_near * sin_far
+    sine = sin_near * cos_far + cos_near * sin_far
     lane = lax.broadcasted_iota(jnp.int32, (1, HD), 1)
     return cosine, jnp.where(lane < HALF, -sine, sine)
 
 
 def project_kernel(
-    tokens, gain, w_q, w_kt, w_vt, near, far, sign, w_out, q_out, kv_out, w0, w1, w2, w3,
+    tokens, gain, w_q, w_kt, w_vt, near, w_out, q_out, kv_out, w0, w1, w2, w3,
     held, held_q, held_kv, held_near, held_w, sum_q, sum_kv, sems, cut_sems,
 ):
     x, core, z, y, parity, number, group = position()
@@ -177,8 +184,8 @@
     scale = lax.rsqrt(jnp.sum(squares, -1, keepdims=True) / width + EPSILON)
     kv_out[...] = (sum_kv[...] * scale).astype(BF16)
     tables.wait()
-    cosine, sine = rope_factors(held_near, far, number)
-    turn = sign[parity]
+    cosine, sine = rope_factors(held_near, number, span)
+    turn = turn_of(held_near, parity, span)
     for h in range(2):
         head = sum_q[:, h * HD:(h + 1) * HD] * scale
         head = head * cosine + pltpu.roll(head, HALF, 1) * sine
@@ -189,12 +196,12 @@
         copy.wait()
 
 
-def project(tokens, gain, w_q, w_kt, w_vt, near, far, sign, w_out):
+def project(tokens, gain, w_q, w_kt, w_vt, near, w_out):
     span, width = tokens.shape
     remain = pl.BlockSpec(memory_space=pl.ANY)
     return pl.pallas_call(
         project_kernel,
-        in_specs=[remain, vmem()] + [remain] * 4 + [vmem(), vmem(), remain],
+        in_specs=[remain, vmem()] + [remain] * 5,
         out_specs=[vmem(), vmem()] + [remain] * 4,
         out_shape=[
             jax.ShapeDtypeStruct((2 * span, HD), BF16),
@@ -211,11 +218,11 @@
             pltpu.SemaphoreType.DMA((4 * CHUNKS + 2,)),
             pltpu.SemaphoreType.DMA((RING * RING,)),
         ],
-        compiler_params=pltpu.CompilerParams(vmem_limit_bytes=60 << 20),
+        compiler_params=pltpu.CompilerParams(vmem_limit_bytes=52 << 20),
         cost_estimate=pl.CostEstimate(
             flops=2 * span * width * 384, bytes_accessed=7 << 20, transcendentals=0
         ),
-    )(tokens, gain, w_q, w_kt, w_vt, near, far, sign, w_out)
+    )(tokens, gain, w_q, w_kt, w_vt, near, w_out)
 
 
 def largest(rows, axis):
@@ -223,7 +230,7 @@
 
 
 def segment_kernel(
-    own, other, prefix, prefix_other, near, far, sign, rows, owners, seg_out, stay_out,
+    own, other, prefix, prefix_other, tables, rows, owners, seg_out, stay_out,
     held, sem,
 ):
     x, core, z, y, parity, number, group = position()
@@ -261,9 +268,9 @@
     lane = lax.broadcasted_iota(jnp.int32, (1, HD), 1)
     key = jnp.where(lane < HALF, first, pltpu.roll(second, HALF, 1))
     value = jnp.where(lane < HALF, pltpu.roll(first, HALF, 1), second).astype(BF16)
-    cosine, sine = rope_factors(near, far, number)
+    cosine, sine = rope_factors(tables, number, own.shape[0])
     key = (key * cosine + pltpu.roll(key, HALF, 1) * sine).astype(BF16)
-    turn = sign[parity]
+    turn = turn_of(tables, parity, own.shape[0])
     unit = HD ** -0.5
     for i, part in enumerate((key, value)):
         turned = lax.dot_general(turn, part, TN, preferred_element_type=F32) * unit
@@ -272,7 +279,7 @@
     halves = [ref[:HALF, :].astype(F32) for ref in (prefix, prefix_other)]
     longest = jnp.maximum(longest, largest(jnp.concatenate(halves, 0), 0)) * 1.01
     seg_out[2 * HD:2 * HD + NOTE, :] = jnp.full((NOTE, own.shape[0]), longest, F32).astype(BF16)
-    plain = sign[0]
+    plain = turn_of(tables, 0, own.shape[0])
     pair = jnp.concatenate(
         [
             (jnp.dot(key, plain, preferred_element_type=F32) * unit).astype(BF16),
@@ -294,7 +301,7 @@
     span = own.shape[0]
     return pl.pallas_call(
         segment_kernel,
-        in_specs=[pl.BlockSpec(memory_space=pl.ANY)] + [vmem()] * 8,
+        in_specs=[pl.BlockSpec(memory_space=pl.ANY)] + [vmem()] * 6,
         out_specs=[vmem()] * 2,
         out_shape=[
             jax.ShapeDtypeStruct((2 * HD + NOTE + 64, span), BF16),
@@ -494,7 +501,7 @@
     eye = lax.broadcasted_iota(jnp.int32, (HD, HD), 0) == lax.broadcasted_iota(
         jnp.int32, (HD, HD), 1
     )
-    turn = sign[parity]
+    turn = sign[pl.ds(HD * parity, HD), :]
     per_head = count // 2
     for b in range(count):
         left, right = [], []
@@ -623,15 +630,14 @@
     seq_count = lax.axis_size("seq")
     span = tokens.shape[0]
     prefix_len = prefix_keys.shape[0] * seq_count
-    near, far = rope_tables(span, seq_count, prefix_len)
-    near, far = jnp.asarray(near), jnp.asarray(far)
+    tables = jnp.asarray(rope_tables(span, SPANS, prefix_len))
     sign = jnp.asarray(signs(), BF16)
 
     own = jnp.concatenate([prefix_keys.T, prefix_values.T], 0)
     other = to_head_pair(own)
     sib_own = to_sibling(own)
     q, kv, *pieces = project(
-        tokens, norm_gain.reshape(-1, HD), w_query, w_key.T, w_value.T, near, far, sign, w_out
+        tokens, norm_gain.reshape(-1, HD), w_query, w_key.T, w_value.T, tables, w_out
     )
     kv_other = to_head_pair(kv)
     queries = [q] + [along_x(q, d) for d in (1, 2, 3)]
@@ -641,7 +647,7 @@
     )
     sib_other = to_sibling(other)
     seg, stay = segment(
-        kv, kv_other, own, other, near, far, sign, keep_rows[0], owners.reshape(owners.shape[1:3])
+        kv, kv_other, own, other, tables, keep_rows[0], owners.reshape(owners.shape[1:3])
     )
     sib_seg = to_sibling(seg)
     queries[3], weights[2] = lax.optimization_barrier((queries[3], weights[2]))

time: 149 us -> 149 us (level)
  waiting for transfers between devices: 14 us -> 15.5 us
    ppermute x20, waiting for transfers between devices: 14 us -> 15.5 us  [send(): return lax.ppermute(value, AXES, pairs_of(move))]
  transfers between devices with their start and end apart: 20 -> 20, of which waited for: 6 -> 7; matrix products, arithmetic and copies ran while one was open for 0% -> 0% of each run, Pallas kernels for 69% -> 68%
where the time goes in v4:
time: 149 us
  Pallas kernels  103 us (69%)
  starting transfers between devices  27.6 us (19%)
  waiting for transfers between devices  15.5 us (10%)
    pallas_call x4, Pallas kernels, attend(): pl.pallas_call(functools.partial(attend_kernel, step), in_specs=[vmem()]...  92.1 us
    ppermute x20, starting transfers between devices, send(): return lax.ppermute(value, AXES, pairs_of(move))  27.6 us
    ppermute x20, waiting for transfers between devices, send(): return lax.ppermute(value, AXES, pairs_of(move))  15.5 us
    pallas_call x1, Pallas kernels, project(): pl.pallas_call(project_kernel, in_specs=[remain, vmem()] + [remain] * 5,...  5.45 us
  transfers between devices with their start and end apart: 20, of which 7 were waited for; matrix products, arithmetic and copies ran while one was open for 0% of the time, Pallas kernels for 68%

profile of v4, /device:TPU:1, one launch (start us, length us, event | category | flops | bytes accessed | tf_op | source)
XLA Modules:
  0.0 148.6 jit_solution(7643074506152325647)
XLA Ops:
  0.6 1.1 pad_maximum_fusion.prefix.own
  1.7 2.2 %collective-permute-start.1 = (bf16[128,2048]{1,0:T(8,128)(2,1)S(1)}, bf16[128,2048]{1,0:T(8,128)(2,1)S(1)}, u32[]{:S(2)}, u32[]{:S(2)}) collective-permute-start(bf16[128,2048]{1,0:T(8,128)(2,1)S(1)} %pad_maximum_fusion.prefix.own), channel_id=1, source_target_pairs={{0,1},{1,0},{2,3},{3,2},{4,5},{5,4},{6,7},{7,6},{8,9},{9,8},{10,11... | collective-permute-start | bytes 1572872 | tf_op jit(solution)/shard_map/ppermute | solution.py:50
  3.9 0.0 copy-start.2
  3.9 0.7 copy-done.2
  4.6 0.0 copy-start.4
  4.6 0.0 copy-start
  4.6 0.0 copy-start.1
  4.6 5.4 %shard_map.131 = (bf16[1024,128]{1,0:T(8,128)(2,1)S(1)}, bf16[512,128]{1,0:T(8,128)(2,1)S(1)}, bf16[256,1024]{1,0:T(8,128)(2,1)S(1)}, bf16[256,1024]{1,0:T(8,128...) custom-call(bf16[512,4096]{1,0:T(8,128)(2,1)} %tokens.1, bf16[32,128]{1,0:T(8,128)(2,1)S(1)} %bitcast.11, ...), custom_call_target="tpu_custom_call" | custom-call | flops 1610612736 | bytes 7340032 | tf_op jit(solution)/shard_map/pallas_call | solution.py:202
  10.1 1.3 collective-permute-start.2
  11.3 1.5 collective-permute-start.3
  12.8 0.1 collective-permute-start
  12.9 3.0 %collective-permute-start.10 = (bf16[256,1024]{1,0:T(8,128)(2,1)S(1)}, bf16[256,1024]{1,0:T(8,128)(2,1)S(1)}, u32[]{:S(2)}, u32[]{:S(2)}) collective-permute-start(bf16[256,1024]{1,0:T(8,128)(2,1)S(1)} %get-tuple-element.32), channel_id=1, source_target_pairs={{0,8},{1,9},{2,10},{3,11},{4,12},{5,13},{6,14},{7,15},{8,0},{9,1},... | collective-permute-start | bytes 1572872 | tf_op jit(solution)/shard_map/ppermute | solution.py:50
  15.9 2.1 %collective-permute-done.other = bf16[512,128]{1,0:T(8,128)(2,1)S(1)} collective-permute-done((bf16[512,128]{1,0:T(8,128)(2,1)S(1)}, bf16[512,128]{1,0:T(8,128)(2,1)S(1)}, u32[]{:S(2)}, u32[]{:S(2)}) %collective-permute-start) | collective-permute-done | bytes 131104 | tf_op jit(solution)/shard_map/ppermute | solution.py:50
  18.0 2.7 %collective-permute-start.4 = (bf16[128,2048]{1,0:T(8,128)(2,1)S(1)}, bf16[128,2048]{1,0:T(8,128)(2,1)S(1)}, u32[]{:S(2)}, u32[]{:S(2)}) collective-permute-start(bf16[128,2048]{1,0:T(8,128)(2,1)S(1)} %pad_maximum_fusion.prefix.own), channel_id=1, source_target_pairs={{0,16},{1,17},{2,18},{3,19},{4,20},{5,21},{6,22},{7,23},{8,24},{9,... | collective-permute-start | bytes 1572872 | tf_op jit(solution)/shard_map/ppermute | solution.py:50
  20.8 0.0 collective-permute-done.2.q
  20.8 0.0 collective-permute-done.3.q
  20.8 0.0 collective-permute-done.1.prefix_other.other
  20.8 0.1 collective-permute-start.5
  20.9 0.0 copy-done.4
  20.9 0.0 copy-done
  20.9 0.0 copy-done.1
  20.9 1.5 shard_map.132
  22.4 0.5 collective-permute-start.6
  22.9 2.9 %collective-permute-start.8 = (bf16[1024,128]{1,0:T(8,128)(2,1)S(1)}, bf16[1024,128]{1,0:T(8,128)(2,1)S(1)}, u32[]{:S(2)}, u32[]{:S(2)}) collective-permute-start(bf16[1024,128]{1,0:T(8,128)(2,1)S(1)} %get-tuple-element.24.q), channel_id=1, source_target_pairs={{0,64},{1,65},{2,66},{3,67},{4,68},{5,69},{6,70},{7,71},{8,72},{9,... | collective-permute-start | bytes 786440 | tf_op jit(solution)/shard_map/ppermute | solution.py:50
  25.8 1.3 collective-permute-done.10.w2
  27.1 0.0 collective-permute-start.15
  27.1 0.0 collective-permute-done.4.sib_own
  27.1 2.7 %collective-permute-start.16 = (bf16[256,1024]{1,0:T(8,128)(2,1)}, bf16[256,1024]{1,0:T(8,128)(2,1)S(1)}, u32[]{:S(2)}, u32[]{:S(2)}) collective-permute-start(bf16[256,1024]{1,0:T(8,128)(2,1)} %get-tuple-element.41), channel_id=1, source_target_pairs={{0,12},{1,13},{2,14},{3,15},{4,0},{5,1},{6,2},{7,3},{8,4},{9,5},{1... | collective-permute-start | bytes 1572872 | tf_op jit(solution)/shard_map/ppermute | solution.py:50
  29.8 0.0 collective-permute-done.6.sib_seg
  29.8 0.0 collective-permute-done.5.sib_other
  29.8 23.0 %shard_map.136 = bf16[1184,128]{1,0:T(8,128)(2,1)S(1)} custom-call(bf16[1024,128]{1,0:T(8,128)(2,1)S(1)} %collective-permute-done.3.q, bf16[128,2048]{1,0:T(8,128)(2,1)S(1)} %pad_maximum_fusion.prefix.own, bf16[128,2048]{1,0:T(8,128)(2,1)S(1)} %collective-permute-done.1.prefix_other.other, bf16[128,2048]{1,0:T(8,128)(2,1)S(1)} %collective-permute-done.4.sib_own, ...), custom_call_target="tpu_custom_call" | custom-call | flops 4294967296 | bytes 4194304 | tf_op jit(solution)/shard_map/pallas_call | solution.py:468
  52.8 1.3 collective-permute-start.11
  54.1 0.0 collective-permute-done.8.q
  54.1 22.8 %shard_map.135 = bf16[1184,128]{1,0:T(8,128)(2,1)S(1)} custom-call(bf16[1024,128]{1,0:T(8,128)(2,1)S(1)} %collective-permute-done.8.q, bf16[128,2048]{1,0:T(8,128)(2,1)S(1)} %pad_maximum_fusion.prefix.own, bf16[128,2048]{1,0:T(8,128)(2,1)S(1)} %collective-permute-done.1.prefix_other.other, bf16[128,2048]{1,0:T(8,128)(2,1)S(1)} %collective-permute-done.4.sib_own, ...), custom_call_target="tpu_custom_call" | custom-call | flops 4294967296 | bytes 4194304 | tf_op jit(solution)/shard_map/pallas_call | solution.py:468
  76.8 0.1 collective-permute-start.9
  76.9 22.8 %shard_map.134 = bf16[1184,128]{1,0:T(8,128)(2,1)S(1)} custom-call(bf16[1024,128]{1,0:T(8,128)(2,1)S(1)} %collective-permute-done.2.q, bf16[128,2048]{1,0:T(8,128)(2,1)S(1)} %pad_maximum_fusion.prefix.own, bf16[128,2048]{1,0:T(8,128)(2,1)S(1)} %collective-permute-done.1.prefix_other.other, bf16[128,2048]{1,0:T(8,128)(2,1)S(1)} %collective-permute-done.4.sib_own, ...), custom_call_target="tpu_custom_call" | custom-call | flops 4294967296 | bytes 4194304 | tf_op jit(solution)/shard_map/pallas_call | solution.py:468
  99.7 0.0 copy-start.3
  99.7 0.1 collective-permute-start.7
  99.8 23.6 %shard_map.133.p0 = bf16[1184,128]{1,0:T(8,128)(2,1)S(1)} custom-call(bf16[1024,128]{1,0:T(8,128)(2,1)S(1)} %get-tuple-element.24.q, bf16[128,2048]{1,0:T(8,128)(2,1)S(1)} %pad_maximum_fusion.prefix.own, bf16[128,2048]{1,0:T(8,128)(2,1)S(1)} %collective-permute-done.1.prefix_other.other, bf16[128,2048]{1,0:T(8,128)(2,1)S(1)} %collective-permute-done.4.sib_own, ...), custom_call_target="tpu_custom_call" | custom-call | flops 4294967296 | bytes 4194304 | tf_op jit(solution)/shard_map/pallas_call | solution.py:468
  123.4 0.0 collective-permute-done.11.p3
  123.4 0.0 collective-permute-done.9.p2
  123.4 0.0 collective-permute-done.7.p1
  123.5 0.0 copy-done.3
  123.5 1.3 shard_map.137
  124.8 0.1 collective-permute-start.12
  124.9 1.2 collective-permute-start.13
  126.1 1.5 collective-permute-start.14
  127.5 0.0 collective-permute-done.15.w1
  127.5 0.0 collective-permute-done.16.w3
  127.5 7.3 %collective-permute-done.12.c1 = bf16[576,256]{1,0:T(8,128)(2,1)S(1)} collective-permute-done((bf16[576,256]{1,0:T(8,128)(2,1)S(1)}, bf16[576,256]{1,0:T(8,128)(2,1)S(1)}, u32[]{:S(2)}, u32[]{:S(2)}) %collective-permute-start.12) | collective-permute-done | bytes 294944 | tf_op jit(solution)/shard_map/ppermute | solution.py:50
  134.8 0.0 collective-permute-done.13.c2
  134.8 0.6 collective-permute-done.14.c3
  135.4 0.5 shard_map.139
  135.9 3.7 %collective-permute-start.18 = (bf16[576,256]{1,0:T(8,128)(2,1)S(1)}, bf16[576,256]{1,0:T(8,128)(2,1)S(1)}, u32[]{:S(2)}, u32[]{:S(2)}) collective-permute-start(bf16[576,256]{1,0:T(8,128)(2,1)S(1)} %shard_map.139), channel_id=1, source_target_pairs={{0,2},{1,3},{2,0},{3,1},{4,6},{5,7},{6,4},{7,5},{8,10},{9,11},{10,... | collective-permute-start | bytes 884744 | tf_op jit(solution)/shard_map/ppermute | solution.py:50
  139.6 1.1 shard_map.138
  140.7 0.8 collective-permute-start.17
  141.5 1.9 %collective-permute-start.19 = (bf16[576,256]{1,0:T(8,128)(2,1)S(1)}, bf16[576,256]{1,0:T(8,128)(2,1)S(1)}, u32[]{:S(2)}, u32[]{:S(2)}) collective-permute-start(bf16[576,256]{1,0:T(8,128)(2,1)S(1)} %get-tuple-element.45), channel_id=1, source_target_pairs={{0,3},{1,0},{2,1},{3,2},{4,7},{5,4},{6,5},{7,6},{8,11},{9,8},{10,9... | collective-permute-start | bytes 884744 | tf_op jit(solution)/shard_map/ppermute | solution.py:50
  143.4 0.3 collective-permute-done.18.a2
  143.7 3.8 %collective-permute-done.17.a1 = bf16[576,256]{1,0:T(8,128)(2,1)S(1)} collective-permute-done((bf16[576,256]{1,0:T(8,128)(2,1)S(1)}, bf16[576,256]{1,0:T(8,128)(2,1)S(1)}, u32[]{:S(2)}, u32[]{:S(2)}) %collective-permute-start.17) | collective-permute-done | bytes 294944 | tf_op jit(solution)/shard_map/ppermute | solution.py:50
  147.5 0.1 collective-permute-done.19.a3
  147.6 1.0 shard_map.140
  (1 shorter events, 0.0 us)
Async XLA Ops:
  1.7 19.1 %collective-permute-start.1 = (bf16[128,2048]{1,0:T(8,128)(2,1)S(1)}, bf16[128,2048]{1,0:T(8,128)(2,1)S(1)}, u32[]{:S(2)}, u32[]{:S(2)}) collective-permute-start(bf16[128,2048]{1,0:T(8,128)(2,1)S(1)} %pad_maximum_fusion.prefix.own), channel_id=1, source_target_pairs={{0,1},{1,0},{2,3},{3,2},{4,5},{5,4},{6,7},{7,6},{8,9},{9,8},{10,11... | collective-permute-start | bytes 1572872 | tf_op jit(solution)/shard_map/ppermute | solution.py:50
  3.9 0.7 copy-start.2
  4.6 16.3 %copy-start.4 = (s32[1,8,384,1]{2,3,1,0:T(1,128)S(1)}, s32[1,8,384,1]{2,3,1,0:T(1,128)}, u32[]{:S(2)}) copy-start(s32[1,8,384,1]{2,3,1,0:T(1,128)} %param.21) | copy-start | bytes 36868
  4.6 16.3 %copy-start = (f32[1296,128]{1,0:T(8,128)S(1)}, f32[1296,128]{1,0:T(8,128)}, u32[]{:S(2)}) copy-start(f32[1296,128]{1,0:T(8,128)} %constant.4.clone.near.tables) | copy-start | bytes 1990660
  4.6 16.3 %copy-start.1 = (s32[1,8,384]{2,1,0:T(8,128)S(1)}, s32[1,8,384]{2,1,0:T(8,128)}, u32[]{:S(2)}) copy-start(s32[1,8,384]{2,1,0:T(8,128)} %param.20) | copy-start | bytes 36868
  10.1 10.7 %collective-permute-start.2 = (bf16[1024,128]{1,0:T(8,128)(2,1)S(1)}, bf16[1024,128]{1,0:T(8,128)(2,1)S(1)}, u32[]{:S(2)}, u32[]{:S(2)}) collective-permute-start(bf16[1024,128]{1,0:T(8,128)(2,1)S(1)} %get-tuple-element.24.q), channel_id=1, source_target_pairs={{0,32},{1,33},{2,34},{3,35},{4,36},{5,37},{6,38},{7,39},{8,40},{9,... | collective-permute-start | bytes 786440 | tf_op jit(solution)/shard_map/ppermute | solution.py:50
  11.3 9.4 %collective-permute-start.3 = (bf16[1024,128]{1,0:T(8,128)(2,1)S(1)}, bf16[1024,128]{1,0:T(8,128)(2,1)S(1)}, u32[]{:S(2)}, u32[]{:S(2)}) collective-permute-start(bf16[1024,128]{1,0:T(8,128)(2,1)S(1)} %get-tuple-element.24.q), channel_id=1, source_target_pairs={{0,96},{1,97},{2,98},{3,99},{4,100},{5,101},{6,102},{7,103},{8,104... | collective-permute-start | bytes 786440 | tf_op jit(solution)/shard_map/ppermute | solution.py:50
  12.8 5.2 %collective-permute-start = (bf16[512,128]{1,0:T(8,128)(2,1)S(1)}, bf16[512,128]{1,0:T(8,128)(2,1)S(1)}, u32[]{:S(2)}, u32[]{:S(2)}) collective-permute-start(bf16[512,128]{1,0:T(8,128)(2,1)S(1)} %get-tuple-element.25.own), channel_id=1, source_target_pairs={{0,1},{1,0},{2,3},{3,2},{4,5},{5,4},{6,7},{7,6},{8,9},{9,8},{10,11... | collective-permute-start | bytes 393224 | tf_op jit(solution)/shard_map/ppermute | solution.py:50
  12.9 14.3 %collective-permute-start.10 = (bf16[256,1024]{1,0:T(8,128)(2,1)S(1)}, bf16[256,1024]{1,0:T(8,128)(2,1)S(1)}, u32[]{:S(2)}, u32[]{:S(2)}) collective-permute-start(bf16[256,1024]{1,0:T(8,128)(2,1)S(1)} %get-tuple-element.32), channel_id=1, source_target_pairs={{0,8},{1,9},{2,10},{3,11},{4,12},{5,13},{6,14},{7,15},{8,0},{9,1},... | collective-permute-start | bytes 1572872 | tf_op jit(solution)/shard_map/ppermute | solution.py:50
  18.0 9.1 %collective-permute-start.4 = (bf16[128,2048]{1,0:T(8,128)(2,1)S(1)}, bf16[128,2048]{1,0:T(8,128)(2,1)S(1)}, u32[]{:S(2)}, u32[]{:S(2)}) collective-permute-start(bf16[128,2048]{1,0:T(8,128)(2,1)S(1)} %pad_maximum_fusion.prefix.own), channel_id=1, source_target_pairs={{0,16},{1,17},{2,18},{3,19},{4,20},{5,21},{6,22},{7,23},{8,24},{9,... | collective-permute-start | bytes 1572872 | tf_op jit(solution)/shard_map/ppermute | solution.py:50
  20.8 9.1 %collective-permute-start.5 = (bf16[128,2048]{1,0:T(8,128)(2,1)S(1)}, bf16[128,2048]{1,0:T(8,128)(2,1)S(1)}, u32[]{:S(2)}, u32[]{:S(2)}) collective-permute-start(bf16[128,2048]{1,0:T(8,128)(2,1)S(1)} %collective-permute-done.1.prefix_other.other), channel_id=1, source_target_pairs={{0,16},{1,17},{2,18},{3,19},{4,20},{5,21},{6,22},{7,23},{8,24},{9,... | collective-permute-start | bytes 1572872 | tf_op jit(solution)/shard_map/ppermute | solution.py:50
  22.4 7.4 %collective-permute-start.6 = (bf16[336,512]{1,0:T(8,128)(2,1)S(1)}, bf16[336,512]{1,0:T(8,128)(2,1)S(1)}, u32[]{:S(2)}, u32[]{:S(2)}) collective-permute-start(bf16[336,512]{1,0:T(8,128)(2,1)S(1)} %get-tuple-element.28.seg), channel_id=1, source_target_pairs={{0,16},{1,17},{2,18},{3,19},{4,20},{5,21},{6,22},{7,23},{8,24},{9,... | collective-permute-start | bytes 1032200 | tf_op jit(solution)/shard_map/ppermute | solution.py:50
  22.9 31.1 %collective-permute-start.8 = (bf16[1024,128]{1,0:T(8,128)(2,1)S(1)}, bf16[1024,128]{1,0:T(8,128)(2,1)S(1)}, u32[]{:S(2)}, u32[]{:S(2)}) collective-permute-start(bf16[1024,128]{1,0:T(8,128)(2,1)S(1)} %get-tuple-element.24.q), channel_id=1, source_target_pairs={{0,64},{1,65},{2,66},{3,67},{4,68},{5,69},{6,70},{7,71},{8,72},{9,... | collective-permute-start | bytes 786440 | tf_op jit(solution)/shard_map/ppermute | solution.py:50
  27.1 100.4 %collective-permute-start.15 = (bf16[256,1024]{1,0:T(8,128)(2,1)S(1)}, bf16[256,1024]{1,0:T(8,128)(2,1)S(1)}, u32[]{:S(2)}, u32[]{:S(2)}) collective-permute-start(bf16[256,1024]{1,0:T(8,128)(2,1)S(1)} %get-tuple-element.39), channel_id=1, source_target_pairs={{0,4},{1,5},{2,6},{3,7},{4,8},{5,9},{6,10},{7,11},{8,12},{9,13},{1... | collective-permute-start | bytes 1572872 | tf_op jit(solution)/shard_map/ppermute | solution.py:50
  27.1 100.4 %collective-permute-start.16 = (bf16[256,1024]{1,0:T(8,128)(2,1)}, bf16[256,1024]{1,0:T(8,128)(2,1)S(1)}, u32[]{:S(2)}, u32[]{:S(2)}) collective-permute-start(bf16[256,1024]{1,0:T(8,128)(2,1)} %get-tuple-element.41), channel_id=1, source_target_pairs={{0,12},{1,13},{2,14},{3,15},{4,0},{5,1},{6,2},{7,3},{8,4},{9,5},{1... | collective-permute-start | bytes 1572872 | tf_op jit(solution)/shard_map/ppermute | solution.py:50
  52.8 70.6 %collective-permute-start.11 = (bf16[1184,128]{1,0:T(8,128)(2,1)S(1)}, bf16[1184,128]{1,0:T(8,128)(2,1)S(1)}, u32[]{:S(2)}, u32[]{:S(2)}) collective-permute-start(bf16[1184,128]{1,0:T(8,128)(2,1)S(1)} %shard_map.136), channel_id=1, source_target_pairs={{0,32},{1,33},{2,34},{3,35},{4,36},{5,37},{6,38},{7,39},{8,40},{9,... | collective-permute-start | bytes 909320 | tf_op jit(solution)/shard_map/ppermute | solution.py:50
  76.8 46.6 %collective-permute-start.9 = (bf16[1184,128]{1,0:T(8,128)(2,1)S(1)}, bf16[1184,128]{1,0:T(8,128)(2,1)S(1)}, u32[]{:S(2)}, u32[]{:S(2)}) collective-permute-start(bf16[1184,128]{1,0:T(8,128)(2,1)S(1)} %shard_map.135), channel_id=1, source_target_pairs={{0,64},{1,65},{2,66},{3,67},{4,68},{5,69},{6,70},{7,71},{8,72},{9,... | collective-permute-start | bytes 909320 | tf_op jit(solution)/shard_map/ppermute | solution.py:50
  99.7 23.8 %copy-start.3 = (bf16[256,128]{1,0:T(8,128)(2,1)S(1)}, bf16[256,128]{1,0:T(8,128)(2,1)}, u32[]{:S(2)}) copy-start(bf16[256,128]{1,0:T(8,128)(2,1)} %constant.5.clone.sign) | copy-start | bytes 196612
  99.7 23.7 %collective-permute-start.7 = (bf16[1184,128]{1,0:T(8,128)(2,1)S(1)}, bf16[1184,128]{1,0:T(8,128)(2,1)S(1)}, u32[]{:S(2)}, u32[]{:S(2)}) collective-permute-start(bf16[1184,128]{1,0:T(8,128)(2,1)S(1)} %shard_map.134), channel_id=1, source_target_pairs={{0,96},{1,97},{2,98},{3,99},{4,100},{5,101},{6,102},{7,103},{8,104... | collective-permute-start | bytes 909320 | tf_op jit(solution)/shard_map/ppermute | solution.py:50
  124.8 10.0 %collective-permute-start.12 = (bf16[576,256]{1,0:T(8,128)(2,1)S(1)}, bf16[576,256]{1,0:T(8,128)(2,1)S(1)}, u32[]{:S(2)}, u32[]{:S(2)}) collective-permute-start(bf16[576,256]{1,0:T(8,128)(2,1)S(1)} %get-tuple-element.35), channel_id=1, source_target_pairs={{0,4},{1,5},{2,6},{3,7},{4,8},{5,9},{6,10},{7,11},{8,12},{9,13},{1... | collective-permute-start | bytes 884744 | tf_op jit(solution)/shard_map/ppermute | solution.py:50
  124.9 9.9 %collective-permute-start.13 = (bf16[576,256]{1,0:T(8,128)(2,1)S(1)}, bf16[576,256]{1,0:T(8,128)(2,1)S(1)}, u32[]{:S(2)}, u32[]{:S(2)}) collective-permute-start(bf16[576,256]{1,0:T(8,128)(2,1)S(1)} %get-tuple-element.36), channel_id=1, source_target_pairs={{0,8},{1,9},{2,10},{3,11},{4,12},{5,13},{6,14},{7,15},{8,0},{9,1},... | collective-permute-start | bytes 884744 | tf_op jit(solution)/shard_map/ppermute | solution.py:50
  126.1 9.4 %collective-permute-start.14 = (bf16[576,256]{1,0:T(8,128)(2,1)S(1)}, bf16[576,256]{1,0:T(8,128)(2,1)S(1)}, u32[]{:S(2)}, u32[]{:S(2)}) collective-permute-start(bf16[576,256]{1,0:T(8,128)(2,1)S(1)} %get-tuple-element.37), channel_id=1, source_target_pairs={{0,12},{1,13},{2,14},{3,15},{4,0},{5,1},{6,2},{7,3},{8,4},{9,5},{1... | collective-permute-start | bytes 884744 | tf_op jit(solution)/shard_map/ppermute | solution.py:50
  135.9 7.8 %collective-permute-start.18 = (bf16[576,256]{1,0:T(8,128)(2,1)S(1)}, bf16[576,256]{1,0:T(8,128)(2,1)S(1)}, u32[]{:S(2)}, u32[]{:S(2)}) collective-permute-start(bf16[576,256]{1,0:T(8,128)(2,1)S(1)} %shard_map.139), channel_id=1, source_target_pairs={{0,2},{1,3},{2,0},{3,1},{4,6},{5,7},{6,4},{7,5},{8,10},{9,11},{10,... | collective-permute-start | bytes 884744 | tf_op jit(solution)/shard_map/ppermute | solution.py:50
  140.7 6.9 %collective-permute-start.17 = (bf16[576,256]{1,0:T(8,128)(2,1)S(1)}, bf16[576,256]{1,0:T(8,128)(2,1)S(1)}, u32[]{:S(2)}, u32[]{:S(2)}) collective-permute-start(bf16[576,256]{1,0:T(8,128)(2,1)S(1)} %get-tuple-element.44), channel_id=1, source_target_pairs={{0,1},{1,2},{2,3},{3,0},{4,5},{5,6},{6,7},{7,4},{8,9},{9,10},{10,1... | collective-permute-start | bytes 884744 | tf_op jit(solution)/shard_map/ppermute | solution.py:50
  141.5 6.1 %collective-permute-start.19 = (bf16[576,256]{1,0:T(8,128)(2,1)S(1)}, bf16[576,256]{1,0:T(8,128)(2,1)S(1)}, u32[]{:S(2)}, u32[]{:S(2)}) collective-permute-start(bf16[576,256]{1,0:T(8,128)(2,1)S(1)} %get-tuple-element.45), channel_id=1, source_target_pairs={{0,3},{1,0},{2,1},{3,2},{4,7},{5,4},{6,5},{7,6},{8,11},{9,8},{10,9... | collective-permute-start | bytes 884744 | tf_op jit(solution)/shard_map/ppermute | solution.py:50

commit v5 on v4

--- a/solution.py
+++ b/solution.py
@@ -366,12 +366,11 @@
 
         for pair in prefix:
             def some_tiles(i, carry, pair=pair):
-                for j in range(2):
-                    begin = pl.multiple_of((2 * i + j) * TILE, TILE)
-                    tile(*prefix_tile(pair, pl.ds(begin, TILE)))
+                begin = pl.multiple_of(i * TILE, TILE)
+                tile(*prefix_tile(pair, pl.ds(begin, TILE)))
                 return carry
 
-            lax.fori_loop(0, blocks // 2, some_tiles, 0)
+            lax.fori_loop(0, blocks, some_tiles, 0)
         for ref, flag in zip((seg, sib_seg), whole_flags):
             if flag is None:
                 tile(ref[:HD, :], ref[HD:2 * HD, :], masked=True)

time: 149 us -> 149 us (level)
  no operation moved by 1% of the time
where the time goes in v5:
time: 149 us; the launch traced here: 148 us
  Pallas kernels  103 us (69%)
  starting transfers between devices  27.6 us (19%)
  waiting for transfers between devices  15.5 us (10%)
    pallas_call x4, Pallas kernels, attend(): pl.pallas_call(functools.partial(attend_kernel, step), in_specs=[vmem()]...  91.9 us
    ppermute x20, starting transfers between devices, send(): return lax.ppermute(value, AXES, pairs_of(move))  27.6 us
    ppermute x20, waiting for transfers between devices, send(): return lax.ppermute(value, AXES, pairs_of(move))  15.5 us
    pallas_call x1, Pallas kernels, project(): pl.pallas_call(project_kernel, in_specs=[remain, vmem()] + [remain] * 5,...  5.45 us
  transfers between devices with their start and end apart: 20, of which 7 were waited for; matrix products, arithmetic and copies ran while one was open for 0% of the time, Pallas kernels for 68%

profile of v5, /device:TPU:1, one launch (start us, length us, event | category | flops | bytes accessed | tf_op | source)
XLA Modules:
  0.0 148.4 jit_solution(2843859074119964052)
XLA Ops:
  0.6 1.1 pad_maximum_fusion.prefix.own
  1.7 2.2 %collective-permute-start.1 = (bf16[128,2048]{1,0:T(8,128)(2,1)S(1)}, bf16[128,2048]{1,0:T(8,128)(2,1)S(1)}, u32[]{:S(2)}, u32[]{:S(2)}) collective-permute-start(bf16[128,2048]{1,0:T(8,128)(2,1)S(1)} %pad_maximum_fusion.prefix.own), channel_id=1, source_target_pairs={{0,1},{1,0},{2,3},{3,2},{4,5},{5,4},{6,7},{7,6},{8,9},{9,8},{10,11... | collective-permute-start | bytes 1572872 | tf_op jit(solution)/shard_map/ppermute | solution.py:50
  3.9 0.0 copy-start.2
  3.9 0.7 copy-done.2
  4.6 0.0 copy-start.4
  4.6 0.0 copy-start
  4.6 0.0 copy-start.1
  4.6 5.4 %shard_map.131 = (bf16[1024,128]{1,0:T(8,128)(2,1)S(1)}, bf16[512,128]{1,0:T(8,128)(2,1)S(1)}, bf16[256,1024]{1,0:T(8,128)(2,1)S(1)}, bf16[256,1024]{1,0:T(8,128...) custom-call(bf16[512,4096]{1,0:T(8,128)(2,1)} %tokens.1, bf16[32,128]{1,0:T(8,128)(2,1)S(1)} %bitcast.11, ...), custom_call_target="tpu_custom_call" | custom-call | flops 1610612736 | bytes 7340032 | tf_op jit(solution)/shard_map/pallas_call | solution.py:202
  10.1 1.3 collective-permute-start.2
  11.3 1.5 collective-permute-start.3
  12.8 0.1 collective-permute-start
  12.9 3.0 %collective-permute-start.10 = (bf16[256,1024]{1,0:T(8,128)(2,1)S(1)}, bf16[256,1024]{1,0:T(8,128)(2,1)S(1)}, u32[]{:S(2)}, u32[]{:S(2)}) collective-permute-start(bf16[256,1024]{1,0:T(8,128)(2,1)S(1)} %get-tuple-element.32), channel_id=1, source_target_pairs={{0,8},{1,9},{2,10},{3,11},{4,12},{5,13},{6,14},{7,15},{8,0},{9,1},... | collective-permute-start | bytes 1572872 | tf_op jit(solution)/shard_map/ppermute | solution.py:50
  15.9 2.1 %collective-permute-done.other = bf16[512,128]{1,0:T(8,128)(2,1)S(1)} collective-permute-done((bf16[512,128]{1,0:T(8,128)(2,1)S(1)}, bf16[512,128]{1,0:T(8,128)(2,1)S(1)}, u32[]{:S(2)}, u32[]{:S(2)}) %collective-permute-start) | collective-permute-done | bytes 131104 | tf_op jit(solution)/shard_map/ppermute | solution.py:50
  18.0 2.7 %collective-permute-start.4 = (bf16[128,2048]{1,0:T(8,128)(2,1)S(1)}, bf16[128,2048]{1,0:T(8,128)(2,1)S(1)}, u32[]{:S(2)}, u32[]{:S(2)}) collective-permute-start(bf16[128,2048]{1,0:T(8,128)(2,1)S(1)} %pad_maximum_fusion.prefix.own), channel_id=1, source_target_pairs={{0,16},{1,17},{2,18},{3,19},{4,20},{5,21},{6,22},{7,23},{8,24},{9,... | collective-permute-start | bytes 1572872 | tf_op jit(solution)/shard_map/ppermute | solution.py:50
  20.8 0.0 collective-permute-done.2.q
  20.8 0.0 collective-permute-done.3.q
  20.8 0.0 collective-permute-done.1.prefix_other.other
  20.8 0.1 collective-permute-start.5
  20.9 0.0 copy-done.4
  20.9 0.0 copy-done
  20.9 0.0 copy-done.1
  20.9 1.5 shard_map.132
  22.4 0.5 collective-permute-start.6
  22.9 2.9 %collective-permute-start.8 = (bf16[1024,128]{1,0:T(8,128)(2,1)S(1)}, bf16[1024,128]{1,0:T(8,128)(2,1)S(1)}, u32[]{:S(2)}, u32[]{:S(2)}) collective-permute-start(bf16[1024,128]{1,0:T(8,128)(2,1)S(1)} %get-tuple-element.24.q), channel_id=1, source_target_pairs={{0,64},{1,65},{2,66},{3,67},{4,68},{5,69},{6,70},{7,71},{8,72},{9,... | collective-permute-start | bytes 786440 | tf_op jit(solution)/shard_map/ppermute | solution.py:50
  25.8 1.3 collective-permute-done.10.w2
  27.1 0.0 collective-permute-start.15
  27.1 0.0 collective-permute-done.4.sib_own
  27.1 2.7 %collective-permute-start.16 = (bf16[256,1024]{1,0:T(8,128)(2,1)}, bf16[256,1024]{1,0:T(8,128)(2,1)S(1)}, u32[]{:S(2)}, u32[]{:S(2)}) collective-permute-start(bf16[256,1024]{1,0:T(8,128)(2,1)} %get-tuple-element.41), channel_id=1, source_target_pairs={{0,12},{1,13},{2,14},{3,15},{4,0},{5,1},{6,2},{7,3},{8,4},{9,5},{1... | collective-permute-start | bytes 1572872 | tf_op jit(solution)/shard_map/ppermute | solution.py:50
  29.8 0.0 collective-permute-done.6.sib_seg
  29.8 0.0 collective-permute-done.5.sib_other
  29.8 22.8 %shard_map.136 = bf16[1184,128]{1,0:T(8,128)(2,1)S(1)} custom-call(bf16[1024,128]{1,0:T(8,128)(2,1)S(1)} %collective-permute-done.3.q, bf16[128,2048]{1,0:T(8,128)(2,1)S(1)} %pad_maximum_fusion.prefix.own, bf16[128,2048]{1,0:T(8,128)(2,1)S(1)} %collective-permute-done.1.prefix_other.other, bf16[128,2048]{1,0:T(8,128)(2,1)S(1)} %collective-permute-done.4.sib_own, ...), custom_call_target="tpu_custom_call" | custom-call | flops 4294967296 | bytes 4194304 | tf_op jit(solution)/shard_map/pallas_call | solution.py:467
  52.6 1.3 collective-permute-start.11
  53.9 0.0 collective-permute-done.8.q
  53.9 23.0 %shard_map.135 = bf16[1184,128]{1,0:T(8,128)(2,1)S(1)} custom-call(bf16[1024,128]{1,0:T(8,128)(2,1)S(1)} %collective-permute-done.8.q, bf16[128,2048]{1,0:T(8,128)(2,1)S(1)} %pad_maximum_fusion.prefix.own, bf16[128,2048]{1,0:T(8,128)(2,1)S(1)} %collective-permute-done.1.prefix_other.other, bf16[128,2048]{1,0:T(8,128)(2,1)S(1)} %collective-permute-done.4.sib_own, ...), custom_call_target="tpu_custom_call" | custom-call | flops 4294967296 | bytes 4194304 | tf_op jit(solution)/shard_map/pallas_call | solution.py:467
  76.9 0.1 collective-permute-start.9
  77.0 22.8 %shard_map.134 = bf16[1184,128]{1,0:T(8,128)(2,1)S(1)} custom-call(bf16[1024,128]{1,0:T(8,128)(2,1)S(1)} %collective-permute-done.2.q, bf16[128,2048]{1,0:T(8,128)(2,1)S(1)} %pad_maximum_fusion.prefix.own, bf16[128,2048]{1,0:T(8,128)(2,1)S(1)} %collective-permute-done.1.prefix_other.other, bf16[128,2048]{1,0:T(8,128)(2,1)S(1)} %collective-permute-done.4.sib_own, ...), custom_call_target="tpu_custom_call" | custom-call | flops 4294967296 | bytes 4194304 | tf_op jit(solution)/shard_map/pallas_call | solution.py:467
  99.8 0.0 copy-start.3
  99.8 0.1 collective-permute-start.7
  99.9 23.4 %shard_map.133.p0 = bf16[1184,128]{1,0:T(8,128)(2,1)S(1)} custom-call(bf16[1024,128]{1,0:T(8,128)(2,1)S(1)} %get-tuple-element.24.q, bf16[128,2048]{1,0:T(8,128)(2,1)S(1)} %pad_maximum_fusion.prefix.own, bf16[128,2048]{1,0:T(8,128)(2,1)S(1)} %collective-permute-done.1.prefix_other.other, bf16[128,2048]{1,0:T(8,128)(2,1)S(1)} %collective-permute-done.4.sib_own, ...), custom_call_target="tpu_custom_call" | custom-call | flops 4294967296 | bytes 4194304 | tf_op jit(solution)/shard_map/pallas_call | solution.py:467
  123.2 0.0 collective-permute-done.11.p3
  123.3 0.0 collective-permute-done.9.p2
  123.3 0.0 collective-permute-done.7.p1
  123.3 0.0 copy-done.3
  123.3 1.3 shard_map.137
  124.6 0.1 collective-permute-start.12
  124.7 1.2 collective-permute-start.13
  125.9 1.5 %collective-permute-start.14 = (bf16[576,256]{1,0:T(8,128)(2,1)S(1)}, bf16[576,256]{1,0:T(8,128)(2,1)S(1)}, u32[]{:S(2)}, u32[]{:S(2)}) collective-permute-start(bf16[576,256]{1,0:T(8,128)(2,1)S(1)} %get-tuple-element.37), channel_id=1, source_target_pairs={{0,12},{1,13},{2,14},{3,15},{4,0},{5,1},{6,2},{7,3},{8,4},{9,5},{1... | collective-permute-start | bytes 884744 | tf_op jit(solution)/shard_map/ppermute | solution.py:50
  127.3 0.0 collective-permute-done.15.w1
  127.3 0.0 collective-permute-done.16.w3
  127.4 7.3 %collective-permute-done.12.c1 = bf16[576,256]{1,0:T(8,128)(2,1)S(1)} collective-permute-done((bf16[576,256]{1,0:T(8,128)(2,1)S(1)}, bf16[576,256]{1,0:T(8,128)(2,1)S(1)}, u32[]{:S(2)}, u32[]{:S(2)}) %collective-permute-start.12) | collective-permute-done | bytes 294944 | tf_op jit(solution)/shard_map/ppermute | solution.py:50
  134.6 0.0 collective-permute-done.13.c2
  134.6 0.6 collective-permute-done.14.c3
  135.2 0.5 shard_map.139
  135.7 3.7 %collective-permute-start.18 = (bf16[576,256]{1,0:T(8,128)(2,1)S(1)}, bf16[576,256]{1,0:T(8,128)(2,1)S(1)}, u32[]{:S(2)}, u32[]{:S(2)}) collective-permute-start(bf16[576,256]{1,0:T(8,128)(2,1)S(1)} %shard_map.139), channel_id=1, source_target_pairs={{0,2},{1,3},{2,0},{3,1},{4,6},{5,7},{6,4},{7,5},{8,10},{9,11},{10,... | collective-permute-start | bytes 884744 | tf_op jit(solution)/shard_map/ppermute | solution.py:50
  139.4 1.1 shard_map.138
  140.5 0.8 collective-permute-start.17
  141.3 1.9 %collective-permute-start.19 = (bf16[576,256]{1,0:T(8,128)(2,1)S(1)}, bf16[576,256]{1,0:T(8,128)(2,1)S(1)}, u32[]{:S(2)}, u32[]{:S(2)}) collective-permute-start(bf16[576,256]{1,0:T(8,128)(2,1)S(1)} %get-tuple-element.45), channel_id=1, source_target_pairs={{0,3},{1,0},{2,1},{3,2},{4,7},{5,4},{6,5},{7,6},{8,11},{9,8},{10,9... | collective-permute-start | bytes 884744 | tf_op jit(solution)/shard_map/ppermute | solution.py:50
  143.2 0.3 collective-permute-done.18.a2
  143.5 3.8 %collective-permute-done.17.a1 = bf16[576,256]{1,0:T(8,128)(2,1)S(1)} collective-permute-done((bf16[576,256]{1,0:T(8,128)(2,1)S(1)}, bf16[576,256]{1,0:T(8,128)(2,1)S(1)}, u32[]{:S(2)}, u32[]{:S(2)}) %collective-permute-start.17) | collective-permute-done | bytes 294944 | tf_op jit(solution)/shard_map/ppermute | solution.py:50
  147.3 0.1 collective-permute-done.19.a3
  147.4 1.0 shard_map.140
  (1 shorter events, 0.0 us)
Async XLA Ops:
  1.7 19.1 %collective-permute-start.1 = (bf16[128,2048]{1,0:T(8,128)(2,1)S(1)}, bf16[128,2048]{1,0:T(8,128)(2,1)S(1)}, u32[]{:S(2)}, u32[]{:S(2)}) collective-permute-start(bf16[128,2048]{1,0:T(8,128)(2,1)S(1)} %pad_maximum_fusion.prefix.own), channel_id=1, source_target_pairs={{0,1},{1,0},{2,3},{3,2},{4,5},{5,4},{6,7},{7,6},{8,9},{9,8},{10,11... | collective-permute-start | bytes 1572872 | tf_op jit(solution)/shard_map/ppermute | solution.py:50
  3.9 0.7 copy-start.2
  4.6 16.3 %copy-start.4 = (s32[1,8,384,1]{2,3,1,0:T(1,128)S(1)}, s32[1,8,384,1]{2,3,1,0:T(1,128)}, u32[]{:S(2)}) copy-start(s32[1,8,384,1]{2,3,1,0:T(1,128)} %param.21) | copy-start | bytes 36868
  4.6 16.3 %copy-start = (f32[1296,128]{1,0:T(8,128)S(1)}, f32[1296,128]{1,0:T(8,128)}, u32[]{:S(2)}) copy-start(f32[1296,128]{1,0:T(8,128)} %constant.4.clone.near.tables) | copy-start | bytes 1990660
  4.6 16.3 %copy-start.1 = (s32[1,8,384]{2,1,0:T(8,128)S(1)}, s32[1,8,384]{2,1,0:T(8,128)}, u32[]{:S(2)}) copy-start(s32[1,8,384]{2,1,0:T(8,128)} %param.20) | copy-start | bytes 36868
  10.1 10.7 %collective-permute-start.2 = (bf16[1024,128]{1,0:T(8,128)(2,1)S(1)}, bf16[1024,128]{1,0:T(8,128)(2,1)S(1)}, u32[]{:S(2)}, u32[]{:S(2)}) collective-permute-start(bf16[1024,128]{1,0:T(8,128)(2,1)S(1)} %get-tuple-element.24.q), channel_id=1, source_target_pairs={{0,32},{1,33},{2,34},{3,35},{4,36},{5,37},{6,38},{7,39},{8,40},{9,... | collective-permute-start | bytes 786440 | tf_op jit(solution)/shard_map/ppermute | solution.py:50
  11.3 9.4 %collective-permute-start.3 = (bf16[1024,128]{1,0:T(8,128)(2,1)S(1)}, bf16[1024,128]{1,0:T(8,128)(2,1)S(1)}, u32[]{:S(2)}, u32[]{:S(2)}) collective-permute-start(bf16[1024,128]{1,0:T(8,128)(2,1)S(1)} %get-tuple-element.24.q), channel_id=1, source_target_pairs={{0,96},{1,97},{2,98},{3,99},{4,100},{5,101},{6,102},{7,103},{8,104... | collective-permute-start | bytes 786440 | tf_op jit(solution)/shard_map/ppermute | solution.py:50
  12.8 5.2 %collective-permute-start = (bf16[512,128]{1,0:T(8,128)(2,1)S(1)}, bf16[512,128]{1,0:T(8,128)(2,1)S(1)}, u32[]{:S(2)}, u32[]{:S(2)}) collective-permute-start(bf16[512,128]{1,0:T(8,128)(2,1)S(1)} %get-tuple-element.25.own), channel_id=1, source_target_pairs={{0,1},{1,0},{2,3},{3,2},{4,5},{5,4},{6,7},{7,6},{8,9},{9,8},{10,11... | collective-permute-start | bytes 393224 | tf_op jit(solution)/shard_map/ppermute | solution.py:50
  12.9 14.3 %collective-permute-start.10 = (bf16[256,1024]{1,0:T(8,128)(2,1)S(1)}, bf16[256,1024]{1,0:T(8,128)(2,1)S(1)}, u32[]{:S(2)}, u32[]{:S(2)}) collective-permute-start(bf16[256,1024]{1,0:T(8,128)(2,1)S(1)} %get-tuple-element.32), channel_id=1, source_target_pairs={{0,8},{1,9},{2,10},{3,11},{4,12},{5,13},{6,14},{7,15},{8,0},{9,1},... | collective-permute-start | bytes 1572872 | tf_op jit(solution)/shard_map/ppermute | solution.py:50
  18.0 9.1 %collective-permute-start.4 = (bf16[128,2048]{1,0:T(8,128)(2,1)S(1)}, bf16[128,2048]{1,0:T(8,128)(2,1)S(1)}, u32[]{:S(2)}, u32[]{:S(2)}) collective-permute-start(bf16[128,2048]{1,0:T(8,128)(2,1)S(1)} %pad_maximum_fusion.prefix.own), channel_id=1, source_target_pairs={{0,16},{1,17},{2,18},{3,19},{4,20},{5,21},{6,22},{7,23},{8,24},{9,... | collective-permute-start | bytes 1572872 | tf_op jit(solution)/shard_map/ppermute | solution.py:50
  20.8 9.1 %collective-permute-start.5 = (bf16[128,2048]{1,0:T(8,128)(2,1)S(1)}, bf16[128,2048]{1,0:T(8,128)(2,1)S(1)}, u32[]{:S(2)}, u32[]{:S(2)}) collective-permute-start(bf16[128,2048]{1,0:T(8,128)(2,1)S(1)} %collective-permute-done.1.prefix_other.other), channel_id=1, source_target_pairs={{0,16},{1,17},{2,18},{3,19},{4,20},{5,21},{6,22},{7,23},{8,24},{9,... | collective-permute-start | bytes 1572872 | tf_op jit(solution)/shard_map/ppermute | solution.py:50
  22.4 7.4 %collective-permute-start.6 = (bf16[336,512]{1,0:T(8,128)(2,1)S(1)}, bf16[336,512]{1,0:T(8,128)(2,1)S(1)}, u32[]{:S(2)}, u32[]{:S(2)}) collective-permute-start(bf16[336,512]{1,0:T(8,128)(2,1)S(1)} %get-tuple-element.28.seg), channel_id=1, source_target_pairs={{0,16},{1,17},{2,18},{3,19},{4,20},{5,21},{6,22},{7,23},{8,24},{9,... | collective-permute-start | bytes 1032200 | tf_op jit(solution)/shard_map/ppermute | solution.py:50
  22.9 31.0 %collective-permute-start.8 = (bf16[1024,128]{1,0:T(8,128)(2,1)S(1)}, bf16[1024,128]{1,0:T(8,128)(2,1)S(1)}, u32[]{:S(2)}, u32[]{:S(2)}) collective-permute-start(bf16[1024,128]{1,0:T(8,128)(2,1)S(1)} %get-tuple-element.24.q), channel_id=1, source_target_pairs={{0,64},{1,65},{2,66},{3,67},{4,68},{5,69},{6,70},{7,71},{8,72},{9,... | collective-permute-start | bytes 786440 | tf_op jit(solution)/shard_map/ppermute | solution.py:50
  27.1 100.2 %collective-permute-start.15 = (bf16[256,1024]{1,0:T(8,128)(2,1)S(1)}, bf16[256,1024]{1,0:T(8,128)(2,1)S(1)}, u32[]{:S(2)}, u32[]{:S(2)}) collective-permute-start(bf16[256,1024]{1,0:T(8,128)(2,1)S(1)} %get-tuple-element.39), channel_id=1, source_target_pairs={{0,4},{1,5},{2,6},{3,7},{4,8},{5,9},{6,10},{7,11},{8,12},{9,13},{1... | collective-permute-start | bytes 1572872 | tf_op jit(solution)/shard_map/ppermute | solution.py:50
  27.1 100.2 %collective-permute-start.16 = (bf16[256,1024]{1,0:T(8,128)(2,1)}, bf16[256,1024]{1,0:T(8,128)(2,1)S(1)}, u32[]{:S(2)}, u32[]{:S(2)}) collective-permute-start(bf16[256,1024]{1,0:T(8,128)(2,1)} %get-tuple-element.41), channel_id=1, source_target_pairs={{0,12},{1,13},{2,14},{3,15},{4,0},{5,1},{6,2},{7,3},{8,4},{9,5},{1... | collective-permute-start | bytes 1572872 | tf_op jit(solution)/shard_map/ppermute | solution.py:50
  52.6 70.7 %collective-permute-start.11 = (bf16[1184,128]{1,0:T(8,128)(2,1)S(1)}, bf16[1184,128]{1,0:T(8,128)(2,1)S(1)}, u32[]{:S(2)}, u32[]{:S(2)}) collective-permute-start(bf16[1184,128]{1,0:T(8,128)(2,1)S(1)} %shard_map.136), channel_id=1, source_target_pairs={{0,32},{1,33},{2,34},{3,35},{4,36},{5,37},{6,38},{7,39},{8,40},{9,... | collective-permute-start | bytes 909320 | tf_op jit(solution)/shard_map/ppermute | solution.py:50
  76.9 46.4 %collective-permute-start.9 = (bf16[1184,128]{1,0:T(8,128)(2,1)S(1)}, bf16[1184,128]{1,0:T(8,128)(2,1)S(1)}, u32[]{:S(2)}, u32[]{:S(2)}) collective-permute-start(bf16[1184,128]{1,0:T(8,128)(2,1)S(1)} %shard_map.135), channel_id=1, source_target_pairs={{0,64},{1,65},{2,66},{3,67},{4,68},{5,69},{6,70},{7,71},{8,72},{9,... | collective-permute-start | bytes 909320 | tf_op jit(solution)/shard_map/ppermute | solution.py:50
  99.8 23.5 %copy-start.3 = (bf16[256,128]{1,0:T(8,128)(2,1)S(1)}, bf16[256,128]{1,0:T(8,128)(2,1)}, u32[]{:S(2)}) copy-start(bf16[256,128]{1,0:T(8,128)(2,1)} %constant.5.clone.sign) | copy-start | bytes 196612
  99.8 23.5 %collective-permute-start.7 = (bf16[1184,128]{1,0:T(8,128)(2,1)S(1)}, bf16[1184,128]{1,0:T(8,128)(2,1)S(1)}, u32[]{:S(2)}, u32[]{:S(2)}) collective-permute-start(bf16[1184,128]{1,0:T(8,128)(2,1)S(1)} %shard_map.134), channel_id=1, source_target_pairs={{0,96},{1,97},{2,98},{3,99},{4,100},{5,101},{6,102},{7,103},{8,104... | collective-permute-start | bytes 909320 | tf_op jit(solution)/shard_map/ppermute | solution.py:50
  124.6 10.0 %collective-permute-start.12 = (bf16[576,256]{1,0:T(8,128)(2,1)S(1)}, bf16[576,256]{1,0:T(8,128)(2,1)S(1)}, u32[]{:S(2)}, u32[]{:S(2)}) collective-permute-start(bf16[576,256]{1,0:T(8,128)(2,1)S(1)} %get-tuple-element.35), channel_id=1, source_target_pairs={{0,4},{1,5},{2,6},{3,7},{4,8},{5,9},{6,10},{7,11},{8,12},{9,13},{1... | collective-permute-start | bytes 884744 | tf_op jit(solution)/shard_map/ppermute | solution.py:50
  124.7 9.9 %collective-permute-start.13 = (bf16[576,256]{1,0:T(8,128)(2,1)S(1)}, bf16[576,256]{1,0:T(8,128)(2,1)S(1)}, u32[]{:S(2)}, u32[]{:S(2)}) collective-permute-start(bf16[576,256]{1,0:T(8,128)(2,1)S(1)} %get-tuple-element.36), channel_id=1, source_target_pairs={{0,8},{1,9},{2,10},{3,11},{4,12},{5,13},{6,14},{7,15},{8,0},{9,1},... | collective-permute-start | bytes 884744 | tf_op jit(solution)/shard_map/ppermute | solution.py:50
  125.9 9.4 %collective-permute-start.14 = (bf16[576,256]{1,0:T(8,128)(2,1)S(1)}, bf16[576,256]{1,0:T(8,128)(2,1)S(1)}, u32[]{:S(2)}, u32[]{:S(2)}) collective-permute-start(bf16[576,256]{1,0:T(8,128)(2,1)S(1)} %get-tuple-element.37), channel_id=1, source_target_pairs={{0,12},{1,13},{2,14},{3,15},{4,0},{5,1},{6,2},{7,3},{8,4},{9,5},{1... | collective-permute-start | bytes 884744 | tf_op jit(solution)/shard_map/ppermute | solution.py:50
  135.7 7.8 %collective-permute-start.18 = (bf16[576,256]{1,0:T(8,128)(2,1)S(1)}, bf16[576,256]{1,0:T(8,128)(2,1)S(1)}, u32[]{:S(2)}, u32[]{:S(2)}) collective-permute-start(bf16[576,256]{1,0:T(8,128)(2,1)S(1)} %shard_map.139), channel_id=1, source_target_pairs={{0,2},{1,3},{2,0},{3,1},{4,6},{5,7},{6,4},{7,5},{8,10},{9,11},{10,... | collective-permute-start | bytes 884744 | tf_op jit(solution)/shard_map/ppermute | solution.py:50
  140.5 6.9 %collective-permute-start.17 = (bf16[576,256]{1,0:T(8,128)(2,1)S(1)}, bf16[576,256]{1,0:T(8,128)(2,1)S(1)}, u32[]{:S(2)}, u32[]{:S(2)}) collective-permute-start(bf16[576,256]{1,0:T(8,128)(2,1)S(1)} %get-tuple-element.44), channel_id=1, source_target_pairs={{0,1},{1,2},{2,3},{3,0},{4,5},{5,6},{6,7},{7,4},{8,9},{9,10},{10,1... | collective-permute-start | bytes 884744 | tf_op jit(solution)/shard_map/ppermute | solution.py:50
  141.3 6.1 %collective-permute-start.19 = (bf16[576,256]{1,0:T(8,128)(2,1)S(1)}, bf16[576,256]{1,0:T(8,128)(2,1)S(1)}, u32[]{:S(2)}, u32[]{:S(2)}) collective-permute-start(bf16[576,256]{1,0:T(8,128)(2,1)S(1)} %get-tuple-element.45), channel_id=1, source_target_pairs={{0,3},{1,0},{2,1},{3,2},{4,7},{5,4},{6,5},{7,6},{8,11},{9,8},{10,9... | collective-permute-start | bytes 884744 | tf_op jit(solution)/shard_map/ppermute | solution.py:50
